TPU v7x, 32 devices: a whole 2x2x4 slice. The times are simulated.
32 devices in a mesh: section: 4 (over y, x), dp: 8 (over z, core).
Axes of the slice: x: 2, y: 2, z: 4, core: 2. Of those that a mesh axis runs over, the one named last changes fastest.
Arguments:
- voxel_feats: bfloat16 [8, 16384, 64], P(None, 'dp'), may hold values from -6 to 6
- down_map: int32 [8, 8, 4096], P(None, None, 'dp'), may hold values from 0 to 2048, as said below
- neighbours: int32 [8, 27, 4096], P(None, None, 'dp'), may hold values from 0 to 512, as said below
- w_down: bfloat16 [8, 64, 128], replicated, may hold values from -0.25 to 0.25
- w_first: bfloat16 [27, 128, 128], replicated, may hold values from -0.109375 to 0.109375
- w_second: bfloat16 [27, 128, 128], replicated, may hold values from -0.109375 to 0.109375
- bn_scale: float32 [3, 128], replicated, may hold values from 0.25 to 1.75
- bn_shift: float32 [3, 128], replicated, may hold values from -3 to 3
- out_grad: bfloat16 [8, 4096, 128], P(None, 'dp'), may hold values from -6 to 6
Outputs:
- features: bfloat16 [8, 4096, 128], P('section', 'dp')
- input_grad: bfloat16 [8, 16384, 64], P('section', 'dp')
- grad_down: float32 [8, 64, 128], replicated
- grad_first: float32 [27, 128, 128], replicated
- grad_second: float32 [27, 128, 128], replicated
- grad_scale: float32 [3, 128], replicated
- grad_shift: float32 [3, 128], replicated
Inputs may be any that keep to these rules, and one draw needn't show every extreme that they name: Offset k stands for the step (k // 9 - 1, (k // 3) % 3 - 1, k % 3 - 1) on the coarse grid. Entries index rows of the same bucket. The live rows of a bucket are its first ones; a live row r has neighbours[m, 13, r] = r, and every entry of a row that is not live is 512. The map is symmetric: where neighbours[m, k, p] = q, neighbours[m, 26 - k, q] = p. A bucket has 32 live rows or more, and in each micro-batch one bucket has all 512 live. `down_map`: entries index fine rows of the same bucket; 2048 marks an absent child. Each fine row is named at most once in a micro-batch. A live coarse row has 1 to 7 children and a row that is not live has none; the children of a bucket's live rows are its first 4 times as many fine rows, grouped by coarse row in order. In each micro-batch one bucket uses all 2048 fine rows.
All inputs are finite; a program needn't handle non-finite values.
Results may differ from a plain program's by a relative error of at most 0.012.
Values may be sent and summed in bfloat16 or wider, within the bound.
No kernel may reach another device: no remote copies, remote signals or barrier semaphores. Data moves between devices by JAX's collectives and lax.ppermute only.
A program may use at most 64 MiB of HBM per device.

v0:
```python
import functools

import jax
import jax.numpy as jnp
from jax import lax
from jax.experimental import pallas as pl
from jax.experimental.pallas import tpu as pltpu
from jax.sharding import PartitionSpec as P

EPSILON = 1e-05
F32 = jnp.float32
BF16 = jnp.bfloat16
F8 = jnp.float8_e4m3fn
VMEM_BYTES = 40 << 20
UNROLL_FORWARD = False
UNROLL_BACKWARD = True
GROUPS = ((0, 1), (2, 3), (4, 5), (6, 7), (8, 9), (10, 11), (12, 13))


def mm(left, right):
    return jnp.dot(left, right, preferred_element_type=F32)


def mm_t(left, right):
    return lax.dot_general(left, right, (((1,), (1,)), ((), ())), preferred_element_type=F32)


def col_sum(values):
    return jnp.sum(values, axis=0, keepdims=True)


def sigmoid(values):
    return 1.0 / (1.0 + jnp.exp(-values))


def tree_sum(parts):
    parts = list(parts)
    while len(parts) > 1:
        parts = [parts[i] + parts[i + 1] for i in range(0, len(parts), 2)]
    return parts[0]


def sum_refs(refs):
    return tree_sum([ref[...].astype(F32) for ref in refs])


def hits(index_row, rows):
    places = lax.broadcasted_iota(jnp.int16, (rows, index_row.shape[1]), 0)
    return jnp.where(places == index_row, jnp.bfloat16(1), jnp.bfloat16(0)).astype(F8)


def live_mask(near_ref, bucket, channels):
    rows = near_ref.shape[2]
    centre = near_ref[bucket, 13:14, :]
    count = jnp.sum((centre < rows).astype(F32), axis=1, keepdims=True)
    places = lax.broadcasted_iota(jnp.int32, (rows, channels), 0).astype(F32)
    return (places < count).astype(F32), count


def power_for(largest):
    power = jnp.full_like(largest, 2.0**-60)
    for exponent in (64, 32, 16, 8, 4, 2, 1):
        raised = power * (2.0**exponent)
        power = jnp.where(largest * raised <= 224.0, raised, power)
    return power


def two_parts(scaled):
    high = scaled.astype(F8)
    low = (scaled - high.astype(F32)).astype(F8)
    return jnp.concatenate([high, low], axis=1)


def moved_rows(near_ref, bucket, offset, pair):
    row = near_ref[bucket, offset : offset + 1, :]
    both = mm(hits(row.astype(jnp.int16), row.shape[1]), pair)
    channels = pair.shape[1] // 2
    return (both[:, :channels] + both[:, channels:]).astype(BF16)


def group_offsets(group):
    return [k for j in group for k in ((j, 26 - j) if j < 13 else (13,))]


def moments(totals):
    count = totals[2:3]
    mean_row = totals[0:1] / count
    square = totals[1:2] / count
    return mean_row, lax.rsqrt(square - mean_row * mean_row + EPSILON), count


def add_sums(out_ref, first, second, count):
    third = jnp.broadcast_to(count, first.shape)
    rows = [first, second, third, jnp.zeros((out_ref.shape[0] - 3, first.shape[1]), F32)]
    out_ref[...] += jnp.concatenate(rows, axis=0)


def norm_back(upstream, centred, live, inv_std, gain_row, back, count):
    return live * (inv_std * gain_row) * (upstream - back[0:1] / count - centred * (back[1:2] / count))


def parent_rows(table, fine_rows):
    first = jnp.min(table, axis=0, keepdims=True)
    children = jnp.sum((table < fine_rows).astype(jnp.int32), axis=0, keepdims=True)
    return first, first + children


def parent_hits(first, last, at, size):
    places = lax.broadcasted_iota(jnp.int16, (size, first.shape[1]), 0) + jnp.int16(at)
    inside = (places >= first.astype(jnp.int16)) & (places < last.astype(jnp.int16))
    return jnp.where(inside, jnp.bfloat16(1), jnp.bfloat16(0))


def pack_kernel(
    where_ref, feats_hbm, down_hbm, weight_hbm,
    feats_send, table_send, feats_own, table_own, weight_ref, arrivals,
):
    copies = [
        pltpu.make_async_copy(source, target, arrivals.at[i])
        for i, (source, target) in enumerate(
            (
                (feats_hbm.at[where_ref[4]], feats_send),
                (down_hbm.at[where_ref[4]], table_send),
                (down_hbm.at[where_ref[0]], table_own),
                (feats_hbm.at[where_ref[0]], feats_own),
                (weight_hbm, weight_ref),
            )
        )
    ]
    for copy in copies:
        copy.start()
    for copy in copies:
        copy.wait()


def down_rows(table, feats_ref, weight_ref, which_ref, spread_ref, parent_ref):
    in_channels, fine_rows = feats_ref.shape
    offsets, coarse_rows = table.shape
    first, last = parent_rows(table, fine_rows)
    rank = table - first
    numbers = lax.broadcasted_iota(jnp.int32, (offsets, coarse_rows), 0) + 1
    rows = [jnp.sum(jnp.where(rank == r, numbers, 0), axis=0, keepdims=True) for r in range(8)]
    safe_first = jnp.where(first < fine_rows, first, 0)
    rows += [(safe_first // 16) * 16, safe_first % 16] + [jnp.zeros_like(first)] * 6
    lookup = jnp.concatenate(rows, axis=0).astype(F32).astype(BF16)
    step = 512
    for at in range(0, fine_rows, step):
        parent_ref[at : at + step] = parent_hits(first, last, at, step)
    found = mm_t(lookup, parent_ref[...])
    place = lax.broadcasted_iota(jnp.int32, (8, fine_rows), 1).astype(F32) - (found[8:9] + found[9:10])
    column = lax.broadcasted_iota(jnp.int32, (8, fine_rows), 0).astype(F32)
    which = jnp.sum(jnp.where(column == place, found[:8], 0.0), axis=0, keepdims=True)
    which_ref[...] = jnp.broadcast_to(which, which_ref.shape)
    code = jnp.broadcast_to(which, (in_channels, fine_rows)).astype(BF16)
    feats = feats_ref[...]
    for k in range(offsets):
        spread_ref[in_channels * k : in_channels * (k + 1)] = jnp.where(
            code == jnp.bfloat16(k + 1), feats, jnp.zeros_like(feats)
        )
    kids = mm(spread_ref[...], parent_ref[...]).astype(BF16)
    hidden = jnp.transpose(mm(jnp.transpose(weight_ref[...]), kids))
    count = jnp.sum((last > first).astype(F32), axis=1, keepdims=True)
    return kids, hidden, count


def down_kernel(
    where_ref, feats_ref, table_ref, weight_ref, near_ref,
    hidden_ref, sums_ref, kids_ref, which_ref, near_own, near_send,
    spread_ref, parent_ref,
):
    for k in range(near_own.shape[0]):
        near_own[k : k + 1] = near_ref[k, pl.ds(where_ref[0], 1), :]
        near_send[k : k + 1] = near_ref[k, pl.ds(where_ref[4], 1), :]
    kids, hidden, count = down_rows(
        table_ref[...], feats_ref, weight_ref, which_ref, spread_ref, parent_ref
    )
    kids_ref[...] = kids
    hidden_ref[...] = hidden
    sums_ref[...] = jnp.zeros_like(sums_ref)
    add_sums(sums_ref, col_sum(hidden), col_sum(hidden * hidden), count)


def down_other_kernel(
    where_ref, feats_ref, table_ref, weight_ref, own_hidden, own_sums, own_kids, own_which, own_table,
    hidden_ref, sums_ref, kids_ref, which_ref, tables_ref,
    spread_ref, parent_ref,
):
    kids, hidden, count = down_rows(
        table_ref[...], feats_ref, weight_ref, which_ref.at[1], spread_ref, parent_ref
    )
    kids_ref[1] = kids
    hidden_ref[1] = hidden
    tables_ref[1] = table_ref[...]
    for both, own in ((kids_ref, own_kids), (hidden_ref, own_hidden), (which_ref, own_which), (tables_ref, own_table)):
        both[0] = own[...]
    sums_ref[...] = own_sums[...]
    add_sums(sums_ref, col_sum(hidden), col_sum(hidden * hidden), count)


def conv_all(source, near_ref, bucket, weight_ref):
    values = source.astype(F32)
    largest = jnp.max(jnp.max(jnp.abs(values), axis=0, keepdims=True), axis=1, keepdims=True)
    power = power_for(largest)
    scaled = values * power
    pair = two_parts(scaled)
    out = None
    for group in GROUPS:
        offsets = group_offsets(group)
        rows = [
            scaled.astype(BF16) if k == 13 else moved_rows(near_ref, bucket, 26 - k, pair)
            for k in offsets
        ]
        weight = jnp.concatenate([weight_ref[k] for k in offsets], axis=0)
        term = mm(jnp.concatenate(rows, axis=1), weight)
        out = term if out is None else out + term
    return out * (1.0 / power)


def each_bucket(count, body, unrolled):
    if unrolled:
        for b in range(count):
            body(b)
        return

    def step(b, carry):
        body(b)
        return carry

    lax.fori_loop(0, count, step, 0)


def near_kernel(where_ref, own_ref, other_ref, near_ref):
    near_ref[0] = own_ref[...]
    near_ref[1] = other_ref[...]


def forward_kernel(norm_at, rounded, where_ref, hidden_ref, near_ref, weight_ref, scale_ref, shift_ref, *refs):
    part_refs, (act_ref, next_ref, sums_ref) = refs[:-3], refs[-3:]
    mean_row, inv_std, _ = moments(sum_refs(part_refs))
    sums_ref[...] = jnp.zeros_like(sums_ref)

    def bucket(b):
        live, count = live_mask(near_ref, b, hidden_ref.shape[2])
        centred = (hidden_ref[b] - mean_row) * inv_std
        value = centred * scale_ref[norm_at : norm_at + 1] + shift_ref[norm_at : norm_at + 1]
        act = (live * (value * sigmoid(value))).astype(BF16)
        act_ref[b] = act
        hidden = conv_all(act, near_ref, b, weight_ref)
        if rounded:
            hidden = hidden.astype(BF16)
        next_ref[b] = hidden
        hidden = hidden.astype(F32)
        add_sums(sums_ref, col_sum(hidden), col_sum(hidden * hidden), count)

    each_bucket(hidden_ref.shape[0], bucket, UNROLL_FORWARD)


def grad_kernel(where_ref, grad_ref, own_ref, send_ref):
    own_ref[...] = grad_ref[where_ref[0]]
    send_ref[...] = grad_ref[where_ref[4]]


def output_kernel(where_ref, hidden_ref, act_ref, own_grad, other_grad, near_ref, scale_ref, shift_ref, *refs):
    part_refs, (own_ref, send_ref, slope_ref, sums_ref) = refs[:-4], refs[-4:]
    mean_row, inv_std, _ = moments(sum_refs(part_refs))
    sums_ref[...] = jnp.zeros_like(sums_ref)
    for b, (grad_ref, features_ref) in enumerate(((own_grad, own_ref), (other_grad, send_ref))):
        live, count = live_mask(near_ref, b, hidden_ref.shape[2])
        centred = (hidden_ref[b].astype(F32) - mean_row) * inv_std
        value = centred * scale_ref[2:3] + shift_ref[2:3] + act_ref[b].astype(F32)
        gate = sigmoid(value)
        features_ref[...] = (live * (value * gate)).astype(BF16)
        upstream = grad_ref[...].astype(F32) * live * (gate * (1.0 + value * (1.0 - gate)))
        slope_ref[b] = upstream
        add_sums(sums_ref, col_sum(upstream), col_sum(upstream * centred), count)


def put_halves(where_ref, grad_ref, keep_ref, send_ref):
    half = keep_ref.shape[0]
    core = where_ref[1]
    keep_ref[...] = grad_ref[pl.ds(pl.multiple_of(core * half, 16), half)].astype(BF16)
    send_ref[...] = grad_ref[pl.ds(pl.multiple_of((1 - core) * half, 16), half)].astype(BF16)


def backward_kernel(norm_at, with_skip, ways, where_ref, *refs):
    upstream_ref, hidden_ref, lower_ref, act_ref, near_ref, weight_ref, scale_ref, shift_ref = refs[:8]
    own, back, low = (sum_refs(refs[8 + i * ways : 8 + (i + 1) * ways]) for i in range(3))
    rest = refs[8 + 3 * ways :]
    next_ref, sums_ref, keep_ref, send_ref, grad_ref = rest[-5:]
    mean_row, inv_std, count = moments(own)
    low_mean, low_std, _ = moments(low)
    channels = hidden_ref.shape[2]
    sums_ref[...] = jnp.zeros_like(sums_ref)
    grad_ref[...] = jnp.zeros_like(grad_ref)

    def bucket(b):
        live, own_count = live_mask(near_ref, b, channels)
        centred = (hidden_ref[b].astype(F32) - mean_row) * inv_std
        rows_grad = norm_back(
            upstream_ref[b], centred, live, inv_std, scale_ref[norm_at : norm_at + 1], back, count
        ).astype(BF16)
        act_t = jnp.transpose(act_ref[b])
        values = rows_grad.astype(F32)
        power = power_for(jnp.max(jnp.abs(values), axis=0, keepdims=True))
        undo = 1.0 / power
        undo_low = undo.astype(BF16)
        scaled = values * power
        pair = two_parts(scaled)
        below = None
        for group in GROUPS:
            offsets = group_offsets(group)
            rows = [
                scaled.astype(BF16) if k == 13 else moved_rows(near_ref, b, k, pair)
                for k in offsets
            ]
            moved = jnp.concatenate(rows, axis=1)
            weight = jnp.concatenate([weight_ref[k] * undo_low for k in offsets], axis=1)
            term = mm_t(moved, weight)
            below = term if below is None else below + term
            products = mm(act_t, moved)
            for i, k in enumerate(offsets):
                grad_ref[k * channels : (k + 1) * channels] += (
                    products[:, i * channels : (i + 1) * channels] * undo
                )
        below = below.astype(BF16).astype(F32)
        if with_skip:
            below = below + rest[0][b].astype(BF16).astype(F32)
        low_centred = (lower_ref[b] - low_mean) * low_std
        value = low_centred * scale_ref[norm_at - 1 : norm_at] + shift_ref[norm_at - 1 : norm_at]
        gate = sigmoid(value)
        upstream = below * live * (gate * (1.0 + value * (1.0 - gate)))
        next_ref[b] = upstream
        add_sums(sums_ref, col_sum(upstream), col_sum(upstream * low_centred), own_count)

    each_bucket(hidden_ref.shape[0], bucket, UNROLL_BACKWARD)
    put_halves(where_ref, grad_ref, keep_ref, send_ref)


def last_kernel(ways, where_ref, upstream_ref, hidden_ref, kids_ref, near_ref, scale_ref, *refs):
    rows_ref, keep_ref, send_ref, norms_ref, grad_ref = refs[4 * ways :]
    mean_row, inv_std, count = moments(sum_refs(refs[:ways]))
    backs = [sum_refs(refs[i * ways : (i + 1) * ways]) for i in (1, 2, 3)]
    back = backs[0]
    rows = [totals[0:2] for totals in backs]
    norms_ref[...] = jnp.concatenate(rows + [jnp.zeros_like(rows[0])], axis=0)
    channels = hidden_ref.shape[2]
    used = kids_ref.shape[1]
    if grad_ref.shape[0] > used:
        grad_ref[used:] = jnp.zeros((grad_ref.shape[0] - used, channels), F32)
    total = None
    for b in range(hidden_ref.shape[0]):
        live, _ = live_mask(near_ref, b, channels)
        centred = (hidden_ref[b] - mean_row) * inv_std
        rows_grad = norm_back(
            upstream_ref[b], centred, live, inv_std, scale_ref[0:1], back, count
        ).astype(BF16)
        rows_ref[b] = rows_grad
        product = mm(kids_ref[b], rows_grad)
        total = product if total is None else total + product
    grad_ref[:used] = total
    put_halves(where_ref, grad_ref, keep_ref, send_ref)


def input_kernel(where_ref, rows_ref, which_ref, tables_ref, weight_ref, own_ref, send_ref):
    in_channels, fine_rows = own_ref.shape
    step = 256
    for b, input_ref in enumerate((own_ref, send_ref)):
        pieces = mm_t(weight_ref[...], rows_ref[b]).astype(BF16)
        first, last = parent_rows(tables_ref[b], fine_rows)
        for at in range(0, fine_rows, step):
            full = mm_t(pieces, parent_hits(first, last, at, step))
            code = jnp.broadcast_to(which_ref[b, 0:1, at : at + step], (in_channels, step))
            out = jnp.zeros((in_channels, step), F32)
            for k in range(full.shape[0] // in_channels):
                out = out + jnp.where(code == float(k + 1), full[in_channels * k : in_channels * (k + 1)], 0.0)
            input_ref[:, at : at + step] = out.astype(BF16)


def place_outputs_kernel(where_ref, own_features, other_features, own_input, other_input, features, inputs, leaving):
    copies = [
        pltpu.make_async_copy(source, target.at[place], leaving.at[i])
        for i, (source, target, place) in enumerate(
            (
                (own_features, features, where_ref[1]),
                (other_features, features, 1 - where_ref[1]),
                (own_input, inputs, where_ref[1]),
                (other_input, inputs, 1 - where_ref[1]),
            )
        )
    ]
    for copy in copies:
        copy.start()
    for copy in copies:
        copy.wait()


def split_kernel(sections, depths, parts, where_ref, *refs):
    pairs, outs = refs[: 2 * len(parts)], refs[2 * len(parts) :]
    total = sum(parts)
    for j in range(sections):
        block = where_ref[2] ^ j
        base = 0
        for i, size in enumerate(parts):
            wide = depths * size
            rows = pl.ds(pl.multiple_of(block * wide, 16), wide)
            both = (pairs[2 * i][rows].astype(F32) + pairs[2 * i + 1][rows].astype(F32)).astype(BF16)
            for z in range(depths):
                outs[j][z * total + base : z * total + base + size] = both[z * size : (z + 1) * size]
            base += size


def spread_kernel(depths, sources, where_ref, *refs):
    blocks, halves, outs = refs[:sources], refs[sources : sources + 2], refs[sources + 2 :]
    small = halves[0].shape[0] // depths
    size = outs[0].shape[0] - small
    for j in range(depths):
        place = where_ref[3] ^ j
        rows = pl.ds(pl.multiple_of(place * size, 16), size)
        outs[j][:size] = tree_sum([ref[rows].astype(F32) for ref in blocks]).astype(BF16)
        rows = pl.ds(pl.multiple_of(place * small, 16), small)
        outs[j][size:] = (halves[0][rows].astype(F32) + halves[1][rows].astype(F32)).astype(BF16)


def add_kernel(where_ref, *refs):
    refs[-1][...] = sum_refs(refs[:-1]).astype(BF16)


def high_and_low(exact):
    high = exact.astype(BF16)
    low = (exact - high.astype(F32)).astype(BF16)
    return jnp.concatenate([high, low], axis=0)


def one_value(high_low):
    rows = high_low.shape[0] // 2
    return high_low[:rows].astype(F32) + high_low[rows:].astype(F32)


def join_kernel(small, where_ref, *refs):
    pieces, norm_refs, out_ref = refs[:-3], refs[-3:-1], refs[-1]
    size = pieces[0].shape[0] - small
    base = len(pieces) * size
    for j, ref in enumerate(pieces):
        place = where_ref[3] ^ j
        out_ref[pl.ds(pl.multiple_of(place * size, 16), size)] = ref[:size]
        out_ref[pl.ds(pl.multiple_of(base + place * small, 16), small)] = ref[size:]
    out_ref[base + len(pieces) * small :] = high_and_low(sum_refs(norm_refs))


def gather_kernel(size, where_ref, *refs):
    pieces, (out_ref, scale_ref, shift_ref) = refs[:-3], refs[-3:]
    for j, ref in enumerate(pieces):
        out_ref[pl.ds(pl.multiple_of((where_ref[2] ^ j) * size, 16), size)] = ref[:size]
    tails = [ref[size:].astype(F32) for ref in pieces]
    middle = tails[0].shape[0] - 16
    out_ref[len(pieces) * size :] = tree_sum([tail[:middle] for tail in tails]).astype(BF16)
    sums = tree_sum([one_value(tail[middle:]) for tail in tails])
    shift_ref[...] = jnp.concatenate([sums[2 * t : 2 * t + 1] for t in range(3)], axis=0)
    scale_ref[...] = jnp.concatenate([sums[2 * t + 1 : 2 * t + 2] for t in range(3)], axis=0)


def final_kernel(parts, blocks, flip, where_ref, half_ref, *refs):
    count = len(parts) + 1
    outs, scratches, leaving = refs[-2 * count - 1 : -count - 1], refs[-count - 1 : -1], refs[-1]
    core = where_ref[1]
    place = 1 - core if flip else core
    total = sum(parts)
    base = 0
    copies, extras = [], []
    for i in range(count):
        scratch, out = scratches[i], outs[i]
        half = scratch.shape[0]
        if i < len(parts):
            size = parts[i]
            for t in range(blocks):
                scratch[t * size : (t + 1) * size] = half_ref[t * total + base : t * total + base + size].astype(F32)
            base += size
        else:
            scratch[...] = half_ref[blocks * total :].astype(F32)
        sure = out.shape[0] - half
        copy = pltpu.make_async_copy(
            scratch.at[pl.ds(0, sure)],
            out.at[pl.ds(pl.multiple_of(place * half, 16), sure)],
            leaving.at[i, 0],
        )
        copy.start()
        copies.append(copy)
        if sure < half:
            extras.append(
                pltpu.make_async_copy(
                    scratch.at[pl.ds(sure, half - sure)], out.at[pl.ds(sure, half - sure)], leaving.at[i, 1]
                )
            )

    @pl.when(place == 0)
    def _():
        for copy in extras:
            copy.start()
        for copy in extras:
            copy.wait()

    for copy in copies:
        copy.wait()


def run(kernel, where, operands, outs, scratch=(), hbm_in=(), hbm_out=False, aliases=None, flops=0, grid=None):
    def place(i):
        return pltpu.HBM if i in hbm_in else pltpu.VMEM

    return pl.pallas_call(
        kernel,
        in_specs=[pl.BlockSpec(memory_space=pltpu.SMEM)]
        + [pl.BlockSpec(memory_space=place(i)) for i in range(len(operands))],
        out_specs=[pl.BlockSpec(memory_space=pltpu.HBM if hbm_out else pltpu.VMEM)] * len(outs),
        out_shape=outs,
        scratch_shapes=list(scratch),
        input_output_aliases=aliases or {},
        compiler_params=pltpu.CompilerParams(vmem_limit_bytes=VMEM_BYTES),
        cost_estimate=pl.CostEstimate(flops=flops, bytes_accessed=1 << 20, transcendentals=0),
    )(where, *operands)


def swapped(value, axis, step):
    count = lax.axis_size(axis)
    return lax.ppermute(value, axis, [(i, i ^ step) for i in range(count)])


def depth_sums(value):
    return [value] + [swapped(value, "dp", step) for step in range(2, lax.axis_size("dp"), 2)]


def local(
    voxel_feats, down_map, neighbours, w_down, w_first, w_second, bn_scale, bn_shift, out_grad
):
    sections = lax.axis_size("section")
    depths = lax.axis_size("dp") // 2
    mine = voxel_feats.shape[0] // sections
    section, bucket = lax.axis_index("section"), lax.axis_index("dp")
    core = bucket % 2
    base = section * mine
    where = jnp.stack([base + core, core, section, bucket // 2, base + 1 - core]).astype(jnp.int32)
    voxel_feats = jnp.swapaxes(voxel_feats, 1, 2)
    near = jnp.swapaxes(neighbours, 0, 1)
    in_channels, fine_rows = voxel_feats.shape[1:]
    coarse_rows = neighbours.shape[2]
    channels = w_first.shape[2]
    offsets = down_map.shape[1]
    wide = offsets * in_channels
    flat_down = w_down.reshape(wide, channels)
    shape = jax.ShapeDtypeStruct
    rows_f32 = shape((mine, coarse_rows, channels), F32)
    rows_bf16 = shape((mine, coarse_rows, channels), BF16)
    one_bf16 = shape((coarse_rows, channels), BF16)
    sums = shape((8, channels), F32)
    table = shape((offsets, coarse_rows), jnp.int32)
    near_one = shape((w_first.shape[0], coarse_rows), jnp.int32)
    conv_flops = 8 * mine * w_first.shape[0] * coarse_rows * coarse_rows * channels

    def in_hbm(value):
        return pltpu.with_memory_space_constraint(value, pltpu.HBM)

    def cores(value):
        return swapped(value, "dp", 1)

    feats_hbm, down_hbm = in_hbm(voxel_feats), in_hbm(down_map)
    feats_one = shape((in_channels, fine_rows), BF16)
    send_feats, send_table, own_feats, own_table, weight_down = run(
        pack_kernel, where, [feats_hbm, down_hbm, in_hbm(flat_down)],
        [feats_one, table, feats_one, table, shape((wide, channels), BF16)],
        [pltpu.SemaphoreType.DMA((5,))], hbm_in=(0, 1, 2),
    )
    got_feats, got_table = cores(send_feats), cores(send_table)
    down_scratch = [pltpu.VMEM((wide, fine_rows), BF16), pltpu.VMEM((fine_rows, coarse_rows), BF16)]
    own_hidden, own_sums, own_kids, own_which, near_own, near_send = run(
        down_kernel, where,
        [own_feats, own_table, weight_down, near],
        [
            shape((coarse_rows, channels), F32), sums, shape((wide, coarse_rows), BF16),
            shape((8, fine_rows), F32), near_one, near_one,
        ],
        down_scratch,
        flops=2 * 10**9,
    )
    hidden_zero, part_zero, kids, which, tables = run(
        down_other_kernel, where,
        [got_feats, got_table, weight_down, own_hidden, own_sums, own_kids, own_which, own_table],
        [
            rows_f32, sums, shape((mine, wide, coarse_rows), BF16), shape((mine, 8, fine_rows), F32),
            shape((mine, offsets, coarse_rows), jnp.int32),
        ],
        down_scratch,
        flops=2 * 10**9,
    )
    stats_zero = depth_sums(part_zero)
    ways = len(stats_zero)
    (nears,) = run(
        near_kernel, where, [near_own, cores(near_send)],
        [shape((mine, w_first.shape[0], coarse_rows), jnp.int32)],
    )
    act_zero, hidden_one, part_one = run(
        functools.partial(forward_kernel, 0, False), where,
        [hidden_zero, nears, w_first, bn_scale, bn_shift] + stats_zero,
        [rows_bf16, rows_f32, sums],
        flops=conv_flops,
    )
    stats_one = depth_sums(part_one)
    grad_own, grad_send = run(grad_kernel, where, [out_grad], [one_bf16, one_bf16])
    grad_other = cores(grad_send)
    act_one, hidden_two, part_two = run(
        functools.partial(forward_kernel, 1, True), where,
        [hidden_one, nears, w_second, bn_scale, bn_shift] + stats_one,
        [rows_bf16, rows_bf16, sums],
        flops=conv_flops,
    )
    stats_two = depth_sums(part_two)
    features_own, features_send, up_two, back_part = run(
        output_kernel, where,
        [hidden_two, act_zero, grad_own, grad_other, nears, bn_scale, bn_shift] + stats_two,
        [one_bf16, one_bf16, rows_f32, sums],
        flops=10**9,
    )
    back_two = depth_sums(back_part)

    def part_rows(rows, pieces):
        return -(-rows // (pieces * 16)) * 16

    def half_shape(rows):
        return shape((rows, channels), BF16)

    def accumulator(rows):
        return [pltpu.VMEM((2 * rows, channels), F32)]

    blocks = sections * depths
    conv_rows = w_first.shape[0] * channels
    parts = [part_rows(conv_rows, 2 * blocks)] * 2
    small = part_rows(wide, 2 * depths)
    total = sum(parts)
    half = half_shape(blocks * parts[0])
    small_half = half_shape(depths * small)
    up_one, back_part, keep_second, send_second = run(
        functools.partial(backward_kernel, 2, False, ways), where,
        [up_two, hidden_two, hidden_one, act_one, nears, w_second, bn_scale, bn_shift]
        + stats_two + back_two + stats_one,
        [rows_f32, sums, half, half],
        accumulator(half.shape[0]),
        flops=conv_flops,
    )
    back_one = depth_sums(back_part)
    got_second = cores(send_second)
    features_other = cores(features_send)
    features_other, up_one = lax.optimization_barrier((features_other, up_one))
    up_zero, back_part, keep_first, send_first = run(
        functools.partial(backward_kernel, 1, True, ways), where,
        [up_one, hidden_one, hidden_zero, act_zero, nears, w_first, bn_scale, bn_shift]
        + stats_one + back_one + stats_zero + [up_two],
        [rows_f32, sums, half, half],
        accumulator(half.shape[0]),
        flops=conv_flops,
    )
    got_first = cores(send_first)
    section_out = run(
        functools.partial(split_kernel, sections, depths, parts), where,
        [keep_second, got_second, keep_first, got_first],
        [half_shape(depths * total)] * sections,
    )
    arrived = [section_out[0]] + [swapped(section_out[j], "section", j) for j in range(1, sections)]
    back_zero = depth_sums(back_part)
    rows_zero, keep_down, send_down, norm_rows = run(
        functools.partial(last_kernel, ways), where,
        [up_zero, hidden_zero, kids, nears, bn_scale] + stats_zero + back_zero + back_one + back_two,
        [rows_bf16, small_half, small_half, sums],
        accumulator(small_half.shape[0]),
        flops=10**9,
    )
    got_down = cores(send_down)
    depth_out = run(
        functools.partial(spread_kernel, depths, sections), where, arrived + [keep_down, got_down],
        [half_shape(total + small)] * depths,
    )
    arrived = [depth_out[0]] + [swapped(depth_out[j], "dp", 2 * j) for j in range(1, depths)]
    (summed,) = run(add_kernel, where, arrived, [half_shape(total + small)])
    arrived = [summed] + [swapped(summed, "dp", 2 * j) for j in range(1, depths)]
    (joined,) = run(
        functools.partial(join_kernel, small), where, arrived + [norm_rows, cores(norm_rows)],
        [half_shape(depths * (total + small) + 16)],
    )
    joined, rows_zero = lax.optimization_barrier((joined, rows_zero))
    arrived = [joined] + [swapped(joined, "section", j) for j in range(1, sections)]
    input_own, input_send = run(
        input_kernel, where, [rows_zero, which, tables, weight_down], [feats_one, feats_one],
        flops=4 * 10**9,
    )
    features, input_grad = run(
        place_outputs_kernel, where,
        [features_own, features_other, input_own, cores(input_send)],
        [rows_bf16, shape((mine, in_channels, fine_rows), BF16)],
        [pltpu.SemaphoreType.DMA((4,))],
        hbm_out=True,
    )
    arrived, features, input_grad = lax.optimization_barrier((arrived, features, input_grad))
    norms = shape(bn_scale.shape, F32)
    gathered, grad_scale, grad_shift = run(
        functools.partial(gather_kernel, depths * total), where, arrived,
        [half_shape(blocks * total + depths * small), norms, norms],
    )
    other = cores(gathered)
    grads = [shape((conv_rows, channels), F32)] * 2 + [shape((wide, channels), F32)]
    staging = [pltpu.VMEM((half.shape[0], channels), F32)] * 2 + [
        pltpu.VMEM((small_half.shape[0], channels), F32),
        pltpu.SemaphoreType.DMA((3, 2)),
    ]
    grads_out = run(
        functools.partial(final_kernel, parts, blocks, False), where, [gathered], grads, staging,
        hbm_out=True, flops=10**9,
    )
    grad_second, grad_first, grad_down = run(
        functools.partial(final_kernel, parts, blocks, True), where, [other] + list(grads_out), grads, staging,
        hbm_in=(1, 2, 3), hbm_out=True, aliases={2: 0, 3: 1, 4: 2}, flops=10**9,
    )
    return (
        features,
        jnp.swapaxes(input_grad, 1, 2),
        grad_down.reshape(w_down.shape),
        grad_first.reshape(w_first.shape),
        grad_second.reshape(w_second.shape),
        grad_scale,
        grad_shift,
    )


def solution(mesh):
    in_specs = (
        P(None, "dp", None),
        P(None, None, "dp"),
        P(None, None, "dp"),
        P(),
        P(),
        P(),
        P(),
        P(),
        P(None, "dp", None),
    )
    out_specs = (P("section", "dp", None), P("section", "dp", None), P(), P(), P(), P(), P())
    return jax.shard_map(local, mesh=mesh, in_specs=in_specs, out_specs=out_specs, check_vma=False)
```

profile of v0, /device:TPU:1, one launch (start us, length us, event | category | flops | bytes accessed | tf_op | source)
XLA Modules:
  0.0 136.3 jit_solution(6425941164990410058)
XLA Ops:
  0.7 1.7 %shard_map.144 = (bf16[64,2048]{1,0:T(8,128)(2,1)S(1)}, s32[8,512]{1,0:T(8,128)S(1)}, bf16[64,2048]{1,0:T(8,128)(2,1)S(1)}, s32[8,512]{1,0:T(8,128)S(1)}, bf16[512,128]{1,0:T(8,128)(2,1)S(1)}) custom-call(s32[5]{0:T(128)S(1)} %stack.23.where_ref, bf16[8,64,2048]{2,1,0:T(8,128)(2,1)} %bitcast.13, s32[8,8,512]{2,1,0:T(8,128)} %down_hbm.1, ...), custom_call_target="tpu_custom_call" | custom-call | bytes 1048576 | tf_op jit(solution)/shard_map/pallas_call | solution.py:510
  3.0 2.7 %shard_map.145 = (f32[512,128]{1,0:T(8,128)S(1)}, f32[8,128]{1,0:T(8,128)S(1)}, bf16[512,512]{1,0:T(8,128)(2,1)S(1)}, f32[8,2048]{1,0:T(8,128)S(1)}, s32[27,512]{1,0:T(8,128)S(1)}, /*index=5*/s32[27,512]{1,0:T(8,128)S(1)}) custom-call(s32[5]{0:T(128)S(1)} %stack.23.where_ref, bf16[64,2048]{1,0:T(8,128)(2,1)S(1)} %get-tuple-element.81.feats_ref, ...), custom_call_target="tpu_custom_call" | custom-call | flops 2000000000 | bytes 1048576 | tf_op jit(solution)/shard_map/pallas_call | solution.py:510
  5.9 2.7 %shard_map.146 = (f32[2,512,128]{2,1,0:T(8,128)S(1)}, f32[8,128]{1,0:T(8,128)S(1)}, bf16[2,512,512]{2,1,0:T(8,128)(2,1)S(1)}, f32[2,8,2048]{2,1,0:T(8,128)S(1)}, s32[2,8,512]{2,1,0:T(8,128)S(1)}) custom-call(s32[5]{0:T(128)S(1)} %stack.23.where_ref, bf16[64,2048]{1,0:T(8,128)(2,1)S(1)} %collective-permute-done.feats_ref, ...), custom_call_target="tpu_custom_call" | custom-call | flops 2000000000 | bytes 1048576 | tf_op jit(solution)/shard_map/pallas_call | solution.py:510
  8.6 4.8 %collective-permute-start.5 = (f32[8,128]{1,0:T(8,128)S(1)}, f32[8,128]{1,0:T(8,128)S(1)}, u32[]{:S(2)}, u32[]{:S(2)}) collective-permute-start(f32[8,128]{1,0:T(8,128)S(1)} %get-tuple-element.90.refs_0_.refs_16_), channel_id=1, source_target_pairs={{0,6},{1,7},{2,4},{3,5},{4,2},{5,3},{6,0},{7,1},{8,14},{9,15},{10,... | collective-permute-start | bytes 12296 | tf_op jit(solution)/shard_map/ppermute | solution.py:525
  14.4 2.4 %collective-permute-done.4.refs_2_.refs_18_ = f32[8,128]{1,0:T(8,128)S(1)} collective-permute-done((f32[8,128]{1,0:T(8,128)S(1)}, f32[8,128]{1,0:T(8,128)S(1)}, u32[]{:S(2)}, u32[]{:S(2)}) %collective-permute-start.4) | collective-permute-done | bytes 4128 | tf_op jit(solution)/shard_map/ppermute | solution.py:525
  16.8 7.2 %shard_map.148 = (bf16[2,512,128]{2,1,0:T(8,128)(2,1)S(1)}, f32[2,512,128]{2,1,0:T(8,128)S(1)}, f32[8,128]{1,0:T(8,128)S(1)}) custom-call(s32[5]{0:T(128)S(1)} %stack.23.where_ref, f32[2,512,128]{2,1,0:T(8,128)S(1)} %get-tuple-element.87.hidden_ref.refs_2_, s32[2,27,512]{2,1,0:T(8,128)S(1)} %shard_map.147.near_ref.refs_4_, ...), custom_call_target="tpu_custom_call" | custom-call | flops 14495514624 | bytes 1048576 | tf_op jit(solution)/shard_map/pallas_call | solution.py:510
  24.0 1.5 %collective-permute-start.8 = (f32[8,128]{1,0:T(8,128)S(1)}, f32[8,128]{1,0:T(8,128)S(1)}, u32[]{:S(2)}, u32[]{:S(2)}) collective-permute-start(f32[8,128]{1,0:T(8,128)S(1)} %get-tuple-element.92.refs_0_.refs_16_.refs_8_), channel_id=1, source_target_pairs={{0,6},{1,7},{2,4},{3,5},{4,2},{5,3},{6,0},{7,1},{8,14},{9,15},{10,... | collective-permute-start | bytes 12296 | tf_op jit(solution)/shard_map/ppermute | solution.py:525
  25.6 2.0 %collective-permute-start.6 = (f32[8,128]{1,0:T(8,128)S(1)}, f32[8,128]{1,0:T(8,128)S(1)}, u32[]{:S(2)}, u32[]{:S(2)}) collective-permute-start(f32[8,128]{1,0:T(8,128)S(1)} %get-tuple-element.92.refs_0_.refs_16_.refs_8_), channel_id=1, source_target_pairs={{0,2},{1,3},{2,0},{3,1},{4,6},{5,7},{6,4},{7,5},{8,10},{9,11},{10,... | collective-permute-start | bytes 12296 | tf_op jit(solution)/shard_map/ppermute | solution.py:525
  28.2 2.4 %collective-permute-start.9 = (bf16[512,128]{1,0:T(8,128)(2,1)S(1)}, bf16[512,128]{1,0:T(8,128)(2,1)S(1)}, u32[]{:S(2)}, u32[]{:S(2)}) collective-permute-start(bf16[512,128]{1,0:T(8,128)(2,1)S(1)} %get-tuple-element.96), channel_id=1, source_target_pairs={{0,1},{1,0},{2,3},{3,2},{4,5},{5,4},{6,7},{7,6},{8,9},{9,8},{10,11... | collective-permute-start | bytes 393224 | tf_op jit(solution)/shard_map/ppermute | solution.py:525
  30.6 7.4 %shard_map.149 = (bf16[2,512,128]{2,1,0:T(8,128)(2,1)S(1)}, bf16[2,512,128]{2,1,0:T(8,128)(2,1)S(1)}, f32[8,128]{1,0:T(8,128)S(1)}) custom-call(s32[5]{0:T(128)S(1)} %stack.23.where_ref, f32[2,512,128]{2,1,0:T(8,128)S(1)} %get-tuple-element.91.hidden_ref.refs_2_.refs_1_, s32[2,27,512]{2,1,0:T(8,128)S(1)} %shard_map.147.near_ref.refs_4_, ...), custom_call_target="tpu_custom_call" | custom-call | flops 14495514624 | bytes 1048576 | tf_op jit(solution)/shard_map/pallas_call | solution.py:510
  38.0 1.2 collective-permute-start.12
  39.2 2.4 %collective-permute-start.10 = (f32[8,128]{1,0:T(8,128)S(1)}, f32[8,128]{1,0:T(8,128)S(1)}, u32[]{:S(2)}, u32[]{:S(2)}) collective-permute-start(f32[8,128]{1,0:T(8,128)S(1)} %get-tuple-element.97.refs_0_.refs_8_), channel_id=1, source_target_pairs={{0,2},{1,3},{2,0},{3,1},{4,6},{5,7},{6,4},{7,5},{8,10},{9,11},{10,... | collective-permute-start | bytes 12296 | tf_op jit(solution)/shard_map/ppermute | solution.py:525
  42.6 1.2 shard_map.151
  43.8 2.1 %collective-permute-start.15 = (f32[8,128]{1,0:T(8,128)S(1)}, f32[8,128]{1,0:T(8,128)S(1)}, u32[]{:S(2)}, u32[]{:S(2)}) collective-permute-start(f32[8,128]{1,0:T(8,128)S(1)} %get-tuple-element.100.refs_12_), channel_id=1, source_target_pairs={{0,6},{1,7},{2,4},{3,5},{4,2},{5,3},{6,0},{7,1},{8,14},{9,15},{10,... | collective-permute-start | bytes 12296 | tf_op jit(solution)/shard_map/ppermute | solution.py:525
  46.5 0.9 collective-permute-start.13
  47.4 4.3 %collective-permute-start.17 = (bf16[512,128]{1,0:T(8,128)(2,1)S(1)}, bf16[512,128]{1,0:T(8,128)(2,1)S(1)}, u32[]{:S(2)}, u32[]{:S(2)}) collective-permute-start(bf16[512,128]{1,0:T(8,128)(2,1)S(1)} %get-tuple-element.103), channel_id=1, source_target_pairs={{0,1},{1,0},{2,3},{3,2},{4,5},{5,4},{6,7},{7,6},{8,9},{9,8},{10,11... | collective-permute-start | bytes 393224 | tf_op jit(solution)/shard_map/ppermute | solution.py:525
  51.7 8.2 %shard_map.152 = (f32[2,512,128]{2,1,0:T(8,128)S(1)}, f32[8,128]{1,0:T(8,128)S(1)}, bf16[1792,128]{1,0:T(8,128)(2,1)S(1)}, bf16[1792,128]{1,0:T(8,128)(2,1)S(1)}) custom-call(s32[5]{0:T(128)S(1)} %stack.23.where_ref, f32[2,512,128]{2,1,0:T(8,128)S(1)} %get-tuple-element.98.refs_0_.refs_20_, bf16[2,512,128]{2,1,0:T(8,128)(2,1)S(1)} %get-tuple-element.93.hidden_ref.refs_1_, ...), custom_call_target="tpu_custom_call" | custom-call | flops 14495514624 | bytes 1048576 | tf_op jit(solution)/shard_map/pallas_call | solution.py:510
  60.0 1.2 collective-permute-start.20
  61.2 2.4 %collective-permute-start.18 = (f32[8,128]{1,0:T(8,128)S(1)}, f32[8,128]{1,0:T(8,128)S(1)}, u32[]{:S(2)}, u32[]{:S(2)}) collective-permute-start(f32[8,128]{1,0:T(8,128)S(1)} %get-tuple-element.106.refs_12_.refs_8_), channel_id=1, source_target_pairs={{0,2},{1,3},{2,0},{3,1},{4,6},{5,7},{6,4},{7,5},{8,10},{9,11},{10,... | collective-permute-start | bytes 12296 | tf_op jit(solution)/shard_map/ppermute | solution.py:525
  63.6 2.4 %collective-permute-start.16 = (bf16[1792,128]{1,0:T(8,128)(2,1)S(1)}, bf16[1792,128]{1,0:T(8,128)(2,1)S(1)}, u32[]{:S(2)}, u32[]{:S(2)}) collective-permute-start(bf16[1792,128]{1,0:T(8,128)(2,1)S(1)} %get-tuple-element.102), channel_id=1, source_target_pairs={{0,1},{1,0},{2,3},{3,2},{4,5},{5,4},{6,7},{7,6},{8,9},{9,8},{10,11... | collective-permute-start | bytes 1376264 | tf_op jit(solution)/shard_map/ppermute | solution.py:525
  66.0 8.5 %shard_map.153 = (f32[2,512,128]{2,1,0:T(8,128)S(1)}, f32[8,128]{1,0:T(8,128)S(1)}, bf16[1792,128]{1,0:T(8,128)(2,1)S(1)}, bf16[1792,128]{1,0:T(8,128)(2,1)S(1)}) custom-call(s32[5]{0:T(128)S(1)} %stack.23.where_ref, f32[2,512,128]{2,1,0:T(8,128)S(1)} %get-tuple-element.105.refs_0_, f32[2,512,128]{2,1,0:T(8,128)S(1)} %get-tuple-element.91.hidden_ref.refs_2_.refs_1_, ...), custom_call_target="tpu_custom_call" | custom-call | flops 14495514624 | bytes 1048576 | tf_op jit(solution)/shard_map/pallas_call | solution.py:510
  74.5 2.7 %collective-permute-start.21 = (bf16[1792,128]{1,0:T(8,128)(2,1)S(1)}, bf16[1792,128]{1,0:T(8,128)(2,1)S(1)}, u32[]{:S(2)}, u32[]{:S(2)}) collective-permute-start(bf16[1792,128]{1,0:T(8,128)(2,1)S(1)} %get-tuple-element.108), channel_id=1, source_target_pairs={{0,1},{1,0},{2,3},{3,2},{4,5},{5,4},{6,7},{7,6},{8,9},{9,8},{10,11... | collective-permute-start | bytes 1376264 | tf_op jit(solution)/shard_map/ppermute | solution.py:525
  77.3 1.4 %collective-permute-done.21.refs_3_ = bf16[1792,128]{1,0:T(8,128)(2,1)S(1)} collective-permute-done((bf16[1792,128]{1,0:T(8,128)(2,1)S(1)}, bf16[1792,128]{1,0:T(8,128)(2,1)S(1)}, u32[]{:S(2)}, u32[]{:S(2)}) %collective-permute-start.21) | collective-permute-done | bytes 458784 | tf_op jit(solution)/shard_map/ppermute | solution.py:525
  79.5 1.3 collective-permute-start.22
  80.8 1.2 collective-permute-start.23
  82.2 1.1 collective-permute-start.27
  84.0 2.4 %collective-permute-done.27.refs_7_ = f32[8,128]{1,0:T(8,128)S(1)} collective-permute-done((f32[8,128]{1,0:T(8,128)S(1)}, f32[8,128]{1,0:T(8,128)S(1)}, u32[]{:S(2)}, u32[]{:S(2)}) %collective-permute-start.27) | collective-permute-done | bytes 4128 | tf_op jit(solution)/shard_map/ppermute | solution.py:525
  86.7 2.5 %collective-permute-done.25.refs_5_ = f32[8,128]{1,0:T(8,128)S(1)} collective-permute-done((f32[8,128]{1,0:T(8,128)S(1)}, f32[8,128]{1,0:T(8,128)S(1)}, u32[]{:S(2)}, u32[]{:S(2)}) %collective-permute-start.25) | collective-permute-done | bytes 4128 | tf_op jit(solution)/shard_map/ppermute | solution.py:525
  89.2 1.1 shard_map.155
  90.3 3.3 %collective-permute-start.28 = (bf16[256,128]{1,0:T(8,128)(2,1)S(1)}, bf16[256,128]{1,0:T(8,128)(2,1)S(1)}, u32[]{:S(2)}, u32[]{:S(2)}) collective-permute-start(bf16[256,128]{1,0:T(8,128)(2,1)S(1)} %get-tuple-element.117), channel_id=1, source_target_pairs={{0,1},{1,0},{2,3},{3,2},{4,5},{5,4},{6,7},{7,6},{8,9},{9,8},{10,11... | collective-permute-start | bytes 196616 | tf_op jit(solution)/shard_map/ppermute | solution.py:525
  93.6 0.9 collective-permute-done.28.refs_5_
  95.3 1.4 %collective-permute-start.30 = (bf16[288,128]{1,0:T(8,128)(2,1)S(1)}, bf16[288,128]{1,0:T(8,128)(2,1)S(1)}, u32[]{:S(2)}, u32[]{:S(2)}) collective-permute-start(bf16[288,128]{1,0:T(8,128)(2,1)S(1)} %get-tuple-element.120), channel_id=1, source_target_pairs={{0,4},{1,5},{2,6},{3,7},{4,0},{5,1},{6,2},{7,3},{8,12},{9,13},{10,... | collective-permute-start | bytes 221192 | tf_op jit(solution)/shard_map/ppermute | solution.py:525
  96.7 2.1 %collective-permute-start.31 = (bf16[288,128]{1,0:T(8,128)(2,1)S(1)}, bf16[288,128]{1,0:T(8,128)(2,1)S(1)}, u32[]{:S(2)}, u32[]{:S(2)}) collective-permute-start(bf16[288,128]{1,0:T(8,128)(2,1)S(1)} %get-tuple-element.121), channel_id=1, source_target_pairs={{0,6},{1,7},{2,4},{3,5},{4,2},{5,3},{6,0},{7,1},{8,14},{9,15},{10,... | collective-permute-start | bytes 221192 | tf_op jit(solution)/shard_map/ppermute | solution.py:525
  99.6 3.2 %collective-permute-done.31.refs_3_ = bf16[288,128]{1,0:T(8,128)(2,1)S(1)} collective-permute-done((bf16[288,128]{1,0:T(8,128)(2,1)S(1)}, bf16[288,128]{1,0:T(8,128)(2,1)S(1)}, u32[]{:S(2)}, u32[]{:S(2)}) %collective-permute-start.31) | collective-permute-done | bytes 73760 | tf_op jit(solution)/shard_map/ppermute | solution.py:525
  103.4 1.1 collective-permute-start.34
  104.5 1.8 %collective-permute-start.33 = (bf16[288,128]{1,0:T(8,128)(2,1)S(1)}, bf16[288,128]{1,0:T(8,128)(2,1)S(1)}, u32[]{:S(2)}, u32[]{:S(2)}) collective-permute-start(bf16[288,128]{1,0:T(8,128)(2,1)S(1)} %shard_map.157.refs_0_), channel_id=1, source_target_pairs={{0,4},{1,5},{2,6},{3,7},{4,0},{5,1},{6,2},{7,3},{8,12},{9,13},{10,... | collective-permute-start | bytes 221192 | tf_op jit(solution)/shard_map/ppermute | solution.py:525
  107.0 2.9 %collective-permute-start.35 = (f32[8,128]{1,0:T(8,128)S(1)}, f32[8,128]{1,0:T(8,128)S(1)}, u32[]{:S(2)}, u32[]{:S(2)}) collective-permute-start(f32[8,128]{1,0:T(8,128)S(1)} %get-tuple-element.122.refs_4_), channel_id=1, source_target_pairs={{0,1},{1,0},{2,3},{3,2},{4,5},{5,4},{6,7},{7,6},{8,9},{9,8},{10,11... | collective-permute-start | bytes 12296 | tf_op jit(solution)/shard_map/ppermute | solution.py:525
  110.7 2.5 %collective-permute-done.33.refs_2_ = bf16[288,128]{1,0:T(8,128)(2,1)S(1)} collective-permute-done((bf16[288,128]{1,0:T(8,128)(2,1)S(1)}, bf16[288,128]{1,0:T(8,128)(2,1)S(1)}, u32[]{:S(2)}, u32[]{:S(2)}) %collective-permute-start.33) | collective-permute-done | bytes 73760 | tf_op jit(solution)/shard_map/ppermute | solution.py:525
  113.8 1.4 %collective-permute-start.38 = (bf16[1168,128]{1,0:T(8,128)(2,1)S(1)}, bf16[1168,128]{1,0:T(8,128)(2,1)S(1)}, u32[]{:S(2)}, u32[]{:S(2)}) collective-permute-start(bf16[1168,128]{1,0:T(8,128)(2,1)S(1)} %shard_map.158.refs_0_), channel_id=1, source_target_pairs={{0,24},{8,16},{16,8},{24,0},{1,25},{9,17},{17,9},{25,1},{2,26},{10... | collective-permute-start | bytes 897032 | tf_op jit(solution)/shard_map/ppermute | solution.py:525
  115.2 0.9 collective-permute-start.37
  116.5 3.2 %shard_map.159 = (bf16[64,2048]{1,0:T(8,128)(2,1)S(1)}, bf16[64,2048]{1,0:T(8,128)(2,1)S(1)}) custom-call(s32[5]{0:T(128)S(1)} %stack.23.where_ref, bf16[2,512,128]{2,1,0:T(8,128)(2,1)S(1)} %get-tuple-element.127.rows_ref, f32[2,8,2048]{2,1,0:T(8,128)S(1)} %get-tuple-element.128.which_ref, s32[2,8,512]{2,1,0:T(8,128)S(1)} %get-tuple-element.129.tables_ref, ...), custom_call_target="tpu_custom_call" | custom-call | flops 4000000000 | bytes 1048576 | tf_op jit(solution)/shard_map/pallas_call | solution.py:510
  119.7 1.9 %collective-permute-start.39 = (bf16[64,2048]{1,0:T(8,128)(2,1)S(1)}, bf16[64,2048]{1,0:T(8,128)(2,1)S(1)}, u32[]{:S(2)}, u32[]{:S(2)}) collective-permute-start(bf16[64,2048]{1,0:T(8,128)(2,1)S(1)} %get-tuple-element.131), channel_id=1, source_target_pairs={{0,1},{1,0},{2,3},{3,2},{4,5},{5,4},{6,7},{7,6},{8,9},{9,8},{10,11... | collective-permute-start | bytes 786440 | tf_op jit(solution)/shard_map/ppermute | solution.py:525
  121.6 1.2 collective-permute-done.39.other_input
  122.8 1.5 %shard_map.160 = (bf16[2,512,128]{2,1,0:T(8,128)(2,1)}, bf16[2,64,2048]{2,1,0:T(8,128)(2,1)}) custom-call(s32[5]{0:T(128)S(1)} %stack.23.where_ref, bf16[512,128]{1,0:T(8,128)(2,1)S(1)} %get-tuple-element.125.own_features, bf16[512,128]{1,0:T(8,128)(2,1)S(1)} %collective-permute-done.17.other_features, bf16[64,2048]{1,0:T(8,128)(2,1)S(1)} %get-tuple-element.130.own_input, ...), custom_call_target="tpu_custom_call" | custom-call | bytes 1048576 | tf_op jit(solution)/shard_map/pallas_call | solution.py:510
  124.3 5.9 %collective-permute-done.37.refs_2_ = bf16[1168,128]{1,0:T(8,128)(2,1)S(1)} collective-permute-done((bf16[1168,128]{1,0:T(8,128)(2,1)S(1)}, bf16[1168,128]{1,0:T(8,128)(2,1)S(1)}, u32[]{:S(2)}, u32[]{:S(2)}) %collective-permute-start.37) | collective-permute-done | bytes 299040 | tf_op jit(solution)/shard_map/ppermute | solution.py:525
  130.2 1.2 shard_map.161
  132.0 1.9 %shard_map.162 = (f32[3456,128]{1,0:T(8,128)}, f32[3456,128]{1,0:T(8,128)}, f32[512,128]{1,0:T(8,128)}) custom-call(s32[5]{0:T(128)S(1)} %stack.23.where_ref, bf16[3840,128]{1,0:T(8,128)(2,1)S(1)} %get-tuple-element.140.half_ref), custom_call_target="tpu_custom_call" | custom-call | flops 1000000000 | bytes 1048576 | tf_op jit(solution)/shard_map/pallas_call | solution.py:510
  134.2 1.9 %shard_map.163 = (f32[3456,128]{1,0:T(8,128)}, f32[3456,128]{1,0:T(8,128)}, f32[512,128]{1,0:T(8,128)}) custom-call(s32[5]{0:T(128)S(1)} %stack.23.where_ref, bf16[3840,128]{1,0:T(8,128)(2,1)S(1)} %collective-permute-done.40.half_ref, f32[3456,128]{1,0:T(8,128)} %get-tuple-element.141.refs_0_, ...), custom_call_target="tpu_custom_call", output_to_operand_aliasing={{0}: (2, {}), {1}: (3, {}), {2}: (4, {})} | custom-call | flops 1000000000 | bytes 1048576 | tf_op jit(solution)/shard_map/pallas_call | solution.py:510
  (67 shorter events, 11.4 us)
Async XLA Ops:
  0.6 2.4 %copy-start.3 = (s32[8,27,512]{2,0,1:T(8,128)S(1)}, s32[8,27,512]{2,0,1:T(8,128)}, u32[]{:S(2)}) copy-start(s32[8,27,512]{2,0,1:T(8,128)} %param.11) | copy-start | bytes 1327108
  2.4 3.4 %collective-permute-start = (bf16[64,2048]{1,0:T(8,128)(2,1)S(1)}, bf16[64,2048]{1,0:T(8,128)(2,1)S(1)}, u32[]{:S(2)}, u32[]{:S(2)}) collective-permute-start(bf16[64,2048]{1,0:T(8,128)(2,1)S(1)} %get-tuple-element.78), channel_id=1, source_target_pairs={{0,1},{1,0},{2,3},{3,2},{4,5},{5,4},{6,7},{7,6},{8,9},{9,8},{10,11... | collective-permute-start | bytes 786440 | tf_op jit(solution)/shard_map/ppermute | solution.py:525
  2.6 3.3 %collective-permute-start.1 = (s32[8,512]{1,0:T(8,128)S(1)}, s32[8,512]{1,0:T(8,128)S(1)}, u32[]{:S(2)}, u32[]{:S(2)}) collective-permute-start(s32[8,512]{1,0:T(8,128)S(1)} %get-tuple-element.79), channel_id=1, source_target_pairs={{0,1},{1,0},{2,3},{3,2},{4,5},{5,4},{6,7},{7,6},{8,9},{9,8},{10,11... | collective-permute-start | bytes 49160 | tf_op jit(solution)/shard_map/ppermute | solution.py:525
  5.7 8.0 %collective-permute-start.2 = (s32[27,512]{1,0:T(8,128)S(1)}, s32[27,512]{1,0:T(8,128)S(1)}, u32[]{:S(2)}, u32[]{:S(2)}) collective-permute-start(s32[27,512]{1,0:T(8,128)S(1)} %get-tuple-element.89), channel_id=1, source_target_pairs={{0,1},{1,0},{2,3},{3,2},{4,5},{5,4},{6,7},{7,6},{8,9},{9,8},{10,11... | collective-permute-start | bytes 165896 | tf_op jit(solution)/shard_map/ppermute | solution.py:525
  5.8 10.9 %copy-start.2 = (bf16[27,128,128]{2,1,0:T(8,128)(2,1)S(1)}, bf16[27,128,128]{2,1,0:T(8,128)(2,1)}, u32[]{:S(2)}) copy-start(bf16[27,128,128]{2,1,0:T(8,128)(2,1)} %refs_5_.3) | copy-start | bytes 2654212
  5.9 10.9 %copy-start.4 = (f32[3,128]{1,0:T(4,128)S(1)}, f32[3,128]{1,0:T(4,128)}, u32[]{:S(2)}) copy-start(f32[3,128]{1,0:T(4,128)} %refs_7_.3) | copy-start | bytes 4612
  5.9 10.9 %copy-start.5 = (f32[3,128]{1,0:T(4,128)S(1)}, f32[3,128]{1,0:T(4,128)}, u32[]{:S(2)}) copy-start(f32[3,128]{1,0:T(4,128)} %scale_ref.7) | copy-start | bytes 4612
  8.6 5.8 %collective-permute-start.5 = (f32[8,128]{1,0:T(8,128)S(1)}, f32[8,128]{1,0:T(8,128)S(1)}, u32[]{:S(2)}, u32[]{:S(2)}) collective-permute-start(f32[8,128]{1,0:T(8,128)S(1)} %get-tuple-element.90.refs_0_.refs_16_), channel_id=1, source_target_pairs={{0,6},{1,7},{2,4},{3,5},{4,2},{5,3},{6,0},{7,1},{8,14},{9,15},{10,... | collective-permute-start | bytes 12296 | tf_op jit(solution)/shard_map/ppermute | solution.py:525
  13.4 3.4 %collective-permute-start.4 = (f32[8,128]{1,0:T(8,128)S(1)}, f32[8,128]{1,0:T(8,128)S(1)}, u32[]{:S(2)}, u32[]{:S(2)}) collective-permute-start(f32[8,128]{1,0:T(8,128)S(1)} %get-tuple-element.90.refs_0_.refs_16_), channel_id=1, source_target_pairs={{0,4},{1,5},{2,6},{3,7},{4,0},{5,1},{6,2},{7,3},{8,12},{9,13},{10,... | collective-permute-start | bytes 12296 | tf_op jit(solution)/shard_map/ppermute | solution.py:525
  13.4 3.4 %collective-permute-start.3 = (f32[8,128]{1,0:T(8,128)S(1)}, f32[8,128]{1,0:T(8,128)S(1)}, u32[]{:S(2)}, u32[]{:S(2)}) collective-permute-start(f32[8,128]{1,0:T(8,128)S(1)} %get-tuple-element.90.refs_0_.refs_16_), channel_id=1, source_target_pairs={{0,2},{1,3},{2,0},{3,1},{4,6},{5,7},{6,4},{7,5},{8,10},{9,11},{10,... | collective-permute-start | bytes 12296 | tf_op jit(solution)/shard_map/ppermute | solution.py:525
  16.8 10.8 %copy-start = (bf16[8,512,128]{2,1,0:T(8,128)(2,1)S(1)}, bf16[8,512,128]{2,1,0:T(8,128)(2,1)}, u32[]{:S(2)}) copy-start(bf16[8,512,128]{2,1,0:T(8,128)(2,1)} %grad_ref.1) | copy-start | bytes 3145732
  16.8 13.8 %copy-start.1 = (bf16[27,128,128]{2,1,0:T(8,128)(2,1)S(1)}, bf16[27,128,128]{2,1,0:T(8,128)(2,1)}, u32[]{:S(2)}) copy-start(bf16[27,128,128]{2,1,0:T(8,128)(2,1)} %refs_5_.2) | copy-start | bytes 2654212
  24.0 6.6 %collective-permute-start.8 = (f32[8,128]{1,0:T(8,128)S(1)}, f32[8,128]{1,0:T(8,128)S(1)}, u32[]{:S(2)}, u32[]{:S(2)}) collective-permute-start(f32[8,128]{1,0:T(8,128)S(1)} %get-tuple-element.92.refs_0_.refs_16_.refs_8_), channel_id=1, source_target_pairs={{0,6},{1,7},{2,4},{3,5},{4,2},{5,3},{6,0},{7,1},{8,14},{9,15},{10,... | collective-permute-start | bytes 12296 | tf_op jit(solution)/shard_map/ppermute | solution.py:525
  25.5 5.1 %collective-permute-start.7 = (f32[8,128]{1,0:T(8,128)S(1)}, f32[8,128]{1,0:T(8,128)S(1)}, u32[]{:S(2)}, u32[]{:S(2)}) collective-permute-start(f32[8,128]{1,0:T(8,128)S(1)} %get-tuple-element.92.refs_0_.refs_16_.refs_8_), channel_id=1, source_target_pairs={{0,4},{1,5},{2,6},{3,7},{4,0},{5,1},{6,2},{7,3},{8,12},{9,13},{10,... | collective-permute-start | bytes 12296 | tf_op jit(solution)/shard_map/ppermute | solution.py:525
  25.6 5.0 %collective-permute-start.6 = (f32[8,128]{1,0:T(8,128)S(1)}, f32[8,128]{1,0:T(8,128)S(1)}, u32[]{:S(2)}, u32[]{:S(2)}) collective-permute-start(f32[8,128]{1,0:T(8,128)S(1)} %get-tuple-element.92.refs_0_.refs_16_.refs_8_), channel_id=1, source_target_pairs={{0,2},{1,3},{2,0},{3,1},{4,6},{5,7},{6,4},{7,5},{8,10},{9,11},{10,... | collective-permute-start | bytes 12296 | tf_op jit(solution)/shard_map/ppermute | solution.py:525
  28.2 13.4 %collective-permute-start.9 = (bf16[512,128]{1,0:T(8,128)(2,1)S(1)}, bf16[512,128]{1,0:T(8,128)(2,1)S(1)}, u32[]{:S(2)}, u32[]{:S(2)}) collective-permute-start(bf16[512,128]{1,0:T(8,128)(2,1)S(1)} %get-tuple-element.96), channel_id=1, source_target_pairs={{0,1},{1,0},{2,3},{3,2},{4,5},{5,4},{6,7},{7,6},{8,9},{9,8},{10,11... | collective-permute-start | bytes 393224 | tf_op jit(solution)/shard_map/ppermute | solution.py:525
  38.0 4.3 %collective-permute-start.12 = (f32[8,128]{1,0:T(8,128)S(1)}, f32[8,128]{1,0:T(8,128)S(1)}, u32[]{:S(2)}, u32[]{:S(2)}) collective-permute-start(f32[8,128]{1,0:T(8,128)S(1)} %get-tuple-element.97.refs_0_.refs_8_), channel_id=1, source_target_pairs={{0,6},{1,7},{2,4},{3,5},{4,2},{5,3},{6,0},{7,1},{8,14},{9,15},{10,... | collective-permute-start | bytes 12296 | tf_op jit(solution)/shard_map/ppermute | solution.py:525
  39.2 3.4 %collective-permute-start.11 = (f32[8,128]{1,0:T(8,128)S(1)}, f32[8,128]{1,0:T(8,128)S(1)}, u32[]{:S(2)}, u32[]{:S(2)}) collective-permute-start(f32[8,128]{1,0:T(8,128)S(1)} %get-tuple-element.97.refs_0_.refs_8_), channel_id=1, source_target_pairs={{0,4},{1,5},{2,6},{3,7},{4,0},{5,1},{6,2},{7,3},{8,12},{9,13},{10,... | collective-permute-start | bytes 12296 | tf_op jit(solution)/shard_map/ppermute | solution.py:525
  39.2 3.4 %collective-permute-start.10 = (f32[8,128]{1,0:T(8,128)S(1)}, f32[8,128]{1,0:T(8,128)S(1)}, u32[]{:S(2)}, u32[]{:S(2)}) collective-permute-start(f32[8,128]{1,0:T(8,128)S(1)} %get-tuple-element.97.refs_0_.refs_8_), channel_id=1, source_target_pairs={{0,2},{1,3},{2,0},{3,1},{4,6},{5,7},{6,4},{7,5},{8,10},{9,11},{10,... | collective-permute-start | bytes 12296 | tf_op jit(solution)/shard_map/ppermute | solution.py:525
  43.8 7.9 %collective-permute-start.15 = (f32[8,128]{1,0:T(8,128)S(1)}, f32[8,128]{1,0:T(8,128)S(1)}, u32[]{:S(2)}, u32[]{:S(2)}) collective-permute-start(f32[8,128]{1,0:T(8,128)S(1)} %get-tuple-element.100.refs_12_), channel_id=1, source_target_pairs={{0,6},{1,7},{2,4},{3,5},{4,2},{5,3},{6,0},{7,1},{8,14},{9,15},{10,... | collective-permute-start | bytes 12296 | tf_op jit(solution)/shard_map/ppermute | solution.py:525
  45.9 5.8 %collective-permute-start.14 = (f32[8,128]{1,0:T(8,128)S(1)}, f32[8,128]{1,0:T(8,128)S(1)}, u32[]{:S(2)}, u32[]{:S(2)}) collective-permute-start(f32[8,128]{1,0:T(8,128)S(1)} %get-tuple-element.100.refs_12_), channel_id=1, source_target_pairs={{0,4},{1,5},{2,6},{3,7},{4,0},{5,1},{6,2},{7,3},{8,12},{9,13},{10,... | collective-permute-start | bytes 12296 | tf_op jit(solution)/shard_map/ppermute | solution.py:525
  46.5 5.3 %collective-permute-start.13 = (f32[8,128]{1,0:T(8,128)S(1)}, f32[8,128]{1,0:T(8,128)S(1)}, u32[]{:S(2)}, u32[]{:S(2)}) collective-permute-start(f32[8,128]{1,0:T(8,128)S(1)} %get-tuple-element.100.refs_12_), channel_id=1, source_target_pairs={{0,2},{1,3},{2,0},{3,1},{4,6},{5,7},{6,4},{7,5},{8,10},{9,11},{10,... | collective-permute-start | bytes 12296 | tf_op jit(solution)/shard_map/ppermute | solution.py:525
  47.4 18.6 %collective-permute-start.17 = (bf16[512,128]{1,0:T(8,128)(2,1)S(1)}, bf16[512,128]{1,0:T(8,128)(2,1)S(1)}, u32[]{:S(2)}, u32[]{:S(2)}) collective-permute-start(bf16[512,128]{1,0:T(8,128)(2,1)S(1)} %get-tuple-element.103), channel_id=1, source_target_pairs={{0,1},{1,0},{2,3},{3,2},{4,5},{5,4},{6,7},{7,6},{8,9},{9,8},{10,11... | collective-permute-start | bytes 393224 | tf_op jit(solution)/shard_map/ppermute | solution.py:525
  60.0 6.0 %collective-permute-start.20 = (f32[8,128]{1,0:T(8,128)S(1)}, f32[8,128]{1,0:T(8,128)S(1)}, u32[]{:S(2)}, u32[]{:S(2)}) collective-permute-start(f32[8,128]{1,0:T(8,128)S(1)} %get-tuple-element.106.refs_12_.refs_8_), channel_id=1, source_target_pairs={{0,6},{1,7},{2,4},{3,5},{4,2},{5,3},{6,0},{7,1},{8,14},{9,15},{10,... | collective-permute-start | bytes 12296 | tf_op jit(solution)/shard_map/ppermute | solution.py:525
  61.2 4.8 %collective-permute-start.19 = (f32[8,128]{1,0:T(8,128)S(1)}, f32[8,128]{1,0:T(8,128)S(1)}, u32[]{:S(2)}, u32[]{:S(2)}) collective-permute-start(f32[8,128]{1,0:T(8,128)S(1)} %get-tuple-element.106.refs_12_.refs_8_), channel_id=1, source_target_pairs={{0,4},{1,5},{2,6},{3,7},{4,0},{5,1},{6,2},{7,3},{8,12},{9,13},{10,... | collective-permute-start | bytes 12296 | tf_op jit(solution)/shard_map/ppermute | solution.py:525
  61.2 4.8 %collective-permute-start.18 = (f32[8,128]{1,0:T(8,128)S(1)}, f32[8,128]{1,0:T(8,128)S(1)}, u32[]{:S(2)}, u32[]{:S(2)}) collective-permute-start(f32[8,128]{1,0:T(8,128)S(1)} %get-tuple-element.106.refs_12_.refs_8_), channel_id=1, source_target_pairs={{0,2},{1,3},{2,0},{3,1},{4,6},{5,7},{6,4},{7,5},{8,10},{9,11},{10,... | collective-permute-start | bytes 12296 | tf_op jit(solution)/shard_map/ppermute | solution.py:525
  63.6 13.7 %collective-permute-start.16 = (bf16[1792,128]{1,0:T(8,128)(2,1)S(1)}, bf16[1792,128]{1,0:T(8,128)(2,1)S(1)}, u32[]{:S(2)}, u32[]{:S(2)}) collective-permute-start(bf16[1792,128]{1,0:T(8,128)(2,1)S(1)} %get-tuple-element.102), channel_id=1, source_target_pairs={{0,1},{1,0},{2,3},{3,2},{4,5},{5,4},{6,7},{7,6},{8,9},{9,8},{10,11... | collective-permute-start | bytes 1376264 | tf_op jit(solution)/shard_map/ppermute | solution.py:525
  74.5 4.2 %collective-permute-start.21 = (bf16[1792,128]{1,0:T(8,128)(2,1)S(1)}, bf16[1792,128]{1,0:T(8,128)(2,1)S(1)}, u32[]{:S(2)}, u32[]{:S(2)}) collective-permute-start(bf16[1792,128]{1,0:T(8,128)(2,1)S(1)} %get-tuple-element.108), channel_id=1, source_target_pairs={{0,1},{1,0},{2,3},{3,2},{4,5},{5,4},{6,7},{7,6},{8,9},{9,8},{10,11... | collective-permute-start | bytes 1376264 | tf_op jit(solution)/shard_map/ppermute | solution.py:525
  79.5 15.0 %collective-permute-start.22 = (bf16[896,128]{1,0:T(8,128)(2,1)S(1)}, bf16[896,128]{1,0:T(8,128)(2,1)S(1)}, u32[]{:S(2)}, u32[]{:S(2)}) collective-permute-start(bf16[896,128]{1,0:T(8,128)(2,1)S(1)} %get-tuple-element.110), channel_id=1, source_target_pairs={{0,8},{8,0},{16,24},{24,16},{1,9},{9,1},{17,25},{25,17},{2,10},{10... | collective-permute-start | bytes 688136 | tf_op jit(solution)/shard_map/ppermute | solution.py:525
  80.8 13.8 %collective-permute-start.23 = (bf16[896,128]{1,0:T(8,128)(2,1)S(1)}, bf16[896,128]{1,0:T(8,128)(2,1)S(1)}, u32[]{:S(2)}, u32[]{:S(2)}) collective-permute-start(bf16[896,128]{1,0:T(8,128)(2,1)S(1)} %get-tuple-element.111), channel_id=1, source_target_pairs={{0,16},{8,24},{16,0},{24,8},{1,17},{9,25},{17,1},{25,9},{2,18},{10... | collective-permute-start | bytes 688136 | tf_op jit(solution)/shard_map/ppermute | solution.py:525
  82.0 12.5 %collective-permute-start.24 = (bf16[896,128]{1,0:T(8,128)(2,1)S(1)}, bf16[896,128]{1,0:T(8,128)(2,1)S(1)}, u32[]{:S(2)}, u32[]{:S(2)}) collective-permute-start(bf16[896,128]{1,0:T(8,128)(2,1)S(1)} %get-tuple-element.112), channel_id=1, source_target_pairs={{0,24},{8,16},{16,8},{24,0},{1,25},{9,17},{17,9},{25,1},{2,26},{10... | collective-permute-start | bytes 688136 | tf_op jit(solution)/shard_map/ppermute | solution.py:525
  82.2 4.3 %collective-permute-start.27 = (f32[8,128]{1,0:T(8,128)S(1)}, f32[8,128]{1,0:T(8,128)S(1)}, u32[]{:S(2)}, u32[]{:S(2)}) collective-permute-start(f32[8,128]{1,0:T(8,128)S(1)} %get-tuple-element.115.refs_4_), channel_id=1, source_target_pairs={{0,6},{1,7},{2,4},{3,5},{4,2},{5,3},{6,0},{7,1},{8,14},{9,15},{10,... | collective-permute-start | bytes 12296 | tf_op jit(solution)/shard_map/ppermute | solution.py:525
  83.3 3.4 %collective-permute-start.26 = (f32[8,128]{1,0:T(8,128)S(1)}, f32[8,128]{1,0:T(8,128)S(1)}, u32[]{:S(2)}, u32[]{:S(2)}) collective-permute-start(f32[8,128]{1,0:T(8,128)S(1)} %get-tuple-element.115.refs_4_), channel_id=1, source_target_pairs={{0,4},{1,5},{2,6},{3,7},{4,0},{5,1},{6,2},{7,3},{8,12},{9,13},{10,... | collective-permute-start | bytes 12296 | tf_op jit(solution)/shard_map/ppermute | solution.py:525
  86.5 2.8 %collective-permute-start.25 = (f32[8,128]{1,0:T(8,128)S(1)}, f32[8,128]{1,0:T(8,128)S(1)}, u32[]{:S(2)}, u32[]{:S(2)}) collective-permute-start(f32[8,128]{1,0:T(8,128)S(1)} %get-tuple-element.115.refs_4_), channel_id=1, source_target_pairs={{0,2},{1,3},{2,0},{3,1},{4,6},{5,7},{6,4},{7,5},{8,10},{9,11},{10,... | collective-permute-start | bytes 12296 | tf_op jit(solution)/shard_map/ppermute | solution.py:525
  90.3 4.2 %collective-permute-start.28 = (bf16[256,128]{1,0:T(8,128)(2,1)S(1)}, bf16[256,128]{1,0:T(8,128)(2,1)S(1)}, u32[]{:S(2)}, u32[]{:S(2)}) collective-permute-start(bf16[256,128]{1,0:T(8,128)(2,1)S(1)} %get-tuple-element.117), channel_id=1, source_target_pairs={{0,1},{1,0},{2,3},{3,2},{4,5},{5,4},{6,7},{7,6},{8,9},{9,8},{10,11... | collective-permute-start | bytes 196616 | tf_op jit(solution)/shard_map/ppermute | solution.py:525
  95.2 3.6 %collective-permute-start.29 = (bf16[288,128]{1,0:T(8,128)(2,1)S(1)}, bf16[288,128]{1,0:T(8,128)(2,1)S(1)}, u32[]{:S(2)}, u32[]{:S(2)}) collective-permute-start(bf16[288,128]{1,0:T(8,128)(2,1)S(1)} %get-tuple-element.119), channel_id=1, source_target_pairs={{0,2},{1,3},{2,0},{3,1},{4,6},{5,7},{6,4},{7,5},{8,10},{9,11},{10,... | collective-permute-start | bytes 221192 | tf_op jit(solution)/shard_map/ppermute | solution.py:525
  95.3 4.3 %collective-permute-start.30 = (bf16[288,128]{1,0:T(8,128)(2,1)S(1)}, bf16[288,128]{1,0:T(8,128)(2,1)S(1)}, u32[]{:S(2)}, u32[]{:S(2)}) collective-permute-start(bf16[288,128]{1,0:T(8,128)(2,1)S(1)} %get-tuple-element.120), channel_id=1, source_target_pairs={{0,4},{1,5},{2,6},{3,7},{4,0},{5,1},{6,2},{7,3},{8,12},{9,13},{10,... | collective-permute-start | bytes 221192 | tf_op jit(solution)/shard_map/ppermute | solution.py:525
  96.7 6.1 %collective-permute-start.31 = (bf16[288,128]{1,0:T(8,128)(2,1)S(1)}, bf16[288,128]{1,0:T(8,128)(2,1)S(1)}, u32[]{:S(2)}, u32[]{:S(2)}) collective-permute-start(bf16[288,128]{1,0:T(8,128)(2,1)S(1)} %get-tuple-element.121), channel_id=1, source_target_pairs={{0,6},{1,7},{2,4},{3,5},{4,2},{5,3},{6,0},{7,1},{8,14},{9,15},{10,... | collective-permute-start | bytes 221192 | tf_op jit(solution)/shard_map/ppermute | solution.py:525
  103.4 7.4 %collective-permute-start.34 = (bf16[288,128]{1,0:T(8,128)(2,1)S(1)}, bf16[288,128]{1,0:T(8,128)(2,1)S(1)}, u32[]{:S(2)}, u32[]{:S(2)}) collective-permute-start(bf16[288,128]{1,0:T(8,128)(2,1)S(1)} %shard_map.157.refs_0_), channel_id=1, source_target_pairs={{0,6},{1,7},{2,4},{3,5},{4,2},{5,3},{6,0},{7,1},{8,14},{9,15},{10,... | collective-permute-start | bytes 221192 | tf_op jit(solution)/shard_map/ppermute | solution.py:525
  104.5 8.8 %collective-permute-start.33 = (bf16[288,128]{1,0:T(8,128)(2,1)S(1)}, bf16[288,128]{1,0:T(8,128)(2,1)S(1)}, u32[]{:S(2)}, u32[]{:S(2)}) collective-permute-start(bf16[288,128]{1,0:T(8,128)(2,1)S(1)} %shard_map.157.refs_0_), channel_id=1, source_target_pairs={{0,4},{1,5},{2,6},{3,7},{4,0},{5,1},{6,2},{7,3},{8,12},{9,13},{10,... | collective-permute-start | bytes 221192 | tf_op jit(solution)/shard_map/ppermute | solution.py:525
  106.3 6.9 %collective-permute-start.32 = (bf16[288,128]{1,0:T(8,128)(2,1)S(1)}, bf16[288,128]{1,0:T(8,128)(2,1)S(1)}, u32[]{:S(2)}, u32[]{:S(2)}) collective-permute-start(bf16[288,128]{1,0:T(8,128)(2,1)S(1)} %shard_map.157.refs_0_), channel_id=1, source_target_pairs={{0,2},{1,3},{2,0},{3,1},{4,6},{5,7},{6,4},{7,5},{8,10},{9,11},{10,... | collective-permute-start | bytes 221192 | tf_op jit(solution)/shard_map/ppermute | solution.py:525
  107.0 3.8 %collective-permute-start.35 = (f32[8,128]{1,0:T(8,128)S(1)}, f32[8,128]{1,0:T(8,128)S(1)}, u32[]{:S(2)}, u32[]{:S(2)}) collective-permute-start(f32[8,128]{1,0:T(8,128)S(1)} %get-tuple-element.122.refs_4_), channel_id=1, source_target_pairs={{0,1},{1,0},{2,3},{3,2},{4,5},{5,4},{6,7},{7,6},{8,9},{9,8},{10,11... | collective-permute-start | bytes 12296 | tf_op jit(solution)/shard_map/ppermute | solution.py:525
  113.8 10.4 %collective-permute-start.38 = (bf16[1168,128]{1,0:T(8,128)(2,1)S(1)}, bf16[1168,128]{1,0:T(8,128)(2,1)S(1)}, u32[]{:S(2)}, u32[]{:S(2)}) collective-permute-start(bf16[1168,128]{1,0:T(8,128)(2,1)S(1)} %shard_map.158.refs_0_), channel_id=1, source_target_pairs={{0,24},{8,16},{16,8},{24,0},{1,25},{9,17},{17,9},{25,1},{2,26},{10... | collective-permute-start | bytes 897032 | tf_op jit(solution)/shard_map/ppermute | solution.py:525
  115.2 15.0 %collective-permute-start.37 = (bf16[1168,128]{1,0:T(8,128)(2,1)S(1)}, bf16[1168,128]{1,0:T(8,128)(2,1)S(1)}, u32[]{:S(2)}, u32[]{:S(2)}) collective-permute-start(bf16[1168,128]{1,0:T(8,128)(2,1)S(1)} %shard_map.158.refs_0_), channel_id=1, source_target_pairs={{0,16},{8,24},{16,0},{24,8},{1,17},{9,25},{17,1},{25,9},{2,18},{10... | collective-permute-start | bytes 897032 | tf_op jit(solution)/shard_map/ppermute | solution.py:525
  116.1 14.1 %collective-permute-start.36 = (bf16[1168,128]{1,0:T(8,128)(2,1)S(1)}, bf16[1168,128]{1,0:T(8,128)(2,1)S(1)}, u32[]{:S(2)}, u32[]{:S(2)}) collective-permute-start(bf16[1168,128]{1,0:T(8,128)(2,1)S(1)} %shard_map.158.refs_0_), channel_id=1, source_target_pairs={{0,8},{8,0},{16,24},{24,16},{1,9},{9,1},{17,25},{25,17},{2,10},{10... | collective-permute-start | bytes 897032 | tf_op jit(solution)/shard_map/ppermute | solution.py:525
  119.7 3.1 %collective-permute-start.39 = (bf16[64,2048]{1,0:T(8,128)(2,1)S(1)}, bf16[64,2048]{1,0:T(8,128)(2,1)S(1)}, u32[]{:S(2)}, u32[]{:S(2)}) collective-permute-start(bf16[64,2048]{1,0:T(8,128)(2,1)S(1)} %get-tuple-element.131), channel_id=1, source_target_pairs={{0,1},{1,0},{2,3},{3,2},{4,5},{5,4},{6,7},{7,6},{8,9},{9,8},{10,11... | collective-permute-start | bytes 786440 | tf_op jit(solution)/shard_map/ppermute | solution.py:525
  131.4 2.8 %collective-permute-start.40 = (bf16[3840,128]{1,0:T(8,128)(2,1)S(1)}, bf16[3840,128]{1,0:T(8,128)(2,1)S(1)}, u32[]{:S(2)}, u32[]{:S(2)}) collective-permute-start(bf16[3840,128]{1,0:T(8,128)(2,1)S(1)} %get-tuple-element.140.half_ref), channel_id=1, source_target_pairs={{0,1},{1,0},{2,3},{3,2},{4,5},{5,4},{6,7},{7,6},{8,9},{9,8},{10,11... | collective-permute-start | bytes 2949128 | tf_op jit(solution)/shard_map/ppermute | solution.py:525
where the time goes:
time: 137 us; the launch traced here: 136 us
  starting transfers between devices  55.4 us (40%)
  Pallas kernels  53.9 us (39%)
  waiting for transfers between devices  25.7 us (19%)
    ppermute x41, starting transfers between devices, swapped(): return lax.ppermute(value, axis, [(i, i ^ step) for i in range(count)])  55.4 us
    pallas_call x20, Pallas kernels, run(): pl.pallas_call(kernel, in_specs=[pl.BlockSpec(memory_space=pltpu.SMEM)] +...  53.9 us
    ppermute x41, waiting for transfers between devices, swapped(): return lax.ppermute(value, axis, [(i, i ^ step) for i in range(count)])  25.7 us
  transfers between devices with their start and end apart: 41, of which 16 were waited for; matrix products, arithmetic and copies ran while one was open for 0% of the time, Pallas kernels for 28%

commit v1 on v0

--- a/solution.py
+++ b/solution.py
@@ -440,83 +440,81 @@
     pieces, norm_refs, out_ref = refs[:-3], refs[-3:-1], refs[-1]
     size = pieces[0].shape[0] - small
     base = len(pieces) * size
-    for j, ref in enumerate(pieces):
+    for j, ref in zip(partners(len(pieces)), pieces):
         place = where_ref[3] ^ j
         out_ref[pl.ds(pl.multiple_of(place * size, 16), size)] = ref[:size]
         out_ref[pl.ds(pl.multiple_of(base + place * small, 16), small)] = ref[size:]
     out_ref[base + len(pieces) * small :] = high_and_low(sum_refs(norm_refs))
 
 
-def gather_kernel(size, where_ref, *refs):
-    pieces, (out_ref, scale_ref, shift_ref) = refs[:-3], refs[-3:]
-    for j, ref in enumerate(pieces):
-        out_ref[pl.ds(pl.multiple_of((where_ref[2] ^ j) * size, 16), size)] = ref[:size]
-    tails = [ref[size:].astype(F32) for ref in pieces]
-    middle = tails[0].shape[0] - 16
-    out_ref[len(pieces) * size :] = tree_sum([tail[:middle] for tail in tails]).astype(BF16)
-    sums = tree_sum([one_value(tail[middle:]) for tail in tails])
-    shift_ref[...] = jnp.concatenate([sums[2 * t : 2 * t + 1] for t in range(3)], axis=0)
-    scale_ref[...] = jnp.concatenate([sums[2 * t + 1 : 2 * t + 2] for t in range(3)], axis=0)
-
-
-def final_kernel(parts, blocks, flip, where_ref, half_ref, *refs):
-    count = len(parts) + 1
-    outs, scratches, leaving = refs[-2 * count - 1 : -count - 1], refs[-count - 1 : -1], refs[-1]
-    core = where_ref[1]
-    place = 1 - core if flip else core
+def settle_blocks(items, parts, depths, sections, where_ref, pieces, outs, staging, leaving):
     total = sum(parts)
-    base = 0
-    copies, extras = [], []
-    for i in range(count):
-        scratch, out = scratches[i], outs[i]
-        half = scratch.shape[0]
-        if i < len(parts):
-            size = parts[i]
-            for t in range(blocks):
-                scratch[t * size : (t + 1) * size] = half_ref[t * total + base : t * total + base + size].astype(F32)
+    copies = []
+    for n, ((flip, j), piece) in enumerate(zip(items, pieces)):
+        core = 1 - where_ref[1] if flip else where_ref[1]
+        base = 0
+        for i, size in enumerate(parts):
+            wide = depths * size
+            block = core * sections + (where_ref[2] ^ j)
+            slot = staging.at[n, i]
+            for z in range(depths):
+                slot[z * size : (z + 1) * size] = piece[z * total + base : z * total + base + size].astype(F32)
             base += size
-        else:
-            scratch[...] = half_ref[blocks * total :].astype(F32)
-        sure = out.shape[0] - half
-        copy = pltpu.make_async_copy(
-            scratch.at[pl.ds(0, sure)],
-            out.at[pl.ds(pl.multiple_of(place * half, 16), sure)],
-            leaving.at[i, 0],
-        )
-        copy.start()
-        copies.append(copy)
-        if sure < half:
-            extras.append(
-                pltpu.make_async_copy(
-                    scratch.at[pl.ds(sure, half - sure)], out.at[pl.ds(sure, half - sure)], leaving.at[i, 1]
+            last, rest = divmod(outs[i].shape[0], wide)
+            start = pl.multiple_of(block * wide, 16)
+            copies.append((block < last, pltpu.make_async_copy(slot, outs[i].at[pl.ds(start, wide)], leaving.at[n, i])))
+            if rest:
+                part_copy = pltpu.make_async_copy(
+                    slot.at[pl.ds(0, rest)], outs[i].at[pl.ds(last * wide, rest)], leaving.at[n, i]
                 )
-            )
-
-    @pl.when(place == 0)
-    def _():
-        for copy in extras:
-            copy.start()
-        for copy in extras:
-            copy.wait()
-
-    for copy in copies:
-        copy.wait()
-
-
-def run(kernel, where, operands, outs, scratch=(), hbm_in=(), hbm_out=False, aliases=None, flops=0, grid=None):
-    def place(i):
-        return pltpu.HBM if i in hbm_in else pltpu.VMEM
+                copies.append((block == last, part_copy))
+    for when, copy in copies:
+        pl.when(when)(copy.start)
+    return copies
+
+
+def finish(copies):
+    for when, copy in copies:
+        pl.when(when)(copy.wait)
+
+
+def settle_rest_kernel(items, parts, depths, small, with_norms, where_ref, *refs):
+    sections = len(items)
+    pieces = refs[:sections]
+    staging, down_staging, leaving, down_leaving = refs[-4:]
+    outs = refs[-9:-4] if with_norms else refs[-7:-4]
+    first, second, down = outs[:3]
+    copies = settle_blocks(items, parts, depths, sections, where_ref, pieces, (first, second), staging, leaving)
+    base = depths * sum(parts)
+    wide = depths * small
+    core = where_ref[1] if with_norms else 1 - where_ref[1]
+    down_staging[...] = tree_sum([piece[base : base + wide].astype(F32) for piece in pieces])
+    down_copy = pltpu.make_async_copy(
+        down_staging, down.at[pl.ds(pl.multiple_of(core * wide, 16), wide)], down_leaving.at[0]
+    )
+    down_copy.start()
+    if with_norms:
+        sums = tree_sum([one_value(piece[base + wide :]) for piece in pieces])
+        outs[4][...] = jnp.concatenate([sums[2 * t : 2 * t + 1] for t in range(3)], axis=0)
+        outs[3][...] = jnp.concatenate([sums[2 * t + 1 : 2 * t + 2] for t in range(3)], axis=0)
+    finish(copies)
+    down_copy.wait()
+
+
+def run(kernel, where, operands, outs, scratch=(), hbm_in=(), hbm_out=(), aliases=None, flops=0):
+    def place(i, hbm):
+        return pltpu.HBM if i in hbm else pltpu.VMEM
 
     return pl.pallas_call(
         kernel,
         in_specs=[pl.BlockSpec(memory_space=pltpu.SMEM)]
-        + [pl.BlockSpec(memory_space=place(i)) for i in range(len(operands))],
-        out_specs=[pl.BlockSpec(memory_space=pltpu.HBM if hbm_out else pltpu.VMEM)] * len(outs),
+        + [pl.BlockSpec(memory_space=place(i, hbm_in)) for i in range(len(operands))],
+        out_specs=[pl.BlockSpec(memory_space=place(i, hbm_out)) for i in range(len(outs))],
         out_shape=outs,
         scratch_shapes=list(scratch),
         input_output_aliases=aliases or {},
         compiler_params=pltpu.CompilerParams(vmem_limit_bytes=VMEM_BYTES),
-        cost_estimate=pl.CostEstimate(flops=flops, bytes_accessed=1 << 20, transcendentals=0),
+        cost_estimate=pl.CostEstimate(flops=flops, bytes_accessed=(1 << 20) if flops else 1, transcendentals=0),
     )(where, *operands)
 
 
@@ -525,8 +523,26 @@
     return lax.ppermute(value, axis, [(i, i ^ step) for i in range(count)])
 
 
+def partners(count):
+    order = [0]
+    step = 1
+    while len(order) < count:
+        order = order + [j ^ (count - step) for j in order]
+        step *= 2
+    return order
+
+
+def from_depths(values):
+    return [values[j] if j == 0 else swapped(values[j], "dp", 2 * j) for j in partners(len(values))]
+
+
+def from_sections(values):
+    return [values[j] if j == 0 else swapped(values[j], "section", j) for j in partners(len(values))]
+
+
 def depth_sums(value):
-    return [value] + [swapped(value, "dp", step) for step in range(2, lax.axis_size("dp"), 2)]
+    steps = range(2, lax.axis_size("dp"), 2)
+    return [value] + [swapped(value, "dp", step) for step in steps]
 
 
 def local(
@@ -663,7 +679,7 @@
         [keep_second, got_second, keep_first, got_first],
         [half_shape(depths * total)] * sections,
     )
-    arrived = [section_out[0]] + [swapped(section_out[j], "section", j) for j in range(1, sections)]
+    arrived = from_sections(section_out)
     back_zero = depth_sums(back_part)
     rows_zero, keep_down, send_down, norm_rows = run(
         functools.partial(last_kernel, ways), where,
@@ -677,45 +693,55 @@
         functools.partial(spread_kernel, depths, sections), where, arrived + [keep_down, got_down],
         [half_shape(total + small)] * depths,
     )
-    arrived = [depth_out[0]] + [swapped(depth_out[j], "dp", 2 * j) for j in range(1, depths)]
+    arrived = from_depths(depth_out)
     (summed,) = run(add_kernel, where, arrived, [half_shape(total + small)])
-    arrived = [summed] + [swapped(summed, "dp", 2 * j) for j in range(1, depths)]
+    arrived = from_depths([summed] * depths)
     (joined,) = run(
         functools.partial(join_kernel, small), where, arrived + [norm_rows, cores(norm_rows)],
         [half_shape(depths * (total + small) + 16)],
     )
     joined, rows_zero = lax.optimization_barrier((joined, rows_zero))
-    arrived = [joined] + [swapped(joined, "section", j) for j in range(1, sections)]
+    arrived = from_sections([joined] * sections)
+    across = cores(joined)
     input_own, input_send = run(
         input_kernel, where, [rows_zero, which, tables, weight_down], [feats_one, feats_one],
-        flops=4 * 10**9,
     )
     features, input_grad = run(
         place_outputs_kernel, where,
         [features_own, features_other, input_own, cores(input_send)],
         [rows_bf16, shape((mine, in_channels, fine_rows), BF16)],
         [pltpu.SemaphoreType.DMA((4,))],
-        hbm_out=True,
-    )
+        hbm_out=(0, 1),
+    )
+    block = (2, depths * parts[0], channels)
+    convs = [shape((conv_rows, channels), F32)] * 2
+    down_shape = shape((wide, channels), F32)
+    norms = shape(bn_scale.shape, F32)
+
+    def staging(count):
+        return [pltpu.VMEM((count,) + block, F32)]
+
+    def rest_scratch():
+        return staging(sections) + [
+            pltpu.VMEM((depths * small, channels), F32),
+            pltpu.SemaphoreType.DMA((sections, 2)),
+            pltpu.SemaphoreType.DMA((1,)),
+        ]
+
     arrived, features, input_grad = lax.optimization_barrier((arrived, features, input_grad))
-    norms = shape(bn_scale.shape, F32)
-    gathered, grad_scale, grad_shift = run(
-        functools.partial(gather_kernel, depths * total), where, arrived,
-        [half_shape(blocks * total + depths * small), norms, norms],
-    )
-    other = cores(gathered)
-    grads = [shape((conv_rows, channels), F32)] * 2 + [shape((wide, channels), F32)]
-    staging = [pltpu.VMEM((half.shape[0], channels), F32)] * 2 + [
-        pltpu.VMEM((small_half.shape[0], channels), F32),
-        pltpu.SemaphoreType.DMA((3, 2)),
-    ]
-    grads_out = run(
-        functools.partial(final_kernel, parts, blocks, False), where, [gathered], grads, staging,
-        hbm_out=True, flops=10**9,
-    )
+    others = [across] + [cores(piece) for piece in arrived[1:]]
+    items = [(False, j) for j in partners(sections)]
+    grad_second, grad_first, grad_down, grad_scale, grad_shift = run(
+        functools.partial(settle_rest_kernel, items, parts, depths, small, True), where,
+        arrived, convs + [down_shape, norms, norms], rest_scratch(),
+        hbm_out=(0, 1, 2), flops=10**9,
+    )
+    items = [(True, j) for j in partners(sections)]
     grad_second, grad_first, grad_down = run(
-        functools.partial(final_kernel, parts, blocks, True), where, [other] + list(grads_out), grads, staging,
-        hbm_in=(1, 2, 3), hbm_out=True, aliases={2: 0, 3: 1, 4: 2}, flops=10**9,
+        functools.partial(settle_rest_kernel, items, parts, depths, small, False), where,
+        others + [grad_second, grad_first, grad_down], convs + [down_shape], rest_scratch(),
+        hbm_in=(sections, sections + 1, sections + 2), hbm_out=(0, 1, 2),
+        aliases={1 + sections: 0, 2 + sections: 1, 3 + sections: 2}, flops=10**9,
     )
     return (
         features,

time: 137 us -> 135 us (0.985)
  waiting for transfers between devices: 25.7 us -> 21.6 us
  starting transfers between devices: 55.4 us -> 58.9 us
    ppermute x41 -> x44, waiting for transfers between devices: 25.7 us -> 21.6 us  [swapped(): return lax.ppermute(value, axis, [(i, i ^ step) for i in range(count)])]
    ppermute x41 -> x44, starting transfers between devices: 55.4 us -> 58.9 us  [swapped(): return lax.ppermute(value, axis, [(i, i ^ step) for i in range(count)])]
    pallas_call x20 -> x19, Pallas kernels: 53.9 us -> 53.5 us  [run(): pl.pallas_call(kernel, in_specs=[pl.BlockSpec(memory_space=pltpu.SMEM)] +...]
  transfers between devices with their start and end apart: 41 -> 44, of which waited for: 16 -> 15; matrix products, arithmetic and copies ran while one was open for 0% -> 0% of each run, Pallas kernels for 28% -> 29%
where the time goes in v1:
time: 135 us
  starting transfers between devices  58.9 us (44%)
  Pallas kernels  53.5 us (40%)
  waiting for transfers between devices  21.6 us (16%)
    ppermute x44, starting transfers between devices, swapped(): return lax.ppermute(value, axis, [(i, i ^ step) for i in range(count)])  58.9 us
    pallas_call x19, Pallas kernels, run(): pl.pallas_call(kernel, in_specs=[pl.BlockSpec(memory_space=pltpu.SMEM)] +...  53.5 us
    ppermute x44, waiting for transfers between devices, swapped(): return lax.ppermute(value, axis, [(i, i ^ step) for i in range(count)])  21.6 us
  transfers between devices with their start and end apart: 44, of which 15 were waited for; matrix products, arithmetic and copies ran while one was open for 0% of the time, Pallas kernels for 29%

profile of v1, /device:TPU:1, one launch (start us, length us, event | category | flops | bytes accessed | tf_op | source)
XLA Modules:
  0.0 135.2 jit_solution(7588790088662396331)
XLA Ops:
  0.7 1.7 %shard_map.144 = (bf16[64,2048]{1,0:T(8,128)(2,1)S(1)}, s32[8,512]{1,0:T(8,128)S(1)}, bf16[64,2048]{1,0:T(8,128)(2,1)S(1)}, s32[8,512]{1,0:T(8,128)S(1)}, bf16[512,128]{1,0:T(8,128)(2,1)S(1)}) custom-call(s32[5]{0:T(128)S(1)} %stack.23.where_ref, bf16[8,64,2048]{2,1,0:T(8,128)(2,1)} %bitcast.13, s32[8,8,512]{2,1,0:T(8,128)} %down_hbm.1, ...), custom_call_target="tpu_custom_call" | custom-call | bytes 1 | tf_op jit(solution)/shard_map/pallas_call | solution.py:508
  3.0 2.7 %shard_map.145 = (f32[512,128]{1,0:T(8,128)S(1)}, f32[8,128]{1,0:T(8,128)S(1)}, bf16[512,512]{1,0:T(8,128)(2,1)S(1)}, f32[8,2048]{1,0:T(8,128)S(1)}, s32[27,512]{1,0:T(8,128)S(1)}, /*index=5*/s32[27,512]{1,0:T(8,128)S(1)}) custom-call(s32[5]{0:T(128)S(1)} %stack.23.where_ref, bf16[64,2048]{1,0:T(8,128)(2,1)S(1)} %get-tuple-element.80.feats_ref, ...), custom_call_target="tpu_custom_call" | custom-call | flops 2000000000 | bytes 1048576 | tf_op jit(solution)/shard_map/pallas_call | solution.py:508
  5.9 2.7 %shard_map.146 = (f32[2,512,128]{2,1,0:T(8,128)S(1)}, f32[8,128]{1,0:T(8,128)S(1)}, bf16[2,512,512]{2,1,0:T(8,128)(2,1)S(1)}, f32[2,8,2048]{2,1,0:T(8,128)S(1)}, s32[2,8,512]{2,1,0:T(8,128)S(1)}) custom-call(s32[5]{0:T(128)S(1)} %stack.23.where_ref, bf16[64,2048]{1,0:T(8,128)(2,1)S(1)} %collective-permute-done.feats_ref, ...), custom_call_target="tpu_custom_call" | custom-call | flops 2000000000 | bytes 1048576 | tf_op jit(solution)/shard_map/pallas_call | solution.py:508
  8.6 4.8 %collective-permute-start.5 = (f32[8,128]{1,0:T(8,128)S(1)}, f32[8,128]{1,0:T(8,128)S(1)}, u32[]{:S(2)}, u32[]{:S(2)}) collective-permute-start(f32[8,128]{1,0:T(8,128)S(1)} %get-tuple-element.89.refs_0_.refs_16_), channel_id=1, source_target_pairs={{0,6},{1,7},{2,4},{3,5},{4,2},{5,3},{6,0},{7,1},{8,14},{9,15},{10,... | collective-permute-start | bytes 12296 | tf_op jit(solution)/shard_map/ppermute | solution.py:523
  14.4 2.4 %collective-permute-done.4.refs_2_.refs_18_ = f32[8,128]{1,0:T(8,128)S(1)} collective-permute-done((f32[8,128]{1,0:T(8,128)S(1)}, f32[8,128]{1,0:T(8,128)S(1)}, u32[]{:S(2)}, u32[]{:S(2)}) %collective-permute-start.4) | collective-permute-done | bytes 4128 | tf_op jit(solution)/shard_map/ppermute | solution.py:523
  16.8 7.2 %shard_map.148 = (bf16[2,512,128]{2,1,0:T(8,128)(2,1)S(1)}, f32[2,512,128]{2,1,0:T(8,128)S(1)}, f32[8,128]{1,0:T(8,128)S(1)}) custom-call(s32[5]{0:T(128)S(1)} %stack.23.where_ref, f32[2,512,128]{2,1,0:T(8,128)S(1)} %get-tuple-element.86.hidden_ref.refs_2_, s32[2,27,512]{2,1,0:T(8,128)S(1)} %shard_map.147.near_ref.refs_4_, ...), custom_call_target="tpu_custom_call" | custom-call | flops 14495514624 | bytes 1048576 | tf_op jit(solution)/shard_map/pallas_call | solution.py:508
  24.0 1.5 %collective-permute-start.8 = (f32[8,128]{1,0:T(8,128)S(1)}, f32[8,128]{1,0:T(8,128)S(1)}, u32[]{:S(2)}, u32[]{:S(2)}) collective-permute-start(f32[8,128]{1,0:T(8,128)S(1)} %get-tuple-element.91.refs_0_.refs_16_.refs_8_), channel_id=1, source_target_pairs={{0,6},{1,7},{2,4},{3,5},{4,2},{5,3},{6,0},{7,1},{8,14},{9,15},{10,... | collective-permute-start | bytes 12296 | tf_op jit(solution)/shard_map/ppermute | solution.py:523
  25.6 2.0 %collective-permute-start.6 = (f32[8,128]{1,0:T(8,128)S(1)}, f32[8,128]{1,0:T(8,128)S(1)}, u32[]{:S(2)}, u32[]{:S(2)}) collective-permute-start(f32[8,128]{1,0:T(8,128)S(1)} %get-tuple-element.91.refs_0_.refs_16_.refs_8_), channel_id=1, source_target_pairs={{0,2},{1,3},{2,0},{3,1},{4,6},{5,7},{6,4},{7,5},{8,10},{9,11},{10,... | collective-permute-start | bytes 12296 | tf_op jit(solution)/shard_map/ppermute | solution.py:523
  28.2 2.4 %collective-permute-start.9 = (bf16[512,128]{1,0:T(8,128)(2,1)S(1)}, bf16[512,128]{1,0:T(8,128)(2,1)S(1)}, u32[]{:S(2)}, u32[]{:S(2)}) collective-permute-start(bf16[512,128]{1,0:T(8,128)(2,1)S(1)} %get-tuple-element.95), channel_id=1, source_target_pairs={{0,1},{1,0},{2,3},{3,2},{4,5},{5,4},{6,7},{7,6},{8,9},{9,8},{10,11... | collective-permute-start | bytes 393224 | tf_op jit(solution)/shard_map/ppermute | solution.py:523
  30.6 7.4 %shard_map.149 = (bf16[2,512,128]{2,1,0:T(8,128)(2,1)S(1)}, bf16[2,512,128]{2,1,0:T(8,128)(2,1)S(1)}, f32[8,128]{1,0:T(8,128)S(1)}) custom-call(s32[5]{0:T(128)S(1)} %stack.23.where_ref, f32[2,512,128]{2,1,0:T(8,128)S(1)} %get-tuple-element.90.hidden_ref.refs_2_.refs_1_, s32[2,27,512]{2,1,0:T(8,128)S(1)} %shard_map.147.near_ref.refs_4_, ...), custom_call_target="tpu_custom_call" | custom-call | flops 14495514624 | bytes 1048576 | tf_op jit(solution)/shard_map/pallas_call | solution.py:508
  38.0 1.2 collective-permute-start.12
  39.2 2.4 %collective-permute-start.10 = (f32[8,128]{1,0:T(8,128)S(1)}, f32[8,128]{1,0:T(8,128)S(1)}, u32[]{:S(2)}, u32[]{:S(2)}) collective-permute-start(f32[8,128]{1,0:T(8,128)S(1)} %get-tuple-element.96.refs_0_.refs_8_), channel_id=1, source_target_pairs={{0,2},{1,3},{2,0},{3,1},{4,6},{5,7},{6,4},{7,5},{8,10},{9,11},{10,... | collective-permute-start | bytes 12296 | tf_op jit(solution)/shard_map/ppermute | solution.py:523
  42.6 1.2 shard_map.151
  43.8 2.1 %collective-permute-start.15 = (f32[8,128]{1,0:T(8,128)S(1)}, f32[8,128]{1,0:T(8,128)S(1)}, u32[]{:S(2)}, u32[]{:S(2)}) collective-permute-start(f32[8,128]{1,0:T(8,128)S(1)} %get-tuple-element.99.refs_12_), channel_id=1, source_target_pairs={{0,6},{1,7},{2,4},{3,5},{4,2},{5,3},{6,0},{7,1},{8,14},{9,15},{10,... | collective-permute-start | bytes 12296 | tf_op jit(solution)/shard_map/ppermute | solution.py:523
  46.5 0.9 collective-permute-start.13
  47.4 4.3 %collective-permute-start.17 = (bf16[512,128]{1,0:T(8,128)(2,1)S(1)}, bf16[512,128]{1,0:T(8,128)(2,1)S(1)}, u32[]{:S(2)}, u32[]{:S(2)}) collective-permute-start(bf16[512,128]{1,0:T(8,128)(2,1)S(1)} %get-tuple-element.102), channel_id=1, source_target_pairs={{0,1},{1,0},{2,3},{3,2},{4,5},{5,4},{6,7},{7,6},{8,9},{9,8},{10,11... | collective-permute-start | bytes 393224 | tf_op jit(solution)/shard_map/ppermute | solution.py:523
  51.7 8.2 %shard_map.152 = (f32[2,512,128]{2,1,0:T(8,128)S(1)}, f32[8,128]{1,0:T(8,128)S(1)}, bf16[1792,128]{1,0:T(8,128)(2,1)S(1)}, bf16[1792,128]{1,0:T(8,128)(2,1)S(1)}) custom-call(s32[5]{0:T(128)S(1)} %stack.23.where_ref, f32[2,512,128]{2,1,0:T(8,128)S(1)} %get-tuple-element.97.refs_0_.refs_20_, bf16[2,512,128]{2,1,0:T(8,128)(2,1)S(1)} %get-tuple-element.92.hidden_ref.refs_1_, ...), custom_call_target="tpu_custom_call" | custom-call | flops 14495514624 | bytes 1048576 | tf_op jit(solution)/shard_map/pallas_call | solution.py:508
  60.0 1.2 collective-permute-start.20
  61.2 2.4 %collective-permute-start.18 = (f32[8,128]{1,0:T(8,128)S(1)}, f32[8,128]{1,0:T(8,128)S(1)}, u32[]{:S(2)}, u32[]{:S(2)}) collective-permute-start(f32[8,128]{1,0:T(8,128)S(1)} %get-tuple-element.105.refs_12_.refs_8_), channel_id=1, source_target_pairs={{0,2},{1,3},{2,0},{3,1},{4,6},{5,7},{6,4},{7,5},{8,10},{9,11},{10,... | collective-permute-start | bytes 12296 | tf_op jit(solution)/shard_map/ppermute | solution.py:523
  63.6 2.4 %collective-permute-start.16 = (bf16[1792,128]{1,0:T(8,128)(2,1)S(1)}, bf16[1792,128]{1,0:T(8,128)(2,1)S(1)}, u32[]{:S(2)}, u32[]{:S(2)}) collective-permute-start(bf16[1792,128]{1,0:T(8,128)(2,1)S(1)} %get-tuple-element.101), channel_id=1, source_target_pairs={{0,1},{1,0},{2,3},{3,2},{4,5},{5,4},{6,7},{7,6},{8,9},{9,8},{10,11... | collective-permute-start | bytes 1376264 | tf_op jit(solution)/shard_map/ppermute | solution.py:523
  66.0 8.5 %shard_map.153 = (f32[2,512,128]{2,1,0:T(8,128)S(1)}, f32[8,128]{1,0:T(8,128)S(1)}, bf16[1792,128]{1,0:T(8,128)(2,1)S(1)}, bf16[1792,128]{1,0:T(8,128)(2,1)S(1)}) custom-call(s32[5]{0:T(128)S(1)} %stack.23.where_ref, f32[2,512,128]{2,1,0:T(8,128)S(1)} %get-tuple-element.104.refs_0_, f32[2,512,128]{2,1,0:T(8,128)S(1)} %get-tuple-element.90.hidden_ref.refs_2_.refs_1_, ...), custom_call_target="tpu_custom_call" | custom-call | flops 14495514624 | bytes 1048576 | tf_op jit(solution)/shard_map/pallas_call | solution.py:508
  74.5 2.7 %collective-permute-start.21 = (bf16[1792,128]{1,0:T(8,128)(2,1)S(1)}, bf16[1792,128]{1,0:T(8,128)(2,1)S(1)}, u32[]{:S(2)}, u32[]{:S(2)}) collective-permute-start(bf16[1792,128]{1,0:T(8,128)(2,1)S(1)} %get-tuple-element.107), channel_id=1, source_target_pairs={{0,1},{1,0},{2,3},{3,2},{4,5},{5,4},{6,7},{7,6},{8,9},{9,8},{10,11... | collective-permute-start | bytes 1376264 | tf_op jit(solution)/shard_map/ppermute | solution.py:523
  77.3 1.4 %collective-permute-done.21.refs_3_ = bf16[1792,128]{1,0:T(8,128)(2,1)S(1)} collective-permute-done((bf16[1792,128]{1,0:T(8,128)(2,1)S(1)}, bf16[1792,128]{1,0:T(8,128)(2,1)S(1)}, u32[]{:S(2)}, u32[]{:S(2)}) %collective-permute-start.21) | collective-permute-done | bytes 458784 | tf_op jit(solution)/shard_map/ppermute | solution.py:523
  79.5 2.2 %collective-permute-start.22 = (bf16[896,128]{1,0:T(8,128)(2,1)S(1)}, bf16[896,128]{1,0:T(8,128)(2,1)S(1)}, u32[]{:S(2)}, u32[]{:S(2)}) collective-permute-start(bf16[896,128]{1,0:T(8,128)(2,1)S(1)} %get-tuple-element.109), channel_id=1, source_target_pairs={{0,24},{8,16},{16,8},{24,0},{1,25},{9,17},{17,9},{25,1},{2,26},{10... | collective-permute-start | bytes 688136 | tf_op jit(solution)/shard_map/ppermute | solution.py:523
  82.2 1.1 collective-permute-start.27
  84.0 2.4 %collective-permute-done.27.refs_7_ = f32[8,128]{1,0:T(8,128)S(1)} collective-permute-done((f32[8,128]{1,0:T(8,128)S(1)}, f32[8,128]{1,0:T(8,128)S(1)}, u32[]{:S(2)}, u32[]{:S(2)}) %collective-permute-start.27) | collective-permute-done | bytes 4128 | tf_op jit(solution)/shard_map/ppermute | solution.py:523
  87.0 2.2 %collective-permute-done.25.refs_5_ = f32[8,128]{1,0:T(8,128)S(1)} collective-permute-done((f32[8,128]{1,0:T(8,128)S(1)}, f32[8,128]{1,0:T(8,128)S(1)}, u32[]{:S(2)}, u32[]{:S(2)}) %collective-permute-start.25) | collective-permute-done | bytes 4128 | tf_op jit(solution)/shard_map/ppermute | solution.py:523
  89.2 1.1 shard_map.155
  90.3 3.3 %collective-permute-start.28 = (bf16[256,128]{1,0:T(8,128)(2,1)S(1)}, bf16[256,128]{1,0:T(8,128)(2,1)S(1)}, u32[]{:S(2)}, u32[]{:S(2)}) collective-permute-start(bf16[256,128]{1,0:T(8,128)(2,1)S(1)} %get-tuple-element.116), channel_id=1, source_target_pairs={{0,1},{1,0},{2,3},{3,2},{4,5},{5,4},{6,7},{7,6},{8,9},{9,8},{10,11... | collective-permute-start | bytes 196616 | tf_op jit(solution)/shard_map/ppermute | solution.py:523
  93.6 0.9 collective-permute-done.28.refs_5_
  95.2 1.2 collective-permute-start.29
  96.4 2.4 %collective-permute-start.31 = (bf16[288,128]{1,0:T(8,128)(2,1)S(1)}, bf16[288,128]{1,0:T(8,128)(2,1)S(1)}, u32[]{:S(2)}, u32[]{:S(2)}) collective-permute-start(bf16[288,128]{1,0:T(8,128)(2,1)S(1)} %get-tuple-element.120), channel_id=1, source_target_pairs={{0,2},{1,3},{2,0},{3,1},{4,6},{5,7},{6,4},{7,5},{8,10},{9,11},{10,... | collective-permute-start | bytes 221192 | tf_op jit(solution)/shard_map/ppermute | solution.py:523
  98.8 1.6 %collective-permute-done.29.refs_1_ = bf16[288,128]{1,0:T(8,128)(2,1)S(1)} collective-permute-done((bf16[288,128]{1,0:T(8,128)(2,1)S(1)}, bf16[288,128]{1,0:T(8,128)(2,1)S(1)}, u32[]{:S(2)}, u32[]{:S(2)}) %collective-permute-start.29) | collective-permute-done | bytes 73760 | tf_op jit(solution)/shard_map/ppermute | solution.py:523
  100.4 4.0 %collective-permute-done.30.refs_2_ = bf16[288,128]{1,0:T(8,128)(2,1)S(1)} collective-permute-done((bf16[288,128]{1,0:T(8,128)(2,1)S(1)}, bf16[288,128]{1,0:T(8,128)(2,1)S(1)}, u32[]{:S(2)}, u32[]{:S(2)}) %collective-permute-start.30) | collective-permute-done | bytes 73760 | tf_op jit(solution)/shard_map/ppermute | solution.py:523
  105.1 1.4 %collective-permute-start.33 = (bf16[288,128]{1,0:T(8,128)(2,1)S(1)}, bf16[288,128]{1,0:T(8,128)(2,1)S(1)}, u32[]{:S(2)}, u32[]{:S(2)}) collective-permute-start(bf16[288,128]{1,0:T(8,128)(2,1)S(1)} %shard_map.157.refs_0_), channel_id=1, source_target_pairs={{0,4},{1,5},{2,6},{3,7},{4,0},{5,1},{6,2},{7,3},{8,12},{9,13},{10,... | collective-permute-start | bytes 221192 | tf_op jit(solution)/shard_map/ppermute | solution.py:523
  106.5 2.1 %collective-permute-start.32 = (bf16[288,128]{1,0:T(8,128)(2,1)S(1)}, bf16[288,128]{1,0:T(8,128)(2,1)S(1)}, u32[]{:S(2)}, u32[]{:S(2)}) collective-permute-start(bf16[288,128]{1,0:T(8,128)(2,1)S(1)} %shard_map.157.refs_0_), channel_id=1, source_target_pairs={{0,6},{1,7},{2,4},{3,5},{4,2},{5,3},{6,0},{7,1},{8,14},{9,15},{10,... | collective-permute-start | bytes 221192 | tf_op jit(solution)/shard_map/ppermute | solution.py:523
  108.6 1.3 collective-permute-start.35
  110.8 1.4 %collective-permute-done.32.refs_1_ = bf16[288,128]{1,0:T(8,128)(2,1)S(1)} collective-permute-done((bf16[288,128]{1,0:T(8,128)(2,1)S(1)}, bf16[288,128]{1,0:T(8,128)(2,1)S(1)}, u32[]{:S(2)}, u32[]{:S(2)}) %collective-permute-start.32) | collective-permute-done | bytes 73760 | tf_op jit(solution)/shard_map/ppermute | solution.py:523
  112.7 1.3 collective-permute-start.38
  114.0 1.2 collective-permute-start.37
  115.5 3.2 %shard_map.159 = (bf16[64,2048]{1,0:T(8,128)(2,1)S(1)}, bf16[64,2048]{1,0:T(8,128)(2,1)S(1)}) custom-call(s32[5]{0:T(128)S(1)} %stack.23.where_ref, bf16[2,512,128]{2,1,0:T(8,128)(2,1)S(1)} %get-tuple-element.126.rows_ref, f32[2,8,2048]{2,1,0:T(8,128)S(1)} %get-tuple-element.127.which_ref, s32[2,8,512]{2,1,0:T(8,128)S(1)} %get-tuple-element.128.tables_ref, ...), custom_call_target="tpu_custom_call" | custom-call | bytes 1 | tf_op jit(solution)/shard_map/pallas_call | solution.py:508
  118.6 3.4 %collective-permute-start.39 = (bf16[64,2048]{1,0:T(8,128)(2,1)S(1)}, bf16[64,2048]{1,0:T(8,128)(2,1)S(1)}, u32[]{:S(2)}, u32[]{:S(2)}) collective-permute-start(bf16[64,2048]{1,0:T(8,128)(2,1)S(1)} %get-tuple-element.130), channel_id=1, source_target_pairs={{0,1},{1,0},{2,3},{3,2},{4,5},{5,4},{6,7},{7,6},{8,9},{9,8},{10,11... | collective-permute-start | bytes 786440 | tf_op jit(solution)/shard_map/ppermute | solution.py:523
  122.1 1.1 collective-permute-done.39.other_input
  123.2 1.5 %shard_map.160 = (bf16[2,512,128]{2,1,0:T(8,128)(2,1)}, bf16[2,64,2048]{2,1,0:T(8,128)(2,1)}) custom-call(s32[5]{0:T(128)S(1)} %stack.23.where_ref, bf16[512,128]{1,0:T(8,128)(2,1)S(1)} %get-tuple-element.124.own_features, bf16[512,128]{1,0:T(8,128)(2,1)S(1)} %collective-permute-done.17.other_features, bf16[64,2048]{1,0:T(8,128)(2,1)S(1)} %get-tuple-element.129.own_input, ...), custom_call_target="tpu_custom_call" | custom-call | bytes 1 | tf_op jit(solution)/shard_map/pallas_call | solution.py:508
  124.7 1.6 %collective-permute-done.36.refs_1_ = bf16[1168,128]{1,0:T(8,128)(2,1)S(1)} collective-permute-done((bf16[1168,128]{1,0:T(8,128)(2,1)S(1)}, bf16[1168,128]{1,0:T(8,128)(2,1)S(1)}, u32[]{:S(2)}, u32[]{:S(2)}) %collective-permute-start.36) | collective-permute-done | bytes 299040 | tf_op jit(solution)/shard_map/ppermute | solution.py:523
  126.3 3.7 %collective-permute-start.41 = (bf16[1168,128]{1,0:T(8,128)(2,1)S(1)}, bf16[1168,128]{1,0:T(8,128)(2,1)S(1)}, u32[]{:S(2)}, u32[]{:S(2)}) collective-permute-start(bf16[1168,128]{1,0:T(8,128)(2,1)S(1)} %collective-permute-done.36.refs_1_), channel_id=1, source_target_pairs={{0,1},{1,0},{2,3},{3,2},{4,5},{5,4},{6,7},{7,6},{8,9},{9,8},{10,11... | collective-permute-start | bytes 897032 | tf_op jit(solution)/shard_map/ppermute | solution.py:523
  130.5 2.5 %shard_map.161 = (f32[3456,128]{1,0:T(8,128)}, f32[3456,128]{1,0:T(8,128)}, f32[512,128]{1,0:T(8,128)}, f32[3,128]{1,0:T(4,128)}, f32[3,128]{1,0:T(4,128)}) custom-call(s32[5]{0:T(128)S(1)} %stack.23.where_ref, bf16[1168,128]{1,0:T(8,128)(2,1)S(1)} %shard_map.158.refs_0_, bf16[1168,128]{1,0:T(8,128)(2,1)S(1)} %collective-permute-done.36.refs_1_, ...), custom_call_target="tpu_custom_call" | custom-call | flops 1000000000 | bytes 1048576 | tf_op jit(solution)/shard_map/pallas_call | solution.py:508
  133.0 2.0 %shard_map.162 = (f32[3456,128]{1,0:T(8,128)}, f32[3456,128]{1,0:T(8,128)}, f32[512,128]{1,0:T(8,128)}) custom-call(s32[5]{0:T(128)S(1)} %stack.23.where_ref, bf16[1168,128]{1,0:T(8,128)(2,1)S(1)} %collective-permute-done.40.refs_0_, ...), custom_call_target="tpu_custom_call", output_to_operand_aliasing={{0}: (5, {}), {1}: (6, {}), {2}: (7, {})} | custom-call | flops 1000000000 | bytes 1048576 | tf_op jit(solution)/shard_map/pallas_call | solution.py:508
  (72 shorter events, 10.1 us)
Async XLA Ops:
  2.4 3.4 %collective-permute-start = (bf16[64,2048]{1,0:T(8,128)(2,1)S(1)}, bf16[64,2048]{1,0:T(8,128)(2,1)S(1)}, u32[]{:S(2)}, u32[]{:S(2)}) collective-permute-start(bf16[64,2048]{1,0:T(8,128)(2,1)S(1)} %get-tuple-element.77), channel_id=1, source_target_pairs={{0,1},{1,0},{2,3},{3,2},{4,5},{5,4},{6,7},{7,6},{8,9},{9,8},{10,11... | collective-permute-start | bytes 786440 | tf_op jit(solution)/shard_map/ppermute | solution.py:523
  2.6 3.3 %collective-permute-start.1 = (s32[8,512]{1,0:T(8,128)S(1)}, s32[8,512]{1,0:T(8,128)S(1)}, u32[]{:S(2)}, u32[]{:S(2)}) collective-permute-start(s32[8,512]{1,0:T(8,128)S(1)} %get-tuple-element.78), channel_id=1, source_target_pairs={{0,1},{1,0},{2,3},{3,2},{4,5},{5,4},{6,7},{7,6},{8,9},{9,8},{10,11... | collective-permute-start | bytes 49160 | tf_op jit(solution)/shard_map/ppermute | solution.py:523
  5.7 8.0 %collective-permute-start.2 = (s32[27,512]{1,0:T(8,128)S(1)}, s32[27,512]{1,0:T(8,128)S(1)}, u32[]{:S(2)}, u32[]{:S(2)}) collective-permute-start(s32[27,512]{1,0:T(8,128)S(1)} %get-tuple-element.88), channel_id=1, source_target_pairs={{0,1},{1,0},{2,3},{3,2},{4,5},{5,4},{6,7},{7,6},{8,9},{9,8},{10,11... | collective-permute-start | bytes 165896 | tf_op jit(solution)/shard_map/ppermute | solution.py:523
  5.9 10.9 %copy-start.2 = (bf16[27,128,128]{2,1,0:T(8,128)(2,1)S(1)}, bf16[27,128,128]{2,1,0:T(8,128)(2,1)}, u32[]{:S(2)}) copy-start(bf16[27,128,128]{2,1,0:T(8,128)(2,1)} %refs_5_.3) | copy-start | bytes 2654212
  5.9 10.9 %copy-start.4 = (f32[3,128]{1,0:T(4,128)S(1)}, f32[3,128]{1,0:T(4,128)}, u32[]{:S(2)}) copy-start(f32[3,128]{1,0:T(4,128)} %refs_7_.3) | copy-start | bytes 4612
  5.9 10.9 %copy-start.5 = (f32[3,128]{1,0:T(4,128)S(1)}, f32[3,128]{1,0:T(4,128)}, u32[]{:S(2)}) copy-start(f32[3,128]{1,0:T(4,128)} %scale_ref.7) | copy-start | bytes 4612
  8.6 5.8 %collective-permute-start.5 = (f32[8,128]{1,0:T(8,128)S(1)}, f32[8,128]{1,0:T(8,128)S(1)}, u32[]{:S(2)}, u32[]{:S(2)}) collective-permute-start(f32[8,128]{1,0:T(8,128)S(1)} %get-tuple-element.89.refs_0_.refs_16_), channel_id=1, source_target_pairs={{0,6},{1,7},{2,4},{3,5},{4,2},{5,3},{6,0},{7,1},{8,14},{9,15},{10,... | collective-permute-start | bytes 12296 | tf_op jit(solution)/shard_map/ppermute | solution.py:523
  13.4 3.4 %collective-permute-start.4 = (f32[8,128]{1,0:T(8,128)S(1)}, f32[8,128]{1,0:T(8,128)S(1)}, u32[]{:S(2)}, u32[]{:S(2)}) collective-permute-start(f32[8,128]{1,0:T(8,128)S(1)} %get-tuple-element.89.refs_0_.refs_16_), channel_id=1, source_target_pairs={{0,4},{1,5},{2,6},{3,7},{4,0},{5,1},{6,2},{7,3},{8,12},{9,13},{10,... | collective-permute-start | bytes 12296 | tf_op jit(solution)/shard_map/ppermute | solution.py:523
  13.4 3.4 %collective-permute-start.3 = (f32[8,128]{1,0:T(8,128)S(1)}, f32[8,128]{1,0:T(8,128)S(1)}, u32[]{:S(2)}, u32[]{:S(2)}) collective-permute-start(f32[8,128]{1,0:T(8,128)S(1)} %get-tuple-element.89.refs_0_.refs_16_), channel_id=1, source_target_pairs={{0,2},{1,3},{2,0},{3,1},{4,6},{5,7},{6,4},{7,5},{8,10},{9,11},{10,... | collective-permute-start | bytes 12296 | tf_op jit(solution)/shard_map/ppermute | solution.py:523
  16.8 13.8 %copy-start.1 = (bf16[27,128,128]{2,1,0:T(8,128)(2,1)S(1)}, bf16[27,128,128]{2,1,0:T(8,128)(2,1)}, u32[]{:S(2)}) copy-start(bf16[27,128,128]{2,1,0:T(8,128)(2,1)} %refs_5_.2) | copy-start | bytes 2654212
  24.0 6.6 %collective-permute-start.8 = (f32[8,128]{1,0:T(8,128)S(1)}, f32[8,128]{1,0:T(8,128)S(1)}, u32[]{:S(2)}, u32[]{:S(2)}) collective-permute-start(f32[8,128]{1,0:T(8,128)S(1)} %get-tuple-element.91.refs_0_.refs_16_.refs_8_), channel_id=1, source_target_pairs={{0,6},{1,7},{2,4},{3,5},{4,2},{5,3},{6,0},{7,1},{8,14},{9,15},{10,... | collective-permute-start | bytes 12296 | tf_op jit(solution)/shard_map/ppermute | solution.py:523
  25.5 5.1 %collective-permute-start.7 = (f32[8,128]{1,0:T(8,128)S(1)}, f32[8,128]{1,0:T(8,128)S(1)}, u32[]{:S(2)}, u32[]{:S(2)}) collective-permute-start(f32[8,128]{1,0:T(8,128)S(1)} %get-tuple-element.91.refs_0_.refs_16_.refs_8_), channel_id=1, source_target_pairs={{0,4},{1,5},{2,6},{3,7},{4,0},{5,1},{6,2},{7,3},{8,12},{9,13},{10,... | collective-permute-start | bytes 12296 | tf_op jit(solution)/shard_map/ppermute | solution.py:523
  25.6 5.0 %collective-permute-start.6 = (f32[8,128]{1,0:T(8,128)S(1)}, f32[8,128]{1,0:T(8,128)S(1)}, u32[]{:S(2)}, u32[]{:S(2)}) collective-permute-start(f32[8,128]{1,0:T(8,128)S(1)} %get-tuple-element.91.refs_0_.refs_16_.refs_8_), channel_id=1, source_target_pairs={{0,2},{1,3},{2,0},{3,1},{4,6},{5,7},{6,4},{7,5},{8,10},{9,11},{10,... | collective-permute-start | bytes 12296 | tf_op jit(solution)/shard_map/ppermute | solution.py:523
  28.2 13.4 %collective-permute-start.9 = (bf16[512,128]{1,0:T(8,128)(2,1)S(1)}, bf16[512,128]{1,0:T(8,128)(2,1)S(1)}, u32[]{:S(2)}, u32[]{:S(2)}) collective-permute-start(bf16[512,128]{1,0:T(8,128)(2,1)S(1)} %get-tuple-element.95), channel_id=1, source_target_pairs={{0,1},{1,0},{2,3},{3,2},{4,5},{5,4},{6,7},{7,6},{8,9},{9,8},{10,11... | collective-permute-start | bytes 393224 | tf_op jit(solution)/shard_map/ppermute | solution.py:523
  38.0 4.3 %collective-permute-start.12 = (f32[8,128]{1,0:T(8,128)S(1)}, f32[8,128]{1,0:T(8,128)S(1)}, u32[]{:S(2)}, u32[]{:S(2)}) collective-permute-start(f32[8,128]{1,0:T(8,128)S(1)} %get-tuple-element.96.refs_0_.refs_8_), channel_id=1, source_target_pairs={{0,6},{1,7},{2,4},{3,5},{4,2},{5,3},{6,0},{7,1},{8,14},{9,15},{10,... | collective-permute-start | bytes 12296 | tf_op jit(solution)/shard_map/ppermute | solution.py:523
  39.2 3.4 %collective-permute-start.11 = (f32[8,128]{1,0:T(8,128)S(1)}, f32[8,128]{1,0:T(8,128)S(1)}, u32[]{:S(2)}, u32[]{:S(2)}) collective-permute-start(f32[8,128]{1,0:T(8,128)S(1)} %get-tuple-element.96.refs_0_.refs_8_), channel_id=1, source_target_pairs={{0,4},{1,5},{2,6},{3,7},{4,0},{5,1},{6,2},{7,3},{8,12},{9,13},{10,... | collective-permute-start | bytes 12296 | tf_op jit(solution)/shard_map/ppermute | solution.py:523
  39.2 3.4 %collective-permute-start.10 = (f32[8,128]{1,0:T(8,128)S(1)}, f32[8,128]{1,0:T(8,128)S(1)}, u32[]{:S(2)}, u32[]{:S(2)}) collective-permute-start(f32[8,128]{1,0:T(8,128)S(1)} %get-tuple-element.96.refs_0_.refs_8_), channel_id=1, source_target_pairs={{0,2},{1,3},{2,0},{3,1},{4,6},{5,7},{6,4},{7,5},{8,10},{9,11},{10,... | collective-permute-start | bytes 12296 | tf_op jit(solution)/shard_map/ppermute | solution.py:523
  43.8 7.9 %collective-permute-start.15 = (f32[8,128]{1,0:T(8,128)S(1)}, f32[8,128]{1,0:T(8,128)S(1)}, u32[]{:S(2)}, u32[]{:S(2)}) collective-permute-start(f32[8,128]{1,0:T(8,128)S(1)} %get-tuple-element.99.refs_12_), channel_id=1, source_target_pairs={{0,6},{1,7},{2,4},{3,5},{4,2},{5,3},{6,0},{7,1},{8,14},{9,15},{10,... | collective-permute-start | bytes 12296 | tf_op jit(solution)/shard_map/ppermute | solution.py:523
  45.9 5.8 %collective-permute-start.14 = (f32[8,128]{1,0:T(8,128)S(1)}, f32[8,128]{1,0:T(8,128)S(1)}, u32[]{:S(2)}, u32[]{:S(2)}) collective-permute-start(f32[8,128]{1,0:T(8,128)S(1)} %get-tuple-element.99.refs_12_), channel_id=1, source_target_pairs={{0,4},{1,5},{2,6},{3,7},{4,0},{5,1},{6,2},{7,3},{8,12},{9,13},{10,... | collective-permute-start | bytes 12296 | tf_op jit(solution)/shard_map/ppermute | solution.py:523
  46.5 5.3 %collective-permute-start.13 = (f32[8,128]{1,0:T(8,128)S(1)}, f32[8,128]{1,0:T(8,128)S(1)}, u32[]{:S(2)}, u32[]{:S(2)}) collective-permute-start(f32[8,128]{1,0:T(8,128)S(1)} %get-tuple-element.99.refs_12_), channel_id=1, source_target_pairs={{0,2},{1,3},{2,0},{3,1},{4,6},{5,7},{6,4},{7,5},{8,10},{9,11},{10,... | collective-permute-start | bytes 12296 | tf_op jit(solution)/shard_map/ppermute | solution.py:523
  47.4 18.6 %collective-permute-start.17 = (bf16[512,128]{1,0:T(8,128)(2,1)S(1)}, bf16[512,128]{1,0:T(8,128)(2,1)S(1)}, u32[]{:S(2)}, u32[]{:S(2)}) collective-permute-start(bf16[512,128]{1,0:T(8,128)(2,1)S(1)} %get-tuple-element.102), channel_id=1, source_target_pairs={{0,1},{1,0},{2,3},{3,2},{4,5},{5,4},{6,7},{7,6},{8,9},{9,8},{10,11... | collective-permute-start | bytes 393224 | tf_op jit(solution)/shard_map/ppermute | solution.py:523
  60.0 6.0 %collective-permute-start.20 = (f32[8,128]{1,0:T(8,128)S(1)}, f32[8,128]{1,0:T(8,128)S(1)}, u32[]{:S(2)}, u32[]{:S(2)}) collective-permute-start(f32[8,128]{1,0:T(8,128)S(1)} %get-tuple-element.105.refs_12_.refs_8_), channel_id=1, source_target_pairs={{0,6},{1,7},{2,4},{3,5},{4,2},{5,3},{6,0},{7,1},{8,14},{9,15},{10,... | collective-permute-start | bytes 12296 | tf_op jit(solution)/shard_map/ppermute | solution.py:523
  61.2 4.8 %collective-permute-start.19 = (f32[8,128]{1,0:T(8,128)S(1)}, f32[8,128]{1,0:T(8,128)S(1)}, u32[]{:S(2)}, u32[]{:S(2)}) collective-permute-start(f32[8,128]{1,0:T(8,128)S(1)} %get-tuple-element.105.refs_12_.refs_8_), channel_id=1, source_target_pairs={{0,4},{1,5},{2,6},{3,7},{4,0},{5,1},{6,2},{7,3},{8,12},{9,13},{10,... | collective-permute-start | bytes 12296 | tf_op jit(solution)/shard_map/ppermute | solution.py:523
  61.2 4.8 %collective-permute-start.18 = (f32[8,128]{1,0:T(8,128)S(1)}, f32[8,128]{1,0:T(8,128)S(1)}, u32[]{:S(2)}, u32[]{:S(2)}) collective-permute-start(f32[8,128]{1,0:T(8,128)S(1)} %get-tuple-element.105.refs_12_.refs_8_), channel_id=1, source_target_pairs={{0,2},{1,3},{2,0},{3,1},{4,6},{5,7},{6,4},{7,5},{8,10},{9,11},{10,... | collective-permute-start | bytes 12296 | tf_op jit(solution)/shard_map/ppermute | solution.py:523
  63.6 13.6 %collective-permute-start.16 = (bf16[1792,128]{1,0:T(8,128)(2,1)S(1)}, bf16[1792,128]{1,0:T(8,128)(2,1)S(1)}, u32[]{:S(2)}, u32[]{:S(2)}) collective-permute-start(bf16[1792,128]{1,0:T(8,128)(2,1)S(1)} %get-tuple-element.101), channel_id=1, source_target_pairs={{0,1},{1,0},{2,3},{3,2},{4,5},{5,4},{6,7},{7,6},{8,9},{9,8},{10,11... | collective-permute-start | bytes 1376264 | tf_op jit(solution)/shard_map/ppermute | solution.py:523
  74.5 4.2 %collective-permute-start.21 = (bf16[1792,128]{1,0:T(8,128)(2,1)S(1)}, bf16[1792,128]{1,0:T(8,128)(2,1)S(1)}, u32[]{:S(2)}, u32[]{:S(2)}) collective-permute-start(bf16[1792,128]{1,0:T(8,128)(2,1)S(1)} %get-tuple-element.107), channel_id=1, source_target_pairs={{0,1},{1,0},{2,3},{3,2},{4,5},{5,4},{6,7},{7,6},{8,9},{9,8},{10,11... | collective-permute-start | bytes 1376264 | tf_op jit(solution)/shard_map/ppermute | solution.py:523
  79.5 15.0 %collective-permute-start.22 = (bf16[896,128]{1,0:T(8,128)(2,1)S(1)}, bf16[896,128]{1,0:T(8,128)(2,1)S(1)}, u32[]{:S(2)}, u32[]{:S(2)}) collective-permute-start(bf16[896,128]{1,0:T(8,128)(2,1)S(1)} %get-tuple-element.109), channel_id=1, source_target_pairs={{0,24},{8,16},{16,8},{24,0},{1,25},{9,17},{17,9},{25,1},{2,26},{10... | collective-permute-start | bytes 688136 | tf_op jit(solution)/shard_map/ppermute | solution.py:523
  81.7 12.8 %collective-permute-start.23 = (bf16[896,128]{1,0:T(8,128)(2,1)S(1)}, bf16[896,128]{1,0:T(8,128)(2,1)S(1)}, u32[]{:S(2)}, u32[]{:S(2)}) collective-permute-start(bf16[896,128]{1,0:T(8,128)(2,1)S(1)} %get-tuple-element.110), channel_id=1, source_target_pairs={{0,16},{8,24},{16,0},{24,8},{1,17},{9,25},{17,1},{25,9},{2,18},{10... | collective-permute-start | bytes 688136 | tf_op jit(solution)/shard_map/ppermute | solution.py:523
  81.9 12.6 %collective-permute-start.24 = (bf16[896,128]{1,0:T(8,128)(2,1)S(1)}, bf16[896,128]{1,0:T(8,128)(2,1)S(1)}, u32[]{:S(2)}, u32[]{:S(2)}) collective-permute-start(bf16[896,128]{1,0:T(8,128)(2,1)S(1)} %get-tuple-element.111), channel_id=1, source_target_pairs={{0,8},{8,0},{16,24},{24,16},{1,9},{9,1},{17,25},{25,17},{2,10},{10... | collective-permute-start | bytes 688136 | tf_op jit(solution)/shard_map/ppermute | solution.py:523
  82.2 4.3 %collective-permute-start.27 = (f32[8,128]{1,0:T(8,128)S(1)}, f32[8,128]{1,0:T(8,128)S(1)}, u32[]{:S(2)}, u32[]{:S(2)}) collective-permute-start(f32[8,128]{1,0:T(8,128)S(1)} %get-tuple-element.114.refs_4_), channel_id=1, source_target_pairs={{0,6},{1,7},{2,4},{3,5},{4,2},{5,3},{6,0},{7,1},{8,14},{9,15},{10,... | collective-permute-start | bytes 12296 | tf_op jit(solution)/shard_map/ppermute | solution.py:523
  83.3 3.7 %collective-permute-start.26 = (f32[8,128]{1,0:T(8,128)S(1)}, f32[8,128]{1,0:T(8,128)S(1)}, u32[]{:S(2)}, u32[]{:S(2)}) collective-permute-start(f32[8,128]{1,0:T(8,128)S(1)} %get-tuple-element.114.refs_4_), channel_id=1, source_target_pairs={{0,4},{1,5},{2,6},{3,7},{4,0},{5,1},{6,2},{7,3},{8,12},{9,13},{10,... | collective-permute-start | bytes 12296 | tf_op jit(solution)/shard_map/ppermute | solution.py:523
  86.4 2.8 %collective-permute-start.25 = (f32[8,128]{1,0:T(8,128)S(1)}, f32[8,128]{1,0:T(8,128)S(1)}, u32[]{:S(2)}, u32[]{:S(2)}) collective-permute-start(f32[8,128]{1,0:T(8,128)S(1)} %get-tuple-element.114.refs_4_), channel_id=1, source_target_pairs={{0,2},{1,3},{2,0},{3,1},{4,6},{5,7},{6,4},{7,5},{8,10},{9,11},{10,... | collective-permute-start | bytes 12296 | tf_op jit(solution)/shard_map/ppermute | solution.py:523
  90.3 4.2 %collective-permute-start.28 = (bf16[256,128]{1,0:T(8,128)(2,1)S(1)}, bf16[256,128]{1,0:T(8,128)(2,1)S(1)}, u32[]{:S(2)}, u32[]{:S(2)}) collective-permute-start(bf16[256,128]{1,0:T(8,128)(2,1)S(1)} %get-tuple-element.116), channel_id=1, source_target_pairs={{0,1},{1,0},{2,3},{3,2},{4,5},{5,4},{6,7},{7,6},{8,9},{9,8},{10,11... | collective-permute-start | bytes 196616 | tf_op jit(solution)/shard_map/ppermute | solution.py:523
  95.2 5.2 %collective-permute-start.29 = (bf16[288,128]{1,0:T(8,128)(2,1)S(1)}, bf16[288,128]{1,0:T(8,128)(2,1)S(1)}, u32[]{:S(2)}, u32[]{:S(2)}) collective-permute-start(bf16[288,128]{1,0:T(8,128)(2,1)S(1)} %get-tuple-element.118), channel_id=1, source_target_pairs={{0,6},{1,7},{2,4},{3,5},{4,2},{5,3},{6,0},{7,1},{8,14},{9,15},{10,... | collective-permute-start | bytes 221192 | tf_op jit(solution)/shard_map/ppermute | solution.py:523
  96.4 8.0 %collective-permute-start.30 = (bf16[288,128]{1,0:T(8,128)(2,1)S(1)}, bf16[288,128]{1,0:T(8,128)(2,1)S(1)}, u32[]{:S(2)}, u32[]{:S(2)}) collective-permute-start(bf16[288,128]{1,0:T(8,128)(2,1)S(1)} %get-tuple-element.119), channel_id=1, source_target_pairs={{0,4},{1,5},{2,6},{3,7},{4,0},{5,1},{6,2},{7,3},{8,12},{9,13},{10,... | collective-permute-start | bytes 221192 | tf_op jit(solution)/shard_map/ppermute | solution.py:523
  96.4 8.0 %collective-permute-start.31 = (bf16[288,128]{1,0:T(8,128)(2,1)S(1)}, bf16[288,128]{1,0:T(8,128)(2,1)S(1)}, u32[]{:S(2)}, u32[]{:S(2)}) collective-permute-start(bf16[288,128]{1,0:T(8,128)(2,1)S(1)} %get-tuple-element.120), channel_id=1, source_target_pairs={{0,2},{1,3},{2,0},{3,1},{4,6},{5,7},{6,4},{7,5},{8,10},{9,11},{10,... | collective-permute-start | bytes 221192 | tf_op jit(solution)/shard_map/ppermute | solution.py:523
  105.0 5.8 %collective-permute-start.34 = (bf16[288,128]{1,0:T(8,128)(2,1)S(1)}, bf16[288,128]{1,0:T(8,128)(2,1)S(1)}, u32[]{:S(2)}, u32[]{:S(2)}) collective-permute-start(bf16[288,128]{1,0:T(8,128)(2,1)S(1)} %shard_map.157.refs_0_), channel_id=1, source_target_pairs={{0,2},{1,3},{2,0},{3,1},{4,6},{5,7},{6,4},{7,5},{8,10},{9,11},{10,... | collective-permute-start | bytes 221192 | tf_op jit(solution)/shard_map/ppermute | solution.py:523
  105.1 5.7 %collective-permute-start.33 = (bf16[288,128]{1,0:T(8,128)(2,1)S(1)}, bf16[288,128]{1,0:T(8,128)(2,1)S(1)}, u32[]{:S(2)}, u32[]{:S(2)}) collective-permute-start(bf16[288,128]{1,0:T(8,128)(2,1)S(1)} %shard_map.157.refs_0_), channel_id=1, source_target_pairs={{0,4},{1,5},{2,6},{3,7},{4,0},{5,1},{6,2},{7,3},{8,12},{9,13},{10,... | collective-permute-start | bytes 221192 | tf_op jit(solution)/shard_map/ppermute | solution.py:523
  106.5 5.7 %collective-permute-start.32 = (bf16[288,128]{1,0:T(8,128)(2,1)S(1)}, bf16[288,128]{1,0:T(8,128)(2,1)S(1)}, u32[]{:S(2)}, u32[]{:S(2)}) collective-permute-start(bf16[288,128]{1,0:T(8,128)(2,1)S(1)} %shard_map.157.refs_0_), channel_id=1, source_target_pairs={{0,6},{1,7},{2,4},{3,5},{4,2},{5,3},{6,0},{7,1},{8,14},{9,15},{10,... | collective-permute-start | bytes 221192 | tf_op jit(solution)/shard_map/ppermute | solution.py:523
  108.6 2.2 %collective-permute-start.35 = (f32[8,128]{1,0:T(8,128)S(1)}, f32[8,128]{1,0:T(8,128)S(1)}, u32[]{:S(2)}, u32[]{:S(2)}) collective-permute-start(f32[8,128]{1,0:T(8,128)S(1)} %get-tuple-element.121.refs_4_), channel_id=1, source_target_pairs={{0,1},{1,0},{2,3},{3,2},{4,5},{5,4},{6,7},{7,6},{8,9},{9,8},{10,11... | collective-permute-start | bytes 12296 | tf_op jit(solution)/shard_map/ppermute | solution.py:523
  112.7 11.9 %collective-permute-start.38 = (bf16[1168,128]{1,0:T(8,128)(2,1)S(1)}, bf16[1168,128]{1,0:T(8,128)(2,1)S(1)}, u32[]{:S(2)}, u32[]{:S(2)}) collective-permute-start(bf16[1168,128]{1,0:T(8,128)(2,1)S(1)} %shard_map.158.refs_0_), channel_id=1, source_target_pairs={{0,8},{8,0},{16,24},{24,16},{1,9},{9,1},{17,25},{25,17},{2,10},{10... | collective-permute-start | bytes 897032 | tf_op jit(solution)/shard_map/ppermute | solution.py:523
  114.0 10.6 %collective-permute-start.37 = (bf16[1168,128]{1,0:T(8,128)(2,1)S(1)}, bf16[1168,128]{1,0:T(8,128)(2,1)S(1)}, u32[]{:S(2)}, u32[]{:S(2)}) collective-permute-start(bf16[1168,128]{1,0:T(8,128)(2,1)S(1)} %shard_map.158.refs_0_), channel_id=1, source_target_pairs={{0,16},{8,24},{16,0},{24,8},{1,17},{9,25},{17,1},{25,9},{2,18},{10... | collective-permute-start | bytes 897032 | tf_op jit(solution)/shard_map/ppermute | solution.py:523
  115.3 11.0 %collective-permute-start.36 = (bf16[1168,128]{1,0:T(8,128)(2,1)S(1)}, bf16[1168,128]{1,0:T(8,128)(2,1)S(1)}, u32[]{:S(2)}, u32[]{:S(2)}) collective-permute-start(bf16[1168,128]{1,0:T(8,128)(2,1)S(1)} %shard_map.158.refs_0_), channel_id=1, source_target_pairs={{0,24},{8,16},{16,8},{24,0},{1,25},{9,17},{17,9},{25,1},{2,26},{10... | collective-permute-start | bytes 897032 | tf_op jit(solution)/shard_map/ppermute | solution.py:523
  118.6 4.6 %collective-permute-start.39 = (bf16[64,2048]{1,0:T(8,128)(2,1)S(1)}, bf16[64,2048]{1,0:T(8,128)(2,1)S(1)}, u32[]{:S(2)}, u32[]{:S(2)}) collective-permute-start(bf16[64,2048]{1,0:T(8,128)(2,1)S(1)} %get-tuple-element.130), channel_id=1, source_target_pairs={{0,1},{1,0},{2,3},{3,2},{4,5},{5,4},{6,7},{7,6},{8,9},{9,8},{10,11... | collective-permute-start | bytes 786440 | tf_op jit(solution)/shard_map/ppermute | solution.py:523
  122.0 11.0 %collective-permute-start.40 = (bf16[1168,128]{1,0:T(8,128)(2,1)S(1)}, bf16[1168,128]{1,0:T(8,128)(2,1)S(1)}, u32[]{:S(2)}, u32[]{:S(2)}) collective-permute-start(bf16[1168,128]{1,0:T(8,128)(2,1)S(1)} %shard_map.158.refs_0_), channel_id=1, source_target_pairs={{0,1},{1,0},{2,3},{3,2},{4,5},{5,4},{6,7},{7,6},{8,9},{9,8},{10,11... | collective-permute-start | bytes 897032 | tf_op jit(solution)/shard_map/ppermute | solution.py:523
  126.3 6.7 %collective-permute-start.41 = (bf16[1168,128]{1,0:T(8,128)(2,1)S(1)}, bf16[1168,128]{1,0:T(8,128)(2,1)S(1)}, u32[]{:S(2)}, u32[]{:S(2)}) collective-permute-start(bf16[1168,128]{1,0:T(8,128)(2,1)S(1)} %collective-permute-done.36.refs_1_), channel_id=1, source_target_pairs={{0,1},{1,0},{2,3},{3,2},{4,5},{5,4},{6,7},{7,6},{8,9},{9,8},{10,11... | collective-permute-start | bytes 897032 | tf_op jit(solution)/shard_map/ppermute | solution.py:523
  130.0 3.1 %collective-permute-start.42 = (bf16[1168,128]{1,0:T(8,128)(2,1)S(1)}, bf16[1168,128]{1,0:T(8,128)(2,1)S(1)}, u32[]{:S(2)}, u32[]{:S(2)}) collective-permute-start(bf16[1168,128]{1,0:T(8,128)(2,1)S(1)} %collective-permute-done.37.refs_2_), channel_id=1, source_target_pairs={{0,1},{1,0},{2,3},{3,2},{4,5},{5,4},{6,7},{7,6},{8,9},{9,8},{10,11... | collective-permute-start | bytes 897032 | tf_op jit(solution)/shard_map/ppermute | solution.py:523
  130.0 3.1 %collective-permute-start.43 = (bf16[1168,128]{1,0:T(8,128)(2,1)S(1)}, bf16[1168,128]{1,0:T(8,128)(2,1)S(1)}, u32[]{:S(2)}, u32[]{:S(2)}) collective-permute-start(bf16[1168,128]{1,0:T(8,128)(2,1)S(1)} %collective-permute-done.38.refs_3_), channel_id=1, source_target_pairs={{0,1},{1,0},{2,3},{3,2},{4,5},{5,4},{6,7},{7,6},{8,9},{9,8},{10,11... | collective-permute-start | bytes 897032 | tf_op jit(solution)/shard_map/ppermute | solution.py:523
  (2 other events, 13.2 us)

commit v2 on v1

--- a/solution.py
+++ b/solution.py
@@ -12,8 +12,6 @@
 BF16 = jnp.bfloat16
 F8 = jnp.float8_e4m3fn
 VMEM_BYTES = 40 << 20
-UNROLL_FORWARD = False
-UNROLL_BACKWARD = True
 GROUPS = ((0, 1), (2, 3), (4, 5), (6, 7), (8, 9), (10, 11), (12, 13))
 
 
@@ -113,14 +111,15 @@
 
 def pack_kernel(
     where_ref, feats_hbm, down_hbm, weight_hbm,
-    feats_send, table_send, feats_own, table_own, weight_ref, arrivals,
+    send_ref, feats_own, table_own, weight_ref, table_ref, arrivals,
 ):
+    channels, fine_rows = feats_own.shape
     copies = [
         pltpu.make_async_copy(source, target, arrivals.at[i])
         for i, (source, target) in enumerate(
             (
-                (feats_hbm.at[where_ref[4]], feats_send),
-                (down_hbm.at[where_ref[4]], table_send),
+                (down_hbm.at[where_ref[4]], table_ref),
+                (feats_hbm.at[where_ref[4]], send_ref.at[pl.ds(0, channels)]),
                 (down_hbm.at[where_ref[0]], table_own),
                 (feats_hbm.at[where_ref[0]], feats_own),
                 (weight_hbm, weight_ref),
@@ -129,7 +128,14 @@
     ]
     for copy in copies:
         copy.start()
-    for copy in copies:
+    copies[0].wait()
+    table = table_ref[...]
+    rows = [table // 16, table % 16]
+    rows.append(jnp.zeros((table.shape[0], fine_rows - 2 * table.shape[1]), jnp.int32))
+    rows = jnp.concatenate(rows, axis=1).astype(F32)
+    rows = jnp.concatenate([rows, jnp.zeros((16 - table.shape[0], fine_rows), F32)], axis=0)
+    send_ref[channels:] = rows.astype(BF16)
+    for copy in copies[1:]:
         copy.wait()
 
 
@@ -181,16 +187,20 @@
 
 
 def down_other_kernel(
-    where_ref, feats_ref, table_ref, weight_ref, own_hidden, own_sums, own_kids, own_which, own_table,
+    where_ref, got_ref, weight_ref, own_hidden, own_sums, own_kids, own_which, own_table,
     hidden_ref, sums_ref, kids_ref, which_ref, tables_ref,
     spread_ref, parent_ref,
 ):
+    offsets, coarse_rows = own_table.shape
+    channels = got_ref.shape[0] - 16
+    coded = got_ref[channels:].astype(F32)[:offsets, : 2 * coarse_rows]
+    table = (coded[:, :coarse_rows] * 16.0 + coded[:, coarse_rows:]).astype(jnp.int32)
     kids, hidden, count = down_rows(
-        table_ref[...], feats_ref, weight_ref, which_ref.at[1], spread_ref, parent_ref
+        table, got_ref.at[pl.ds(0, channels)], weight_ref, which_ref.at[1], spread_ref, parent_ref
     )
     kids_ref[1] = kids
     hidden_ref[1] = hidden
-    tables_ref[1] = table_ref[...]
+    tables_ref[1] = table
     for both, own in ((kids_ref, own_kids), (hidden_ref, own_hidden), (which_ref, own_which), (tables_ref, own_table)):
         both[0] = own[...]
     sums_ref[...] = own_sums[...]
@@ -252,7 +262,7 @@
         hidden = hidden.astype(F32)
         add_sums(sums_ref, col_sum(hidden), col_sum(hidden * hidden), count)
 
-    each_bucket(hidden_ref.shape[0], bucket, UNROLL_FORWARD)
+    each_bucket(hidden_ref.shape[0], bucket, True)
 
 
 def grad_kernel(where_ref, grad_ref, own_ref, send_ref):
@@ -332,7 +342,7 @@
         next_ref[b] = upstream
         add_sums(sums_ref, col_sum(upstream), col_sum(upstream * low_centred), own_count)
 
-    each_bucket(hidden_ref.shape[0], bucket, UNROLL_BACKWARD)
+    each_bucket(hidden_ref.shape[0], bucket, with_skip)
     put_halves(where_ref, grad_ref, keep_ref, send_ref)
 
 
@@ -463,13 +473,13 @@
             last, rest = divmod(outs[i].shape[0], wide)
             start = pl.multiple_of(block * wide, 16)
             copies.append((block < last, pltpu.make_async_copy(slot, outs[i].at[pl.ds(start, wide)], leaving.at[n, i])))
+            pl.when(copies[-1][0])(copies[-1][1].start)
             if rest:
                 part_copy = pltpu.make_async_copy(
                     slot.at[pl.ds(0, rest)], outs[i].at[pl.ds(last * wide, rest)], leaving.at[n, i]
                 )
                 copies.append((block == last, part_copy))
-    for when, copy in copies:
-        pl.when(when)(copy.start)
+                pl.when(copies[-1][0])(part_copy.start)
     return copies
 
 
@@ -580,12 +590,13 @@
 
     feats_hbm, down_hbm = in_hbm(voxel_feats), in_hbm(down_map)
     feats_one = shape((in_channels, fine_rows), BF16)
-    send_feats, send_table, own_feats, own_table, weight_down = run(
+    payload = shape((in_channels + 16, fine_rows), BF16)
+    send_feats, own_feats, own_table, weight_down = run(
         pack_kernel, where, [feats_hbm, down_hbm, in_hbm(flat_down)],
-        [feats_one, table, feats_one, table, shape((wide, channels), BF16)],
-        [pltpu.SemaphoreType.DMA((5,))], hbm_in=(0, 1, 2),
-    )
-    got_feats, got_table = cores(send_feats), cores(send_table)
+        [payload, feats_one, table, shape((wide, channels), BF16)],
+        [pltpu.VMEM((offsets, coarse_rows), jnp.int32), pltpu.SemaphoreType.DMA((5,))], hbm_in=(0, 1, 2),
+    )
+    got_feats = cores(send_feats)
     down_scratch = [pltpu.VMEM((wide, fine_rows), BF16), pltpu.VMEM((fine_rows, coarse_rows), BF16)]
     own_hidden, own_sums, own_kids, own_which, near_own, near_send = run(
         down_kernel, where,
@@ -599,7 +610,7 @@
     )
     hidden_zero, part_zero, kids, which, tables = run(
         down_other_kernel, where,
-        [got_feats, got_table, weight_down, own_hidden, own_sums, own_kids, own_which, own_table],
+        [got_feats, weight_down, own_hidden, own_sums, own_kids, own_which, own_table],
         [
             rows_f32, sums, shape((mine, wide, coarse_rows), BF16), shape((mine, 8, fine_rows), F32),
             shape((mine, offsets, coarse_rows), jnp.int32),
@@ -693,19 +704,20 @@
         functools.partial(spread_kernel, depths, sections), where, arrived + [keep_down, got_down],
         [half_shape(total + small)] * depths,
     )
+    depth_out, rows_zero = lax.optimization_barrier((depth_out, rows_zero))
     arrived = from_depths(depth_out)
+    input_own, input_send = run(
+        input_kernel, where, [rows_zero, which, tables, weight_down], [feats_one, feats_one],
+    )
+    arrived, input_own, input_send = lax.optimization_barrier((arrived, input_own, input_send))
     (summed,) = run(add_kernel, where, arrived, [half_shape(total + small)])
     arrived = from_depths([summed] * depths)
     (joined,) = run(
         functools.partial(join_kernel, small), where, arrived + [norm_rows, cores(norm_rows)],
         [half_shape(depths * (total + small) + 16)],
     )
-    joined, rows_zero = lax.optimization_barrier((joined, rows_zero))
     arrived = from_sections([joined] * sections)
     across = cores(joined)
-    input_own, input_send = run(
-        input_kernel, where, [rows_zero, which, tables, weight_down], [feats_one, feats_one],
-    )
     features, input_grad = run(
         place_outputs_kernel, where,
         [features_own, features_other, input_own, cores(input_send)],

time: 135 us -> 134 us (level)
    ppermute x44 -> x43, starting transfers between devices: 58.9 us -> 58.7 us  [swapped(): return lax.ppermute(value, axis, [(i, i ^ step) for i in range(count)])]
    ppermute x44 -> x43, waiting for transfers between devices: 21.6 us -> 21.7 us  [swapped(): return lax.ppermute(value, axis, [(i, i ^ step) for i in range(count)])]
  transfers between devices with their start and end apart: 44 -> 43, of which waited for: 15 -> 14; matrix products, arithmetic and copies ran while one was open for 0% -> 0% of each run, Pallas kernels for 29% -> 29%
where the time goes in v2:
time: 134 us
  starting transfers between devices  58.7 us (44%)
  Pallas kernels  52.6 us (39%)
  waiting for transfers between devices  21.7 us (16%)
    ppermute x43, starting transfers between devices, swapped(): return lax.ppermute(value, axis, [(i, i ^ step) for i in range(count)])  58.7 us
    pallas_call x19, Pallas kernels, run(): pl.pallas_call(kernel, in_specs=[pl.BlockSpec(memory_space=pltpu.SMEM)] +...  52.6 us
    ppermute x43, waiting for transfers between devices, swapped(): return lax.ppermute(value, axis, [(i, i ^ step) for i in range(count)])  21.7 us
  transfers between devices with their start and end apart: 43, of which 14 were waited for; matrix products, arithmetic and copies ran while one was open for 0% of the time, Pallas kernels for 29%

profile of v2, /device:TPU:1, one launch (start us, length us, event | category | flops | bytes accessed | tf_op | source)
XLA Modules:
  0.0 134.3 jit_solution(12556819000632920678)
XLA Ops:
  0.7 1.7 %shard_map.144 = (bf16[80,2048]{1,0:T(8,128)(2,1)S(1)}, bf16[64,2048]{1,0:T(8,128)(2,1)S(1)}, s32[8,512]{1,0:T(8,128)S(1)}, bf16[512,128]{1,0:T(8,128)(2,1)S(1)}) custom-call(s32[5]{0:T(128)S(1)} %stack.23.where_ref, bf16[8,64,2048]{2,1,0:T(8,128)(2,1)} %bitcast.13, s32[8,8,512]{2,1,0:T(8,128)} %down_hbm.1, bf16[512,128]{1,0:T(8,128)(2,1)} %bitcast.17), custom_call_target="tpu_custom_call" | custom-call | bytes 1 | tf_op jit(solution)/shard_map/pallas_call | solution.py:518
  2.6 2.7 %shard_map.145 = (f32[512,128]{1,0:T(8,128)S(1)}, f32[8,128]{1,0:T(8,128)S(1)}, bf16[512,512]{1,0:T(8,128)(2,1)S(1)}, f32[8,2048]{1,0:T(8,128)S(1)}, s32[27,512]{1,0:T(8,128)S(1)}, /*index=5*/s32[27,512]{1,0:T(8,128)S(1)}) custom-call(s32[5]{0:T(128)S(1)} %stack.23.where_ref, bf16[64,2048]{1,0:T(8,128)(2,1)S(1)} %get-tuple-element.87.feats_ref, ...), custom_call_target="tpu_custom_call" | custom-call | flops 2000000000 | bytes 1048576 | tf_op jit(solution)/shard_map/pallas_call | solution.py:518
  5.8 2.7 %shard_map.146 = (f32[2,512,128]{2,1,0:T(8,128)S(1)}, f32[8,128]{1,0:T(8,128)S(1)}, bf16[2,512,512]{2,1,0:T(8,128)(2,1)S(1)}, f32[2,8,2048]{2,1,0:T(8,128)S(1)}, s32[2,8,512]{2,1,0:T(8,128)S(1)}) custom-call(s32[5]{0:T(128)S(1)} %stack.23.where_ref, bf16[80,2048]{1,0:T(8,128)(2,1)S(1)} %collective-permute-done.got_ref, ...), custom_call_target="tpu_custom_call" | custom-call | flops 2000000000 | bytes 1048576 | tf_op jit(solution)/shard_map/pallas_call | solution.py:518
  8.5 4.4 %collective-permute-start.4 = (f32[8,128]{1,0:T(8,128)S(1)}, f32[8,128]{1,0:T(8,128)S(1)}, u32[]{:S(2)}, u32[]{:S(2)}) collective-permute-start(f32[8,128]{1,0:T(8,128)S(1)} %get-tuple-element.96.refs_0_.refs_16_), channel_id=1, source_target_pairs={{0,6},{1,7},{2,4},{3,5},{4,2},{5,3},{6,0},{7,1},{8,14},{9,15},{10,... | collective-permute-start | bytes 12296 | tf_op jit(solution)/shard_map/ppermute | solution.py:533
  13.9 2.4 %collective-permute-done.3.refs_2_.refs_18_ = f32[8,128]{1,0:T(8,128)S(1)} collective-permute-done((f32[8,128]{1,0:T(8,128)S(1)}, f32[8,128]{1,0:T(8,128)S(1)}, u32[]{:S(2)}, u32[]{:S(2)}) %collective-permute-start.3) | collective-permute-done | bytes 4128 | tf_op jit(solution)/shard_map/ppermute | solution.py:533
  16.3 6.7 %shard_map.148 = (bf16[2,512,128]{2,1,0:T(8,128)(2,1)S(1)}, f32[2,512,128]{2,1,0:T(8,128)S(1)}, f32[8,128]{1,0:T(8,128)S(1)}) custom-call(s32[5]{0:T(128)S(1)} %stack.23.where_ref, f32[2,512,128]{2,1,0:T(8,128)S(1)} %get-tuple-element.93.hidden_ref.refs_2_, s32[2,27,512]{2,1,0:T(8,128)S(1)} %shard_map.147.near_ref.refs_4_, ...), custom_call_target="tpu_custom_call" | custom-call | flops 14495514624 | bytes 1048576 | tf_op jit(solution)/shard_map/pallas_call | solution.py:518
  23.0 1.5 %collective-permute-start.7 = (f32[8,128]{1,0:T(8,128)S(1)}, f32[8,128]{1,0:T(8,128)S(1)}, u32[]{:S(2)}, u32[]{:S(2)}) collective-permute-start(f32[8,128]{1,0:T(8,128)S(1)} %get-tuple-element.98.refs_0_.refs_16_.refs_8_), channel_id=1, source_target_pairs={{0,6},{1,7},{2,4},{3,5},{4,2},{5,3},{6,0},{7,1},{8,14},{9,15},{10,... | collective-permute-start | bytes 12296 | tf_op jit(solution)/shard_map/ppermute | solution.py:533
  24.6 2.0 %collective-permute-start.5 = (f32[8,128]{1,0:T(8,128)S(1)}, f32[8,128]{1,0:T(8,128)S(1)}, u32[]{:S(2)}, u32[]{:S(2)}) collective-permute-start(f32[8,128]{1,0:T(8,128)S(1)} %get-tuple-element.98.refs_0_.refs_16_.refs_8_), channel_id=1, source_target_pairs={{0,2},{1,3},{2,0},{3,1},{4,6},{5,7},{6,4},{7,5},{8,10},{9,11},{10,... | collective-permute-start | bytes 12296 | tf_op jit(solution)/shard_map/ppermute | solution.py:533
  27.2 2.8 %collective-permute-start.8 = (bf16[512,128]{1,0:T(8,128)(2,1)S(1)}, bf16[512,128]{1,0:T(8,128)(2,1)S(1)}, u32[]{:S(2)}, u32[]{:S(2)}) collective-permute-start(bf16[512,128]{1,0:T(8,128)(2,1)S(1)} %get-tuple-element.102), channel_id=1, source_target_pairs={{0,1},{1,0},{2,3},{3,2},{4,5},{5,4},{6,7},{7,6},{8,9},{9,8},{10,11... | collective-permute-start | bytes 393224 | tf_op jit(solution)/shard_map/ppermute | solution.py:533
  30.0 6.9 %shard_map.149 = (bf16[2,512,128]{2,1,0:T(8,128)(2,1)S(1)}, bf16[2,512,128]{2,1,0:T(8,128)(2,1)S(1)}, f32[8,128]{1,0:T(8,128)S(1)}) custom-call(s32[5]{0:T(128)S(1)} %stack.23.where_ref, f32[2,512,128]{2,1,0:T(8,128)S(1)} %get-tuple-element.97.hidden_ref.refs_2_.refs_1_, s32[2,27,512]{2,1,0:T(8,128)S(1)} %shard_map.147.near_ref.refs_4_, ...), custom_call_target="tpu_custom_call" | custom-call | flops 14495514624 | bytes 1048576 | tf_op jit(solution)/shard_map/pallas_call | solution.py:518
  36.9 1.2 collective-permute-start.11
  38.1 2.4 %collective-permute-start.9 = (f32[8,128]{1,0:T(8,128)S(1)}, f32[8,128]{1,0:T(8,128)S(1)}, u32[]{:S(2)}, u32[]{:S(2)}) collective-permute-start(f32[8,128]{1,0:T(8,128)S(1)} %get-tuple-element.103.refs_0_.refs_8_), channel_id=1, source_target_pairs={{0,2},{1,3},{2,0},{3,1},{4,6},{5,7},{6,4},{7,5},{8,10},{9,11},{10,... | collective-permute-start | bytes 12296 | tf_op jit(solution)/shard_map/ppermute | solution.py:533
  41.5 1.2 shard_map.151
  42.7 2.1 %collective-permute-start.14 = (f32[8,128]{1,0:T(8,128)S(1)}, f32[8,128]{1,0:T(8,128)S(1)}, u32[]{:S(2)}, u32[]{:S(2)}) collective-permute-start(f32[8,128]{1,0:T(8,128)S(1)} %get-tuple-element.106.refs_12_), channel_id=1, source_target_pairs={{0,6},{1,7},{2,4},{3,5},{4,2},{5,3},{6,0},{7,1},{8,14},{9,15},{10,... | collective-permute-start | bytes 12296 | tf_op jit(solution)/shard_map/ppermute | solution.py:533
  45.4 0.9 collective-permute-start.12
  46.3 4.3 %collective-permute-start.16 = (bf16[512,128]{1,0:T(8,128)(2,1)S(1)}, bf16[512,128]{1,0:T(8,128)(2,1)S(1)}, u32[]{:S(2)}, u32[]{:S(2)}) collective-permute-start(bf16[512,128]{1,0:T(8,128)(2,1)S(1)} %get-tuple-element.109), channel_id=1, source_target_pairs={{0,1},{1,0},{2,3},{3,2},{4,5},{5,4},{6,7},{7,6},{8,9},{9,8},{10,11... | collective-permute-start | bytes 393224 | tf_op jit(solution)/shard_map/ppermute | solution.py:533
  50.7 8.8 %shard_map.152 = (f32[2,512,128]{2,1,0:T(8,128)S(1)}, f32[8,128]{1,0:T(8,128)S(1)}, bf16[1792,128]{1,0:T(8,128)(2,1)S(1)}, bf16[1792,128]{1,0:T(8,128)(2,1)S(1)}) custom-call(s32[5]{0:T(128)S(1)} %stack.23.where_ref, f32[2,512,128]{2,1,0:T(8,128)S(1)} %get-tuple-element.104.refs_0_.refs_20_, bf16[2,512,128]{2,1,0:T(8,128)(2,1)S(1)} %get-tuple-element.99.hidden_ref.refs_1_, ...), custom_call_target="tpu_custom_call" | custom-call | flops 14495514624 | bytes 1048576 | tf_op jit(solution)/shard_map/pallas_call | solution.py:518
  59.5 1.2 collective-permute-start.19
  60.7 2.4 %collective-permute-start.17 = (f32[8,128]{1,0:T(8,128)S(1)}, f32[8,128]{1,0:T(8,128)S(1)}, u32[]{:S(2)}, u32[]{:S(2)}) collective-permute-start(f32[8,128]{1,0:T(8,128)S(1)} %get-tuple-element.112.refs_12_.refs_8_), channel_id=1, source_target_pairs={{0,2},{1,3},{2,0},{3,1},{4,6},{5,7},{6,4},{7,5},{8,10},{9,11},{10,... | collective-permute-start | bytes 12296 | tf_op jit(solution)/shard_map/ppermute | solution.py:533
  63.1 2.4 %collective-permute-start.15 = (bf16[1792,128]{1,0:T(8,128)(2,1)S(1)}, bf16[1792,128]{1,0:T(8,128)(2,1)S(1)}, u32[]{:S(2)}, u32[]{:S(2)}) collective-permute-start(bf16[1792,128]{1,0:T(8,128)(2,1)S(1)} %get-tuple-element.108), channel_id=1, source_target_pairs={{0,1},{1,0},{2,3},{3,2},{4,5},{5,4},{6,7},{7,6},{8,9},{9,8},{10,11... | collective-permute-start | bytes 1376264 | tf_op jit(solution)/shard_map/ppermute | solution.py:533
  65.5 8.3 %shard_map.153 = (f32[2,512,128]{2,1,0:T(8,128)S(1)}, f32[8,128]{1,0:T(8,128)S(1)}, bf16[1792,128]{1,0:T(8,128)(2,1)S(1)}, bf16[1792,128]{1,0:T(8,128)(2,1)S(1)}) custom-call(s32[5]{0:T(128)S(1)} %stack.23.where_ref, f32[2,512,128]{2,1,0:T(8,128)S(1)} %get-tuple-element.111.refs_0_, f32[2,512,128]{2,1,0:T(8,128)S(1)} %get-tuple-element.97.hidden_ref.refs_2_.refs_1_, ...), custom_call_target="tpu_custom_call" | custom-call | flops 14495514624 | bytes 1048576 | tf_op jit(solution)/shard_map/pallas_call | solution.py:518
  73.8 2.7 %collective-permute-start.20 = (bf16[1792,128]{1,0:T(8,128)(2,1)S(1)}, bf16[1792,128]{1,0:T(8,128)(2,1)S(1)}, u32[]{:S(2)}, u32[]{:S(2)}) collective-permute-start(bf16[1792,128]{1,0:T(8,128)(2,1)S(1)} %get-tuple-element.114), channel_id=1, source_target_pairs={{0,1},{1,0},{2,3},{3,2},{4,5},{5,4},{6,7},{7,6},{8,9},{9,8},{10,11... | collective-permute-start | bytes 1376264 | tf_op jit(solution)/shard_map/ppermute | solution.py:533
  76.5 1.4 %collective-permute-done.20.refs_3_ = bf16[1792,128]{1,0:T(8,128)(2,1)S(1)} collective-permute-done((bf16[1792,128]{1,0:T(8,128)(2,1)S(1)}, bf16[1792,128]{1,0:T(8,128)(2,1)S(1)}, u32[]{:S(2)}, u32[]{:S(2)}) %collective-permute-start.20) | collective-permute-done | bytes 458784 | tf_op jit(solution)/shard_map/ppermute | solution.py:533
  78.7 2.2 %collective-permute-start.21 = (bf16[896,128]{1,0:T(8,128)(2,1)S(1)}, bf16[896,128]{1,0:T(8,128)(2,1)S(1)}, u32[]{:S(2)}, u32[]{:S(2)}) collective-permute-start(bf16[896,128]{1,0:T(8,128)(2,1)S(1)} %get-tuple-element.116), channel_id=1, source_target_pairs={{0,24},{8,16},{16,8},{24,0},{1,25},{9,17},{17,9},{25,1},{2,26},{10... | collective-permute-start | bytes 688136 | tf_op jit(solution)/shard_map/ppermute | solution.py:533
  81.4 1.1 collective-permute-start.26
  83.3 2.5 %collective-permute-done.26.refs_7_ = f32[8,128]{1,0:T(8,128)S(1)} collective-permute-done((f32[8,128]{1,0:T(8,128)S(1)}, f32[8,128]{1,0:T(8,128)S(1)}, u32[]{:S(2)}, u32[]{:S(2)}) %collective-permute-start.26) | collective-permute-done | bytes 4128 | tf_op jit(solution)/shard_map/ppermute | solution.py:533
  86.3 2.2 %collective-permute-done.24.refs_5_ = f32[8,128]{1,0:T(8,128)S(1)} collective-permute-done((f32[8,128]{1,0:T(8,128)S(1)}, f32[8,128]{1,0:T(8,128)S(1)}, u32[]{:S(2)}, u32[]{:S(2)}) %collective-permute-start.24) | collective-permute-done | bytes 4128 | tf_op jit(solution)/shard_map/ppermute | solution.py:533
  88.5 1.1 shard_map.155
  89.6 3.3 %collective-permute-start.27 = (bf16[256,128]{1,0:T(8,128)(2,1)S(1)}, bf16[256,128]{1,0:T(8,128)(2,1)S(1)}, u32[]{:S(2)}, u32[]{:S(2)}) collective-permute-start(bf16[256,128]{1,0:T(8,128)(2,1)S(1)} %get-tuple-element.123), channel_id=1, source_target_pairs={{0,1},{1,0},{2,3},{3,2},{4,5},{5,4},{6,7},{7,6},{8,9},{9,8},{10,11... | collective-permute-start | bytes 196616 | tf_op jit(solution)/shard_map/ppermute | solution.py:533
  92.9 0.9 collective-permute-done.27.refs_5_
  94.5 1.2 collective-permute-start.28
  95.7 2.4 %collective-permute-start.30 = (bf16[288,128]{1,0:T(8,128)(2,1)S(1)}, bf16[288,128]{1,0:T(8,128)(2,1)S(1)}, u32[]{:S(2)}, u32[]{:S(2)}) collective-permute-start(bf16[288,128]{1,0:T(8,128)(2,1)S(1)} %get-tuple-element.132), channel_id=1, source_target_pairs={{0,2},{1,3},{2,0},{3,1},{4,6},{5,7},{6,4},{7,5},{8,10},{9,11},{10,... | collective-permute-start | bytes 221192 | tf_op jit(solution)/shard_map/ppermute | solution.py:533
  98.1 3.2 %shard_map.157 = (bf16[64,2048]{1,0:T(8,128)(2,1)S(1)}, bf16[64,2048]{1,0:T(8,128)(2,1)S(1)}) custom-call(s32[5]{0:T(128)S(1)} %stack.23.where_ref, bf16[2,512,128]{2,1,0:T(8,128)(2,1)S(1)} %get-tuple-element.133.rows_ref, f32[2,8,2048]{2,1,0:T(8,128)S(1)} %get-tuple-element.134.which_ref, s32[2,8,512]{2,1,0:T(8,128)S(1)} %get-tuple-element.135.tables_ref, ...), custom_call_target="tpu_custom_call" | custom-call | bytes 1 | tf_op jit(solution)/shard_map/pallas_call | solution.py:518
  101.3 2.4 %collective-permute-done.29.refs_2_ = bf16[288,128]{1,0:T(8,128)(2,1)S(1)} collective-permute-done((bf16[288,128]{1,0:T(8,128)(2,1)S(1)}, bf16[288,128]{1,0:T(8,128)(2,1)S(1)}, u32[]{:S(2)}, u32[]{:S(2)}) %collective-permute-start.29) | collective-permute-done | bytes 73760 | tf_op jit(solution)/shard_map/ppermute | solution.py:533
  104.3 1.4 %collective-permute-start.32 = (bf16[288,128]{1,0:T(8,128)(2,1)S(1)}, bf16[288,128]{1,0:T(8,128)(2,1)S(1)}, u32[]{:S(2)}, u32[]{:S(2)}) collective-permute-start(bf16[288,128]{1,0:T(8,128)(2,1)S(1)} %shard_map.158.refs_0_), channel_id=1, source_target_pairs={{0,4},{1,5},{2,6},{3,7},{4,0},{5,1},{6,2},{7,3},{8,12},{9,13},{10,... | collective-permute-start | bytes 221192 | tf_op jit(solution)/shard_map/ppermute | solution.py:533
  105.8 2.1 %collective-permute-start.31 = (bf16[288,128]{1,0:T(8,128)(2,1)S(1)}, bf16[288,128]{1,0:T(8,128)(2,1)S(1)}, u32[]{:S(2)}, u32[]{:S(2)}) collective-permute-start(bf16[288,128]{1,0:T(8,128)(2,1)S(1)} %shard_map.158.refs_0_), channel_id=1, source_target_pairs={{0,6},{1,7},{2,4},{3,5},{4,2},{5,3},{6,0},{7,1},{8,14},{9,15},{10,... | collective-permute-start | bytes 221192 | tf_op jit(solution)/shard_map/ppermute | solution.py:533
  107.9 1.3 collective-permute-start.34
  109.2 0.8 collective-permute-done.34.refs_5_
  110.0 1.4 %collective-permute-done.31.refs_1_ = bf16[288,128]{1,0:T(8,128)(2,1)S(1)} collective-permute-done((bf16[288,128]{1,0:T(8,128)(2,1)S(1)}, bf16[288,128]{1,0:T(8,128)(2,1)S(1)}, u32[]{:S(2)}, u32[]{:S(2)}) %collective-permute-start.31) | collective-permute-done | bytes 73760 | tf_op jit(solution)/shard_map/ppermute | solution.py:533
  112.0 1.3 collective-permute-start.37
  113.3 1.2 collective-permute-start.36
  114.7 3.3 %collective-permute-start.38 = (bf16[64,2048]{1,0:T(8,128)(2,1)S(1)}, bf16[64,2048]{1,0:T(8,128)(2,1)S(1)}, u32[]{:S(2)}, u32[]{:S(2)}) collective-permute-start(bf16[64,2048]{1,0:T(8,128)(2,1)S(1)} %get-tuple-element.146), channel_id=1, source_target_pairs={{0,1},{1,0},{2,3},{3,2},{4,5},{5,4},{6,7},{7,6},{8,9},{9,8},{10,11... | collective-permute-start | bytes 786440 | tf_op jit(solution)/shard_map/ppermute | solution.py:533
  118.1 1.2 collective-permute-done.38.other_input
  119.2 1.5 %shard_map.160 = (bf16[2,512,128]{2,1,0:T(8,128)(2,1)}, bf16[2,64,2048]{2,1,0:T(8,128)(2,1)}) custom-call(s32[5]{0:T(128)S(1)} %stack.23.where_ref, bf16[512,128]{1,0:T(8,128)(2,1)S(1)} %get-tuple-element.143.own_features, bf16[512,128]{1,0:T(8,128)(2,1)S(1)} %collective-permute-done.16.other_features, bf16[64,2048]{1,0:T(8,128)(2,1)S(1)} %get-tuple-element.145.own_input, ...), custom_call_target="tpu_custom_call" | custom-call | bytes 1 | tf_op jit(solution)/shard_map/pallas_call | solution.py:518
  120.7 4.8 %collective-permute-done.35.refs_1_ = bf16[1168,128]{1,0:T(8,128)(2,1)S(1)} collective-permute-done((bf16[1168,128]{1,0:T(8,128)(2,1)S(1)}, bf16[1168,128]{1,0:T(8,128)(2,1)S(1)}, u32[]{:S(2)}, u32[]{:S(2)}) %collective-permute-start.35) | collective-permute-done | bytes 299040 | tf_op jit(solution)/shard_map/ppermute | solution.py:533
  125.6 3.7 %collective-permute-start.40 = (bf16[1168,128]{1,0:T(8,128)(2,1)S(1)}, bf16[1168,128]{1,0:T(8,128)(2,1)S(1)}, u32[]{:S(2)}, u32[]{:S(2)}) collective-permute-start(bf16[1168,128]{1,0:T(8,128)(2,1)S(1)} %collective-permute-done.35.refs_1_), channel_id=1, source_target_pairs={{0,1},{1,0},{2,3},{3,2},{4,5},{5,4},{6,7},{7,6},{8,9},{9,8},{10,11... | collective-permute-start | bytes 897032 | tf_op jit(solution)/shard_map/ppermute | solution.py:533
  129.7 2.4 %shard_map.161 = (f32[3456,128]{1,0:T(8,128)}, f32[3456,128]{1,0:T(8,128)}, f32[512,128]{1,0:T(8,128)}, f32[3,128]{1,0:T(4,128)}, f32[3,128]{1,0:T(4,128)}) custom-call(s32[5]{0:T(128)S(1)} %stack.23.where_ref, bf16[1168,128]{1,0:T(8,128)(2,1)S(1)} %shard_map.159.refs_0_, bf16[1168,128]{1,0:T(8,128)(2,1)S(1)} %collective-permute-done.35.refs_1_, ...), custom_call_target="tpu_custom_call" | custom-call | flops 1000000000 | bytes 1048576 | tf_op jit(solution)/shard_map/pallas_call | solution.py:518
  132.2 1.9 %shard_map.162 = (f32[3456,128]{1,0:T(8,128)}, f32[3456,128]{1,0:T(8,128)}, f32[512,128]{1,0:T(8,128)}) custom-call(s32[5]{0:T(128)S(1)} %stack.23.where_ref, bf16[1168,128]{1,0:T(8,128)(2,1)S(1)} %collective-permute-done.39.refs_0_, ...), custom_call_target="tpu_custom_call", output_to_operand_aliasing={{0}: (5, {}), {1}: (6, {}), {2}: (7, {})} | custom-call | flops 1000000000 | bytes 1048576 | tf_op jit(solution)/shard_map/pallas_call | solution.py:518
  (70 shorter events, 9.1 us)
Async XLA Ops:
  2.4 3.3 %collective-permute-start = (bf16[80,2048]{1,0:T(8,128)(2,1)S(1)}, bf16[80,2048]{1,0:T(8,128)(2,1)S(1)}, u32[]{:S(2)}, u32[]{:S(2)}) collective-permute-start(bf16[80,2048]{1,0:T(8,128)(2,1)S(1)} %get-tuple-element.85), channel_id=1, source_target_pairs={{0,1},{1,0},{2,3},{3,2},{4,5},{5,4},{6,7},{7,6},{8,9},{9,8},{10,11... | collective-permute-start | bytes 983048 | tf_op jit(solution)/shard_map/ppermute | solution.py:533
  5.2 8.0 %collective-permute-start.1 = (s32[27,512]{1,0:T(8,128)S(1)}, s32[27,512]{1,0:T(8,128)S(1)}, u32[]{:S(2)}, u32[]{:S(2)}) collective-permute-start(s32[27,512]{1,0:T(8,128)S(1)} %get-tuple-element.95), channel_id=1, source_target_pairs={{0,1},{1,0},{2,3},{3,2},{4,5},{5,4},{6,7},{7,6},{8,9},{9,8},{10,11... | collective-permute-start | bytes 165896 | tf_op jit(solution)/shard_map/ppermute | solution.py:533
  5.8 10.5 %copy-start.2 = (bf16[27,128,128]{2,1,0:T(8,128)(2,1)S(1)}, bf16[27,128,128]{2,1,0:T(8,128)(2,1)}, u32[]{:S(2)}) copy-start(bf16[27,128,128]{2,1,0:T(8,128)(2,1)} %refs_5_.3) | copy-start | bytes 2654212
  5.8 10.5 %copy-start.4 = (f32[3,128]{1,0:T(4,128)S(1)}, f32[3,128]{1,0:T(4,128)}, u32[]{:S(2)}) copy-start(f32[3,128]{1,0:T(4,128)} %refs_7_.3) | copy-start | bytes 4612
  5.8 10.5 %copy-start.5 = (f32[3,128]{1,0:T(4,128)S(1)}, f32[3,128]{1,0:T(4,128)}, u32[]{:S(2)}) copy-start(f32[3,128]{1,0:T(4,128)} %scale_ref.7) | copy-start | bytes 4612
  8.5 5.4 %collective-permute-start.4 = (f32[8,128]{1,0:T(8,128)S(1)}, f32[8,128]{1,0:T(8,128)S(1)}, u32[]{:S(2)}, u32[]{:S(2)}) collective-permute-start(f32[8,128]{1,0:T(8,128)S(1)} %get-tuple-element.96.refs_0_.refs_16_), channel_id=1, source_target_pairs={{0,6},{1,7},{2,4},{3,5},{4,2},{5,3},{6,0},{7,1},{8,14},{9,15},{10,... | collective-permute-start | bytes 12296 | tf_op jit(solution)/shard_map/ppermute | solution.py:533
  12.9 3.4 %collective-permute-start.3 = (f32[8,128]{1,0:T(8,128)S(1)}, f32[8,128]{1,0:T(8,128)S(1)}, u32[]{:S(2)}, u32[]{:S(2)}) collective-permute-start(f32[8,128]{1,0:T(8,128)S(1)} %get-tuple-element.96.refs_0_.refs_16_), channel_id=1, source_target_pairs={{0,4},{1,5},{2,6},{3,7},{4,0},{5,1},{6,2},{7,3},{8,12},{9,13},{10,... | collective-permute-start | bytes 12296 | tf_op jit(solution)/shard_map/ppermute | solution.py:533
  12.9 3.4 %collective-permute-start.2 = (f32[8,128]{1,0:T(8,128)S(1)}, f32[8,128]{1,0:T(8,128)S(1)}, u32[]{:S(2)}, u32[]{:S(2)}) collective-permute-start(f32[8,128]{1,0:T(8,128)S(1)} %get-tuple-element.96.refs_0_.refs_16_), channel_id=1, source_target_pairs={{0,2},{1,3},{2,0},{3,1},{4,6},{5,7},{6,4},{7,5},{8,10},{9,11},{10,... | collective-permute-start | bytes 12296 | tf_op jit(solution)/shard_map/ppermute | solution.py:533
  16.3 10.3 %copy-start = (bf16[8,512,128]{2,1,0:T(8,128)(2,1)S(1)}, bf16[8,512,128]{2,1,0:T(8,128)(2,1)}, u32[]{:S(2)}) copy-start(bf16[8,512,128]{2,1,0:T(8,128)(2,1)} %grad_ref.1) | copy-start | bytes 3145732
  16.3 13.7 %copy-start.1 = (bf16[27,128,128]{2,1,0:T(8,128)(2,1)S(1)}, bf16[27,128,128]{2,1,0:T(8,128)(2,1)}, u32[]{:S(2)}) copy-start(bf16[27,128,128]{2,1,0:T(8,128)(2,1)} %refs_5_.2) | copy-start | bytes 2654212
  23.0 7.0 %collective-permute-start.7 = (f32[8,128]{1,0:T(8,128)S(1)}, f32[8,128]{1,0:T(8,128)S(1)}, u32[]{:S(2)}, u32[]{:S(2)}) collective-permute-start(f32[8,128]{1,0:T(8,128)S(1)} %get-tuple-element.98.refs_0_.refs_16_.refs_8_), channel_id=1, source_target_pairs={{0,6},{1,7},{2,4},{3,5},{4,2},{5,3},{6,0},{7,1},{8,14},{9,15},{10,... | collective-permute-start | bytes 12296 | tf_op jit(solution)/shard_map/ppermute | solution.py:533
  24.5 5.4 %collective-permute-start.6 = (f32[8,128]{1,0:T(8,128)S(1)}, f32[8,128]{1,0:T(8,128)S(1)}, u32[]{:S(2)}, u32[]{:S(2)}) collective-permute-start(f32[8,128]{1,0:T(8,128)S(1)} %get-tuple-element.98.refs_0_.refs_16_.refs_8_), channel_id=1, source_target_pairs={{0,4},{1,5},{2,6},{3,7},{4,0},{5,1},{6,2},{7,3},{8,12},{9,13},{10,... | collective-permute-start | bytes 12296 | tf_op jit(solution)/shard_map/ppermute | solution.py:533
  24.6 5.4 %collective-permute-start.5 = (f32[8,128]{1,0:T(8,128)S(1)}, f32[8,128]{1,0:T(8,128)S(1)}, u32[]{:S(2)}, u32[]{:S(2)}) collective-permute-start(f32[8,128]{1,0:T(8,128)S(1)} %get-tuple-element.98.refs_0_.refs_16_.refs_8_), channel_id=1, source_target_pairs={{0,2},{1,3},{2,0},{3,1},{4,6},{5,7},{6,4},{7,5},{8,10},{9,11},{10,... | collective-permute-start | bytes 12296 | tf_op jit(solution)/shard_map/ppermute | solution.py:533
  27.2 13.3 %collective-permute-start.8 = (bf16[512,128]{1,0:T(8,128)(2,1)S(1)}, bf16[512,128]{1,0:T(8,128)(2,1)S(1)}, u32[]{:S(2)}, u32[]{:S(2)}) collective-permute-start(bf16[512,128]{1,0:T(8,128)(2,1)S(1)} %get-tuple-element.102), channel_id=1, source_target_pairs={{0,1},{1,0},{2,3},{3,2},{4,5},{5,4},{6,7},{7,6},{8,9},{9,8},{10,11... | collective-permute-start | bytes 393224 | tf_op jit(solution)/shard_map/ppermute | solution.py:533
  36.9 4.3 %collective-permute-start.11 = (f32[8,128]{1,0:T(8,128)S(1)}, f32[8,128]{1,0:T(8,128)S(1)}, u32[]{:S(2)}, u32[]{:S(2)}) collective-permute-start(f32[8,128]{1,0:T(8,128)S(1)} %get-tuple-element.103.refs_0_.refs_8_), channel_id=1, source_target_pairs={{0,6},{1,7},{2,4},{3,5},{4,2},{5,3},{6,0},{7,1},{8,14},{9,15},{10,... | collective-permute-start | bytes 12296 | tf_op jit(solution)/shard_map/ppermute | solution.py:533
  38.1 3.4 %collective-permute-start.10 = (f32[8,128]{1,0:T(8,128)S(1)}, f32[8,128]{1,0:T(8,128)S(1)}, u32[]{:S(2)}, u32[]{:S(2)}) collective-permute-start(f32[8,128]{1,0:T(8,128)S(1)} %get-tuple-element.103.refs_0_.refs_8_), channel_id=1, source_target_pairs={{0,4},{1,5},{2,6},{3,7},{4,0},{5,1},{6,2},{7,3},{8,12},{9,13},{10,... | collective-permute-start | bytes 12296 | tf_op jit(solution)/shard_map/ppermute | solution.py:533
  38.1 3.4 %collective-permute-start.9 = (f32[8,128]{1,0:T(8,128)S(1)}, f32[8,128]{1,0:T(8,128)S(1)}, u32[]{:S(2)}, u32[]{:S(2)}) collective-permute-start(f32[8,128]{1,0:T(8,128)S(1)} %get-tuple-element.103.refs_0_.refs_8_), channel_id=1, source_target_pairs={{0,2},{1,3},{2,0},{3,1},{4,6},{5,7},{6,4},{7,5},{8,10},{9,11},{10,... | collective-permute-start | bytes 12296 | tf_op jit(solution)/shard_map/ppermute | solution.py:533
  42.7 7.9 %collective-permute-start.14 = (f32[8,128]{1,0:T(8,128)S(1)}, f32[8,128]{1,0:T(8,128)S(1)}, u32[]{:S(2)}, u32[]{:S(2)}) collective-permute-start(f32[8,128]{1,0:T(8,128)S(1)} %get-tuple-element.106.refs_12_), channel_id=1, source_target_pairs={{0,6},{1,7},{2,4},{3,5},{4,2},{5,3},{6,0},{7,1},{8,14},{9,15},{10,... | collective-permute-start | bytes 12296 | tf_op jit(solution)/shard_map/ppermute | solution.py:533
  44.8 5.8 %collective-permute-start.13 = (f32[8,128]{1,0:T(8,128)S(1)}, f32[8,128]{1,0:T(8,128)S(1)}, u32[]{:S(2)}, u32[]{:S(2)}) collective-permute-start(f32[8,128]{1,0:T(8,128)S(1)} %get-tuple-element.106.refs_12_), channel_id=1, source_target_pairs={{0,4},{1,5},{2,6},{3,7},{4,0},{5,1},{6,2},{7,3},{8,12},{9,13},{10,... | collective-permute-start | bytes 12296 | tf_op jit(solution)/shard_map/ppermute | solution.py:533
  45.4 5.3 %collective-permute-start.12 = (f32[8,128]{1,0:T(8,128)S(1)}, f32[8,128]{1,0:T(8,128)S(1)}, u32[]{:S(2)}, u32[]{:S(2)}) collective-permute-start(f32[8,128]{1,0:T(8,128)S(1)} %get-tuple-element.106.refs_12_), channel_id=1, source_target_pairs={{0,2},{1,3},{2,0},{3,1},{4,6},{5,7},{6,4},{7,5},{8,10},{9,11},{10,... | collective-permute-start | bytes 12296 | tf_op jit(solution)/shard_map/ppermute | solution.py:533
  46.3 19.2 %collective-permute-start.16 = (bf16[512,128]{1,0:T(8,128)(2,1)S(1)}, bf16[512,128]{1,0:T(8,128)(2,1)S(1)}, u32[]{:S(2)}, u32[]{:S(2)}) collective-permute-start(bf16[512,128]{1,0:T(8,128)(2,1)S(1)} %get-tuple-element.109), channel_id=1, source_target_pairs={{0,1},{1,0},{2,3},{3,2},{4,5},{5,4},{6,7},{7,6},{8,9},{9,8},{10,11... | collective-permute-start | bytes 393224 | tf_op jit(solution)/shard_map/ppermute | solution.py:533
  59.5 6.0 %collective-permute-start.19 = (f32[8,128]{1,0:T(8,128)S(1)}, f32[8,128]{1,0:T(8,128)S(1)}, u32[]{:S(2)}, u32[]{:S(2)}) collective-permute-start(f32[8,128]{1,0:T(8,128)S(1)} %get-tuple-element.112.refs_12_.refs_8_), channel_id=1, source_target_pairs={{0,6},{1,7},{2,4},{3,5},{4,2},{5,3},{6,0},{7,1},{8,14},{9,15},{10,... | collective-permute-start | bytes 12296 | tf_op jit(solution)/shard_map/ppermute | solution.py:533
  60.7 4.8 %collective-permute-start.18 = (f32[8,128]{1,0:T(8,128)S(1)}, f32[8,128]{1,0:T(8,128)S(1)}, u32[]{:S(2)}, u32[]{:S(2)}) collective-permute-start(f32[8,128]{1,0:T(8,128)S(1)} %get-tuple-element.112.refs_12_.refs_8_), channel_id=1, source_target_pairs={{0,4},{1,5},{2,6},{3,7},{4,0},{5,1},{6,2},{7,3},{8,12},{9,13},{10,... | collective-permute-start | bytes 12296 | tf_op jit(solution)/shard_map/ppermute | solution.py:533
  60.7 4.8 %collective-permute-start.17 = (f32[8,128]{1,0:T(8,128)S(1)}, f32[8,128]{1,0:T(8,128)S(1)}, u32[]{:S(2)}, u32[]{:S(2)}) collective-permute-start(f32[8,128]{1,0:T(8,128)S(1)} %get-tuple-element.112.refs_12_.refs_8_), channel_id=1, source_target_pairs={{0,2},{1,3},{2,0},{3,1},{4,6},{5,7},{6,4},{7,5},{8,10},{9,11},{10,... | collective-permute-start | bytes 12296 | tf_op jit(solution)/shard_map/ppermute | solution.py:533
  63.1 13.4 %collective-permute-start.15 = (bf16[1792,128]{1,0:T(8,128)(2,1)S(1)}, bf16[1792,128]{1,0:T(8,128)(2,1)S(1)}, u32[]{:S(2)}, u32[]{:S(2)}) collective-permute-start(bf16[1792,128]{1,0:T(8,128)(2,1)S(1)} %get-tuple-element.108), channel_id=1, source_target_pairs={{0,1},{1,0},{2,3},{3,2},{4,5},{5,4},{6,7},{7,6},{8,9},{9,8},{10,11... | collective-permute-start | bytes 1376264 | tf_op jit(solution)/shard_map/ppermute | solution.py:533
  73.8 4.2 %collective-permute-start.20 = (bf16[1792,128]{1,0:T(8,128)(2,1)S(1)}, bf16[1792,128]{1,0:T(8,128)(2,1)S(1)}, u32[]{:S(2)}, u32[]{:S(2)}) collective-permute-start(bf16[1792,128]{1,0:T(8,128)(2,1)S(1)} %get-tuple-element.114), channel_id=1, source_target_pairs={{0,1},{1,0},{2,3},{3,2},{4,5},{5,4},{6,7},{7,6},{8,9},{9,8},{10,11... | collective-permute-start | bytes 1376264 | tf_op jit(solution)/shard_map/ppermute | solution.py:533
  78.7 15.0 %collective-permute-start.21 = (bf16[896,128]{1,0:T(8,128)(2,1)S(1)}, bf16[896,128]{1,0:T(8,128)(2,1)S(1)}, u32[]{:S(2)}, u32[]{:S(2)}) collective-permute-start(bf16[896,128]{1,0:T(8,128)(2,1)S(1)} %get-tuple-element.116), channel_id=1, source_target_pairs={{0,24},{8,16},{16,8},{24,0},{1,25},{9,17},{17,9},{25,1},{2,26},{10... | collective-permute-start | bytes 688136 | tf_op jit(solution)/shard_map/ppermute | solution.py:533
  81.0 12.8 %collective-permute-start.22 = (bf16[896,128]{1,0:T(8,128)(2,1)S(1)}, bf16[896,128]{1,0:T(8,128)(2,1)S(1)}, u32[]{:S(2)}, u32[]{:S(2)}) collective-permute-start(bf16[896,128]{1,0:T(8,128)(2,1)S(1)} %get-tuple-element.117), channel_id=1, source_target_pairs={{0,16},{8,24},{16,0},{24,8},{1,17},{9,25},{17,1},{25,9},{2,18},{10... | collective-permute-start | bytes 688136 | tf_op jit(solution)/shard_map/ppermute | solution.py:533
  81.2 12.6 %collective-permute-start.23 = (bf16[896,128]{1,0:T(8,128)(2,1)S(1)}, bf16[896,128]{1,0:T(8,128)(2,1)S(1)}, u32[]{:S(2)}, u32[]{:S(2)}) collective-permute-start(bf16[896,128]{1,0:T(8,128)(2,1)S(1)} %get-tuple-element.118), channel_id=1, source_target_pairs={{0,8},{8,0},{16,24},{24,16},{1,9},{9,1},{17,25},{25,17},{2,10},{10... | collective-permute-start | bytes 688136 | tf_op jit(solution)/shard_map/ppermute | solution.py:533
  81.4 4.3 %collective-permute-start.26 = (f32[8,128]{1,0:T(8,128)S(1)}, f32[8,128]{1,0:T(8,128)S(1)}, u32[]{:S(2)}, u32[]{:S(2)}) collective-permute-start(f32[8,128]{1,0:T(8,128)S(1)} %get-tuple-element.121.refs_4_), channel_id=1, source_target_pairs={{0,6},{1,7},{2,4},{3,5},{4,2},{5,3},{6,0},{7,1},{8,14},{9,15},{10,... | collective-permute-start | bytes 12296 | tf_op jit(solution)/shard_map/ppermute | solution.py:533
  82.6 3.7 %collective-permute-start.25 = (f32[8,128]{1,0:T(8,128)S(1)}, f32[8,128]{1,0:T(8,128)S(1)}, u32[]{:S(2)}, u32[]{:S(2)}) collective-permute-start(f32[8,128]{1,0:T(8,128)S(1)} %get-tuple-element.121.refs_4_), channel_id=1, source_target_pairs={{0,4},{1,5},{2,6},{3,7},{4,0},{5,1},{6,2},{7,3},{8,12},{9,13},{10,... | collective-permute-start | bytes 12296 | tf_op jit(solution)/shard_map/ppermute | solution.py:533
  85.7 2.8 %collective-permute-start.24 = (f32[8,128]{1,0:T(8,128)S(1)}, f32[8,128]{1,0:T(8,128)S(1)}, u32[]{:S(2)}, u32[]{:S(2)}) collective-permute-start(f32[8,128]{1,0:T(8,128)S(1)} %get-tuple-element.121.refs_4_), channel_id=1, source_target_pairs={{0,2},{1,3},{2,0},{3,1},{4,6},{5,7},{6,4},{7,5},{8,10},{9,11},{10,... | collective-permute-start | bytes 12296 | tf_op jit(solution)/shard_map/ppermute | solution.py:533
  89.6 4.2 %collective-permute-start.27 = (bf16[256,128]{1,0:T(8,128)(2,1)S(1)}, bf16[256,128]{1,0:T(8,128)(2,1)S(1)}, u32[]{:S(2)}, u32[]{:S(2)}) collective-permute-start(bf16[256,128]{1,0:T(8,128)(2,1)S(1)} %get-tuple-element.123), channel_id=1, source_target_pairs={{0,1},{1,0},{2,3},{3,2},{4,5},{5,4},{6,7},{7,6},{8,9},{9,8},{10,11... | collective-permute-start | bytes 196616 | tf_op jit(solution)/shard_map/ppermute | solution.py:533
  94.5 6.8 %collective-permute-start.28 = (bf16[288,128]{1,0:T(8,128)(2,1)S(1)}, bf16[288,128]{1,0:T(8,128)(2,1)S(1)}, u32[]{:S(2)}, u32[]{:S(2)}) collective-permute-start(bf16[288,128]{1,0:T(8,128)(2,1)S(1)} %get-tuple-element.130), channel_id=1, source_target_pairs={{0,6},{1,7},{2,4},{3,5},{4,2},{5,3},{6,0},{7,1},{8,14},{9,15},{10,... | collective-permute-start | bytes 221192 | tf_op jit(solution)/shard_map/ppermute | solution.py:533
  95.7 8.0 %collective-permute-start.29 = (bf16[288,128]{1,0:T(8,128)(2,1)S(1)}, bf16[288,128]{1,0:T(8,128)(2,1)S(1)}, u32[]{:S(2)}, u32[]{:S(2)}) collective-permute-start(bf16[288,128]{1,0:T(8,128)(2,1)S(1)} %get-tuple-element.131), channel_id=1, source_target_pairs={{0,4},{1,5},{2,6},{3,7},{4,0},{5,1},{6,2},{7,3},{8,12},{9,13},{10,... | collective-permute-start | bytes 221192 | tf_op jit(solution)/shard_map/ppermute | solution.py:533
  95.7 8.0 %collective-permute-start.30 = (bf16[288,128]{1,0:T(8,128)(2,1)S(1)}, bf16[288,128]{1,0:T(8,128)(2,1)S(1)}, u32[]{:S(2)}, u32[]{:S(2)}) collective-permute-start(bf16[288,128]{1,0:T(8,128)(2,1)S(1)} %get-tuple-element.132), channel_id=1, source_target_pairs={{0,2},{1,3},{2,0},{3,1},{4,6},{5,7},{6,4},{7,5},{8,10},{9,11},{10,... | collective-permute-start | bytes 221192 | tf_op jit(solution)/shard_map/ppermute | solution.py:533
  104.3 5.8 %collective-permute-start.33 = (bf16[288,128]{1,0:T(8,128)(2,1)S(1)}, bf16[288,128]{1,0:T(8,128)(2,1)S(1)}, u32[]{:S(2)}, u32[]{:S(2)}) collective-permute-start(bf16[288,128]{1,0:T(8,128)(2,1)S(1)} %shard_map.158.refs_0_), channel_id=1, source_target_pairs={{0,2},{1,3},{2,0},{3,1},{4,6},{5,7},{6,4},{7,5},{8,10},{9,11},{10,... | collective-permute-start | bytes 221192 | tf_op jit(solution)/shard_map/ppermute | solution.py:533
  104.3 5.7 %collective-permute-start.32 = (bf16[288,128]{1,0:T(8,128)(2,1)S(1)}, bf16[288,128]{1,0:T(8,128)(2,1)S(1)}, u32[]{:S(2)}, u32[]{:S(2)}) collective-permute-start(bf16[288,128]{1,0:T(8,128)(2,1)S(1)} %shard_map.158.refs_0_), channel_id=1, source_target_pairs={{0,4},{1,5},{2,6},{3,7},{4,0},{5,1},{6,2},{7,3},{8,12},{9,13},{10,... | collective-permute-start | bytes 221192 | tf_op jit(solution)/shard_map/ppermute | solution.py:533
  105.8 5.7 %collective-permute-start.31 = (bf16[288,128]{1,0:T(8,128)(2,1)S(1)}, bf16[288,128]{1,0:T(8,128)(2,1)S(1)}, u32[]{:S(2)}, u32[]{:S(2)}) collective-permute-start(bf16[288,128]{1,0:T(8,128)(2,1)S(1)} %shard_map.158.refs_0_), channel_id=1, source_target_pairs={{0,6},{1,7},{2,4},{3,5},{4,2},{5,3},{6,0},{7,1},{8,14},{9,15},{10,... | collective-permute-start | bytes 221192 | tf_op jit(solution)/shard_map/ppermute | solution.py:533
  107.9 2.2 %collective-permute-start.34 = (f32[8,128]{1,0:T(8,128)S(1)}, f32[8,128]{1,0:T(8,128)S(1)}, u32[]{:S(2)}, u32[]{:S(2)}) collective-permute-start(f32[8,128]{1,0:T(8,128)S(1)} %get-tuple-element.142.refs_4_), channel_id=1, source_target_pairs={{0,1},{1,0},{2,3},{3,2},{4,5},{5,4},{6,7},{7,6},{8,9},{9,8},{10,11... | collective-permute-start | bytes 12296 | tf_op jit(solution)/shard_map/ppermute | solution.py:533
  112.0 8.7 %collective-permute-start.37 = (bf16[1168,128]{1,0:T(8,128)(2,1)S(1)}, bf16[1168,128]{1,0:T(8,128)(2,1)S(1)}, u32[]{:S(2)}, u32[]{:S(2)}) collective-permute-start(bf16[1168,128]{1,0:T(8,128)(2,1)S(1)} %shard_map.159.refs_0_), channel_id=1, source_target_pairs={{0,8},{8,0},{16,24},{24,16},{1,9},{9,1},{17,25},{25,17},{2,10},{10... | collective-permute-start | bytes 897032 | tf_op jit(solution)/shard_map/ppermute | solution.py:533
  113.3 7.4 %collective-permute-start.36 = (bf16[1168,128]{1,0:T(8,128)(2,1)S(1)}, bf16[1168,128]{1,0:T(8,128)(2,1)S(1)}, u32[]{:S(2)}, u32[]{:S(2)}) collective-permute-start(bf16[1168,128]{1,0:T(8,128)(2,1)S(1)} %shard_map.159.refs_0_), channel_id=1, source_target_pairs={{0,16},{8,24},{16,0},{24,8},{1,17},{9,25},{17,1},{25,9},{2,18},{10... | collective-permute-start | bytes 897032 | tf_op jit(solution)/shard_map/ppermute | solution.py:533
  114.5 11.0 %collective-permute-start.35 = (bf16[1168,128]{1,0:T(8,128)(2,1)S(1)}, bf16[1168,128]{1,0:T(8,128)(2,1)S(1)}, u32[]{:S(2)}, u32[]{:S(2)}) collective-permute-start(bf16[1168,128]{1,0:T(8,128)(2,1)S(1)} %shard_map.159.refs_0_), channel_id=1, source_target_pairs={{0,24},{8,16},{16,8},{24,0},{1,25},{9,17},{17,9},{25,1},{2,26},{10... | collective-permute-start | bytes 897032 | tf_op jit(solution)/shard_map/ppermute | solution.py:533
  114.7 4.5 %collective-permute-start.38 = (bf16[64,2048]{1,0:T(8,128)(2,1)S(1)}, bf16[64,2048]{1,0:T(8,128)(2,1)S(1)}, u32[]{:S(2)}, u32[]{:S(2)}) collective-permute-start(bf16[64,2048]{1,0:T(8,128)(2,1)S(1)} %get-tuple-element.146), channel_id=1, source_target_pairs={{0,1},{1,0},{2,3},{3,2},{4,5},{5,4},{6,7},{7,6},{8,9},{9,8},{10,11... | collective-permute-start | bytes 786440 | tf_op jit(solution)/shard_map/ppermute | solution.py:533
  118.1 14.1 %collective-permute-start.39 = (bf16[1168,128]{1,0:T(8,128)(2,1)S(1)}, bf16[1168,128]{1,0:T(8,128)(2,1)S(1)}, u32[]{:S(2)}, u32[]{:S(2)}) collective-permute-start(bf16[1168,128]{1,0:T(8,128)(2,1)S(1)} %shard_map.159.refs_0_), channel_id=1, source_target_pairs={{0,1},{1,0},{2,3},{3,2},{4,5},{5,4},{6,7},{7,6},{8,9},{9,8},{10,11... | collective-permute-start | bytes 897032 | tf_op jit(solution)/shard_map/ppermute | solution.py:533
  125.6 6.6 %collective-permute-start.40 = (bf16[1168,128]{1,0:T(8,128)(2,1)S(1)}, bf16[1168,128]{1,0:T(8,128)(2,1)S(1)}, u32[]{:S(2)}, u32[]{:S(2)}) collective-permute-start(bf16[1168,128]{1,0:T(8,128)(2,1)S(1)} %collective-permute-done.35.refs_1_), channel_id=1, source_target_pairs={{0,1},{1,0},{2,3},{3,2},{4,5},{5,4},{6,7},{7,6},{8,9},{9,8},{10,11... | collective-permute-start | bytes 897032 | tf_op jit(solution)/shard_map/ppermute | solution.py:533
  129.2 3.0 %collective-permute-start.41 = (bf16[1168,128]{1,0:T(8,128)(2,1)S(1)}, bf16[1168,128]{1,0:T(8,128)(2,1)S(1)}, u32[]{:S(2)}, u32[]{:S(2)}) collective-permute-start(bf16[1168,128]{1,0:T(8,128)(2,1)S(1)} %collective-permute-done.36.refs_2_), channel_id=1, source_target_pairs={{0,1},{1,0},{2,3},{3,2},{4,5},{5,4},{6,7},{7,6},{8,9},{9,8},{10,11... | collective-permute-start | bytes 897032 | tf_op jit(solution)/shard_map/ppermute | solution.py:533
  129.2 3.0 %collective-permute-start.42 = (bf16[1168,128]{1,0:T(8,128)(2,1)S(1)}, bf16[1168,128]{1,0:T(8,128)(2,1)S(1)}, u32[]{:S(2)}, u32[]{:S(2)}) collective-permute-start(bf16[1168,128]{1,0:T(8,128)(2,1)S(1)} %collective-permute-done.37.refs_3_), channel_id=1, source_target_pairs={{0,1},{1,0},{2,3},{3,2},{4,5},{5,4},{6,7},{7,6},{8,9},{9,8},{10,11... | collective-permute-start | bytes 897032 | tf_op jit(solution)/shard_map/ppermute | solution.py:533
  (1 other events, 1.9 us)

commit v3 on v2

--- a/solution.py
+++ b/solution.py
@@ -12,7 +12,7 @@
 BF16 = jnp.bfloat16
 F8 = jnp.float8_e4m3fn
 VMEM_BYTES = 40 << 20
-GROUPS = ((0, 1), (2, 3), (4, 5), (6, 7), (8, 9), (10, 11), (12, 13))
+GROUPS = ((0, 1, 2, 3, 4, 5, 6), (7, 8, 9, 10, 11, 12, 13))
 
 
 def mm(left, right):
@@ -44,7 +44,7 @@
 
 def hits(index_row, rows):
     places = lax.broadcasted_iota(jnp.int16, (rows, index_row.shape[1]), 0)
-    return jnp.where(places == index_row, jnp.bfloat16(1), jnp.bfloat16(0)).astype(F8)
+    return jnp.where(places == index_row, jnp.ones(places.shape, F8), jnp.zeros(places.shape, F8))
 
 
 def live_mask(near_ref, bucket, channels):

time: 134 us -> 133 us (level)
  Pallas kernels: 52.6 us -> 50.7 us
    pallas_call x19, Pallas kernels: 52.6 us -> 50.7 us  [run(): pl.pallas_call(kernel, in_specs=[pl.BlockSpec(memory_space=pltpu.SMEM)] +...]
  transfers between devices with their start and end apart: 43 -> 43, of which waited for: 14 -> 14; matrix products, arithmetic and copies ran while one was open for 0% -> 0% of each run, Pallas kernels for 29% -> 28%
where the time goes in v3:
time: 133 us; the launch traced here: 132 us
  starting transfers between devices  58.7 us (44%)
  Pallas kernels  50.7 us (38%)
  waiting for transfers between devices  21.7 us (16%)
    ppermute x43, starting transfers between devices, swapped(): return lax.ppermute(value, axis, [(i, i ^ step) for i in range(count)])  58.7 us
    pallas_call x19, Pallas kernels, run(): pl.pallas_call(kernel, in_specs=[pl.BlockSpec(memory_space=pltpu.SMEM)] +...  50.7 us
    ppermute x43, waiting for transfers between devices, swapped(): return lax.ppermute(value, axis, [(i, i ^ step) for i in range(count)])  21.7 us
  transfers between devices with their start and end apart: 43, of which 14 were waited for; matrix products, arithmetic and copies ran while one was open for 0% of the time, Pallas kernels for 28%

profile of v3, /device:TPU:1, one launch (start us, length us, event | category | flops | bytes accessed | tf_op | source)
XLA Modules:
  0.0 132.4 jit_solution(8347620066847970699)
XLA Ops:
  0.7 1.7 %shard_map.144 = (bf16[80,2048]{1,0:T(8,128)(2,1)S(1)}, bf16[64,2048]{1,0:T(8,128)(2,1)S(1)}, s32[8,512]{1,0:T(8,128)S(1)}, bf16[512,128]{1,0:T(8,128)(2,1)S(1)}) custom-call(s32[5]{0:T(128)S(1)} %stack.23.where_ref, bf16[8,64,2048]{2,1,0:T(8,128)(2,1)} %bitcast.13, s32[8,8,512]{2,1,0:T(8,128)} %down_hbm.1, bf16[512,128]{1,0:T(8,128)(2,1)} %bitcast.17), custom_call_target="tpu_custom_call" | custom-call | bytes 1 | tf_op jit(solution)/shard_map/pallas_call | solution.py:518
  2.6 2.7 %shard_map.145 = (f32[512,128]{1,0:T(8,128)S(1)}, f32[8,128]{1,0:T(8,128)S(1)}, bf16[512,512]{1,0:T(8,128)(2,1)S(1)}, f32[8,2048]{1,0:T(8,128)S(1)}, s32[27,512]{1,0:T(8,128)S(1)}, /*index=5*/s32[27,512]{1,0:T(8,128)S(1)}) custom-call(s32[5]{0:T(128)S(1)} %stack.23.where_ref, bf16[64,2048]{1,0:T(8,128)(2,1)S(1)} %get-tuple-element.87.feats_ref, ...), custom_call_target="tpu_custom_call" | custom-call | flops 2000000000 | bytes 1048576 | tf_op jit(solution)/shard_map/pallas_call | solution.py:518
  5.8 2.7 %shard_map.146 = (f32[2,512,128]{2,1,0:T(8,128)S(1)}, f32[8,128]{1,0:T(8,128)S(1)}, bf16[2,512,512]{2,1,0:T(8,128)(2,1)S(1)}, f32[2,8,2048]{2,1,0:T(8,128)S(1)}, s32[2,8,512]{2,1,0:T(8,128)S(1)}) custom-call(s32[5]{0:T(128)S(1)} %stack.23.where_ref, bf16[80,2048]{1,0:T(8,128)(2,1)S(1)} %collective-permute-done.got_ref, ...), custom_call_target="tpu_custom_call" | custom-call | flops 2000000000 | bytes 1048576 | tf_op jit(solution)/shard_map/pallas_call | solution.py:518
  8.5 4.4 %collective-permute-start.4 = (f32[8,128]{1,0:T(8,128)S(1)}, f32[8,128]{1,0:T(8,128)S(1)}, u32[]{:S(2)}, u32[]{:S(2)}) collective-permute-start(f32[8,128]{1,0:T(8,128)S(1)} %get-tuple-element.96.refs_0_.refs_16_), channel_id=1, source_target_pairs={{0,6},{1,7},{2,4},{3,5},{4,2},{5,3},{6,0},{7,1},{8,14},{9,15},{10,... | collective-permute-start | bytes 12296 | tf_op jit(solution)/shard_map/ppermute | solution.py:533
  13.9 2.4 %collective-permute-done.3.refs_2_.refs_18_ = f32[8,128]{1,0:T(8,128)S(1)} collective-permute-done((f32[8,128]{1,0:T(8,128)S(1)}, f32[8,128]{1,0:T(8,128)S(1)}, u32[]{:S(2)}, u32[]{:S(2)}) %collective-permute-start.3) | collective-permute-done | bytes 4128 | tf_op jit(solution)/shard_map/ppermute | solution.py:533
  16.3 6.4 %shard_map.148 = (bf16[2,512,128]{2,1,0:T(8,128)(2,1)S(1)}, f32[2,512,128]{2,1,0:T(8,128)S(1)}, f32[8,128]{1,0:T(8,128)S(1)}) custom-call(s32[5]{0:T(128)S(1)} %stack.23.where_ref, f32[2,512,128]{2,1,0:T(8,128)S(1)} %get-tuple-element.93.hidden_ref.refs_2_, s32[2,27,512]{2,1,0:T(8,128)S(1)} %shard_map.147.near_ref.refs_4_, ...), custom_call_target="tpu_custom_call" | custom-call | flops 14495514624 | bytes 1048576 | tf_op jit(solution)/shard_map/pallas_call | solution.py:518
  22.7 1.5 %collective-permute-start.7 = (f32[8,128]{1,0:T(8,128)S(1)}, f32[8,128]{1,0:T(8,128)S(1)}, u32[]{:S(2)}, u32[]{:S(2)}) collective-permute-start(f32[8,128]{1,0:T(8,128)S(1)} %get-tuple-element.98.refs_0_.refs_16_.refs_8_), channel_id=1, source_target_pairs={{0,6},{1,7},{2,4},{3,5},{4,2},{5,3},{6,0},{7,1},{8,14},{9,15},{10,... | collective-permute-start | bytes 12296 | tf_op jit(solution)/shard_map/ppermute | solution.py:533
  24.3 2.0 %collective-permute-start.5 = (f32[8,128]{1,0:T(8,128)S(1)}, f32[8,128]{1,0:T(8,128)S(1)}, u32[]{:S(2)}, u32[]{:S(2)}) collective-permute-start(f32[8,128]{1,0:T(8,128)S(1)} %get-tuple-element.98.refs_0_.refs_16_.refs_8_), channel_id=1, source_target_pairs={{0,2},{1,3},{2,0},{3,1},{4,6},{5,7},{6,4},{7,5},{8,10},{9,11},{10,... | collective-permute-start | bytes 12296 | tf_op jit(solution)/shard_map/ppermute | solution.py:533
  26.9 2.8 %collective-permute-start.8 = (bf16[512,128]{1,0:T(8,128)(2,1)S(1)}, bf16[512,128]{1,0:T(8,128)(2,1)S(1)}, u32[]{:S(2)}, u32[]{:S(2)}) collective-permute-start(bf16[512,128]{1,0:T(8,128)(2,1)S(1)} %get-tuple-element.102), channel_id=1, source_target_pairs={{0,1},{1,0},{2,3},{3,2},{4,5},{5,4},{6,7},{7,6},{8,9},{9,8},{10,11... | collective-permute-start | bytes 393224 | tf_op jit(solution)/shard_map/ppermute | solution.py:533
  29.7 6.6 %shard_map.149 = (bf16[2,512,128]{2,1,0:T(8,128)(2,1)S(1)}, bf16[2,512,128]{2,1,0:T(8,128)(2,1)S(1)}, f32[8,128]{1,0:T(8,128)S(1)}) custom-call(s32[5]{0:T(128)S(1)} %stack.23.where_ref, f32[2,512,128]{2,1,0:T(8,128)S(1)} %get-tuple-element.97.hidden_ref.refs_2_.refs_1_, s32[2,27,512]{2,1,0:T(8,128)S(1)} %shard_map.147.near_ref.refs_4_, ...), custom_call_target="tpu_custom_call" | custom-call | flops 14495514624 | bytes 1048576 | tf_op jit(solution)/shard_map/pallas_call | solution.py:518
  36.3 1.2 collective-permute-start.11
  37.5 2.4 %collective-permute-start.9 = (f32[8,128]{1,0:T(8,128)S(1)}, f32[8,128]{1,0:T(8,128)S(1)}, u32[]{:S(2)}, u32[]{:S(2)}) collective-permute-start(f32[8,128]{1,0:T(8,128)S(1)} %get-tuple-element.103.refs_0_.refs_8_), channel_id=1, source_target_pairs={{0,2},{1,3},{2,0},{3,1},{4,6},{5,7},{6,4},{7,5},{8,10},{9,11},{10,... | collective-permute-start | bytes 12296 | tf_op jit(solution)/shard_map/ppermute | solution.py:533
  40.9 1.2 shard_map.151
  42.1 2.1 %collective-permute-start.14 = (f32[8,128]{1,0:T(8,128)S(1)}, f32[8,128]{1,0:T(8,128)S(1)}, u32[]{:S(2)}, u32[]{:S(2)}) collective-permute-start(f32[8,128]{1,0:T(8,128)S(1)} %get-tuple-element.106.refs_12_), channel_id=1, source_target_pairs={{0,6},{1,7},{2,4},{3,5},{4,2},{5,3},{6,0},{7,1},{8,14},{9,15},{10,... | collective-permute-start | bytes 12296 | tf_op jit(solution)/shard_map/ppermute | solution.py:533
  44.8 0.9 collective-permute-start.12
  45.8 4.3 %collective-permute-start.16 = (bf16[512,128]{1,0:T(8,128)(2,1)S(1)}, bf16[512,128]{1,0:T(8,128)(2,1)S(1)}, u32[]{:S(2)}, u32[]{:S(2)}) collective-permute-start(bf16[512,128]{1,0:T(8,128)(2,1)S(1)} %get-tuple-element.109), channel_id=1, source_target_pairs={{0,1},{1,0},{2,3},{3,2},{4,5},{5,4},{6,7},{7,6},{8,9},{9,8},{10,11... | collective-permute-start | bytes 393224 | tf_op jit(solution)/shard_map/ppermute | solution.py:533
  50.1 8.1 %shard_map.152 = (f32[2,512,128]{2,1,0:T(8,128)S(1)}, f32[8,128]{1,0:T(8,128)S(1)}, bf16[1792,128]{1,0:T(8,128)(2,1)S(1)}, bf16[1792,128]{1,0:T(8,128)(2,1)S(1)}) custom-call(s32[5]{0:T(128)S(1)} %stack.23.where_ref, f32[2,512,128]{2,1,0:T(8,128)S(1)} %get-tuple-element.104.refs_0_.refs_20_, bf16[2,512,128]{2,1,0:T(8,128)(2,1)S(1)} %get-tuple-element.99.hidden_ref.refs_1_, ...), custom_call_target="tpu_custom_call" | custom-call | flops 14495514624 | bytes 1048576 | tf_op jit(solution)/shard_map/pallas_call | solution.py:518
  58.2 1.2 collective-permute-start.19
  59.5 2.4 %collective-permute-start.17 = (f32[8,128]{1,0:T(8,128)S(1)}, f32[8,128]{1,0:T(8,128)S(1)}, u32[]{:S(2)}, u32[]{:S(2)}) collective-permute-start(f32[8,128]{1,0:T(8,128)S(1)} %get-tuple-element.112.refs_12_.refs_8_), channel_id=1, source_target_pairs={{0,2},{1,3},{2,0},{3,1},{4,6},{5,7},{6,4},{7,5},{8,10},{9,11},{10,... | collective-permute-start | bytes 12296 | tf_op jit(solution)/shard_map/ppermute | solution.py:533
  61.9 2.4 %collective-permute-start.15 = (bf16[1792,128]{1,0:T(8,128)(2,1)S(1)}, bf16[1792,128]{1,0:T(8,128)(2,1)S(1)}, u32[]{:S(2)}, u32[]{:S(2)}) collective-permute-start(bf16[1792,128]{1,0:T(8,128)(2,1)S(1)} %get-tuple-element.108), channel_id=1, source_target_pairs={{0,1},{1,0},{2,3},{3,2},{4,5},{5,4},{6,7},{7,6},{8,9},{9,8},{10,11... | collective-permute-start | bytes 1376264 | tf_op jit(solution)/shard_map/ppermute | solution.py:533
  64.3 7.6 %shard_map.153 = (f32[2,512,128]{2,1,0:T(8,128)S(1)}, f32[8,128]{1,0:T(8,128)S(1)}, bf16[1792,128]{1,0:T(8,128)(2,1)S(1)}, bf16[1792,128]{1,0:T(8,128)(2,1)S(1)}) custom-call(s32[5]{0:T(128)S(1)} %stack.23.where_ref, f32[2,512,128]{2,1,0:T(8,128)S(1)} %get-tuple-element.111.refs_0_, f32[2,512,128]{2,1,0:T(8,128)S(1)} %get-tuple-element.97.hidden_ref.refs_2_.refs_1_, ...), custom_call_target="tpu_custom_call" | custom-call | flops 14495514624 | bytes 1048576 | tf_op jit(solution)/shard_map/pallas_call | solution.py:518
  71.9 2.7 %collective-permute-start.20 = (bf16[1792,128]{1,0:T(8,128)(2,1)S(1)}, bf16[1792,128]{1,0:T(8,128)(2,1)S(1)}, u32[]{:S(2)}, u32[]{:S(2)}) collective-permute-start(bf16[1792,128]{1,0:T(8,128)(2,1)S(1)} %get-tuple-element.114), channel_id=1, source_target_pairs={{0,1},{1,0},{2,3},{3,2},{4,5},{5,4},{6,7},{7,6},{8,9},{9,8},{10,11... | collective-permute-start | bytes 1376264 | tf_op jit(solution)/shard_map/ppermute | solution.py:533
  74.6 1.4 %collective-permute-done.20.refs_3_ = bf16[1792,128]{1,0:T(8,128)(2,1)S(1)} collective-permute-done((bf16[1792,128]{1,0:T(8,128)(2,1)S(1)}, bf16[1792,128]{1,0:T(8,128)(2,1)S(1)}, u32[]{:S(2)}, u32[]{:S(2)}) %collective-permute-start.20) | collective-permute-done | bytes 458784 | tf_op jit(solution)/shard_map/ppermute | solution.py:533
  76.8 2.2 %collective-permute-start.21 = (bf16[896,128]{1,0:T(8,128)(2,1)S(1)}, bf16[896,128]{1,0:T(8,128)(2,1)S(1)}, u32[]{:S(2)}, u32[]{:S(2)}) collective-permute-start(bf16[896,128]{1,0:T(8,128)(2,1)S(1)} %get-tuple-element.116), channel_id=1, source_target_pairs={{0,24},{8,16},{16,8},{24,0},{1,25},{9,17},{17,9},{25,1},{2,26},{10... | collective-permute-start | bytes 688136 | tf_op jit(solution)/shard_map/ppermute | solution.py:533
  79.5 1.1 collective-permute-start.26
  81.3 2.4 %collective-permute-done.26.refs_7_ = f32[8,128]{1,0:T(8,128)S(1)} collective-permute-done((f32[8,128]{1,0:T(8,128)S(1)}, f32[8,128]{1,0:T(8,128)S(1)}, u32[]{:S(2)}, u32[]{:S(2)}) %collective-permute-start.26) | collective-permute-done | bytes 4128 | tf_op jit(solution)/shard_map/ppermute | solution.py:533
  84.4 2.2 %collective-permute-done.24.refs_5_ = f32[8,128]{1,0:T(8,128)S(1)} collective-permute-done((f32[8,128]{1,0:T(8,128)S(1)}, f32[8,128]{1,0:T(8,128)S(1)}, u32[]{:S(2)}, u32[]{:S(2)}) %collective-permute-start.24) | collective-permute-done | bytes 4128 | tf_op jit(solution)/shard_map/ppermute | solution.py:533
  86.5 1.1 shard_map.155
  87.7 3.3 %collective-permute-start.27 = (bf16[256,128]{1,0:T(8,128)(2,1)S(1)}, bf16[256,128]{1,0:T(8,128)(2,1)S(1)}, u32[]{:S(2)}, u32[]{:S(2)}) collective-permute-start(bf16[256,128]{1,0:T(8,128)(2,1)S(1)} %get-tuple-element.123), channel_id=1, source_target_pairs={{0,1},{1,0},{2,3},{3,2},{4,5},{5,4},{6,7},{7,6},{8,9},{9,8},{10,11... | collective-permute-start | bytes 196616 | tf_op jit(solution)/shard_map/ppermute | solution.py:533
  90.9 0.9 collective-permute-done.27.refs_5_
  92.5 1.2 collective-permute-start.28
  93.7 2.4 %collective-permute-start.30 = (bf16[288,128]{1,0:T(8,128)(2,1)S(1)}, bf16[288,128]{1,0:T(8,128)(2,1)S(1)}, u32[]{:S(2)}, u32[]{:S(2)}) collective-permute-start(bf16[288,128]{1,0:T(8,128)(2,1)S(1)} %get-tuple-element.132), channel_id=1, source_target_pairs={{0,2},{1,3},{2,0},{3,1},{4,6},{5,7},{6,4},{7,5},{8,10},{9,11},{10,... | collective-permute-start | bytes 221192 | tf_op jit(solution)/shard_map/ppermute | solution.py:533
  96.1 3.2 %shard_map.157 = (bf16[64,2048]{1,0:T(8,128)(2,1)S(1)}, bf16[64,2048]{1,0:T(8,128)(2,1)S(1)}) custom-call(s32[5]{0:T(128)S(1)} %stack.23.where_ref, bf16[2,512,128]{2,1,0:T(8,128)(2,1)S(1)} %get-tuple-element.133.rows_ref, f32[2,8,2048]{2,1,0:T(8,128)S(1)} %get-tuple-element.134.which_ref, s32[2,8,512]{2,1,0:T(8,128)S(1)} %get-tuple-element.135.tables_ref, ...), custom_call_target="tpu_custom_call" | custom-call | bytes 1 | tf_op jit(solution)/shard_map/pallas_call | solution.py:518
  99.3 2.4 %collective-permute-done.29.refs_2_ = bf16[288,128]{1,0:T(8,128)(2,1)S(1)} collective-permute-done((bf16[288,128]{1,0:T(8,128)(2,1)S(1)}, bf16[288,128]{1,0:T(8,128)(2,1)S(1)}, u32[]{:S(2)}, u32[]{:S(2)}) %collective-permute-start.29) | collective-permute-done | bytes 73760 | tf_op jit(solution)/shard_map/ppermute | solution.py:533
  102.4 1.4 %collective-permute-start.32 = (bf16[288,128]{1,0:T(8,128)(2,1)S(1)}, bf16[288,128]{1,0:T(8,128)(2,1)S(1)}, u32[]{:S(2)}, u32[]{:S(2)}) collective-permute-start(bf16[288,128]{1,0:T(8,128)(2,1)S(1)} %shard_map.158.refs_0_), channel_id=1, source_target_pairs={{0,4},{1,5},{2,6},{3,7},{4,0},{5,1},{6,2},{7,3},{8,12},{9,13},{10,... | collective-permute-start | bytes 221192 | tf_op jit(solution)/shard_map/ppermute | solution.py:533
  103.8 2.1 %collective-permute-start.31 = (bf16[288,128]{1,0:T(8,128)(2,1)S(1)}, bf16[288,128]{1,0:T(8,128)(2,1)S(1)}, u32[]{:S(2)}, u32[]{:S(2)}) collective-permute-start(bf16[288,128]{1,0:T(8,128)(2,1)S(1)} %shard_map.158.refs_0_), channel_id=1, source_target_pairs={{0,6},{1,7},{2,4},{3,5},{4,2},{5,3},{6,0},{7,1},{8,14},{9,15},{10,... | collective-permute-start | bytes 221192 | tf_op jit(solution)/shard_map/ppermute | solution.py:533
  106.0 1.3 %collective-permute-start.34 = (f32[8,128]{1,0:T(8,128)S(1)}, f32[8,128]{1,0:T(8,128)S(1)}, u32[]{:S(2)}, u32[]{:S(2)}) collective-permute-start(f32[8,128]{1,0:T(8,128)S(1)} %get-tuple-element.142.refs_4_), channel_id=1, source_target_pairs={{0,1},{1,0},{2,3},{3,2},{4,5},{5,4},{6,7},{7,6},{8,9},{9,8},{10,11... | collective-permute-start | bytes 12296 | tf_op jit(solution)/shard_map/ppermute | solution.py:533
  107.3 0.8 collective-permute-done.34.refs_5_
  108.1 1.4 %collective-permute-done.31.refs_1_ = bf16[288,128]{1,0:T(8,128)(2,1)S(1)} collective-permute-done((bf16[288,128]{1,0:T(8,128)(2,1)S(1)}, bf16[288,128]{1,0:T(8,128)(2,1)S(1)}, u32[]{:S(2)}, u32[]{:S(2)}) %collective-permute-start.31) | collective-permute-done | bytes 73760 | tf_op jit(solution)/shard_map/ppermute | solution.py:533
  110.1 1.3 collective-permute-start.37
  111.4 1.2 collective-permute-start.36
  112.8 3.3 %collective-permute-start.38 = (bf16[64,2048]{1,0:T(8,128)(2,1)S(1)}, bf16[64,2048]{1,0:T(8,128)(2,1)S(1)}, u32[]{:S(2)}, u32[]{:S(2)}) collective-permute-start(bf16[64,2048]{1,0:T(8,128)(2,1)S(1)} %get-tuple-element.146), channel_id=1, source_target_pairs={{0,1},{1,0},{2,3},{3,2},{4,5},{5,4},{6,7},{7,6},{8,9},{9,8},{10,11... | collective-permute-start | bytes 786440 | tf_op jit(solution)/shard_map/ppermute | solution.py:533
  116.2 1.2 collective-permute-done.38.other_input
  117.3 1.5 %shard_map.160 = (bf16[2,512,128]{2,1,0:T(8,128)(2,1)}, bf16[2,64,2048]{2,1,0:T(8,128)(2,1)}) custom-call(s32[5]{0:T(128)S(1)} %stack.23.where_ref, bf16[512,128]{1,0:T(8,128)(2,1)S(1)} %get-tuple-element.143.own_features, bf16[512,128]{1,0:T(8,128)(2,1)S(1)} %collective-permute-done.16.other_features, bf16[64,2048]{1,0:T(8,128)(2,1)S(1)} %get-tuple-element.145.own_input, ...), custom_call_target="tpu_custom_call" | custom-call | bytes 1 | tf_op jit(solution)/shard_map/pallas_call | solution.py:518
  118.8 4.8 %collective-permute-done.35.refs_1_ = bf16[1168,128]{1,0:T(8,128)(2,1)S(1)} collective-permute-done((bf16[1168,128]{1,0:T(8,128)(2,1)S(1)}, bf16[1168,128]{1,0:T(8,128)(2,1)S(1)}, u32[]{:S(2)}, u32[]{:S(2)}) %collective-permute-start.35) | collective-permute-done | bytes 299040 | tf_op jit(solution)/shard_map/ppermute | solution.py:533
  123.6 3.7 %collective-permute-start.40 = (bf16[1168,128]{1,0:T(8,128)(2,1)S(1)}, bf16[1168,128]{1,0:T(8,128)(2,1)S(1)}, u32[]{:S(2)}, u32[]{:S(2)}) collective-permute-start(bf16[1168,128]{1,0:T(8,128)(2,1)S(1)} %collective-permute-done.35.refs_1_), channel_id=1, source_target_pairs={{0,1},{1,0},{2,3},{3,2},{4,5},{5,4},{6,7},{7,6},{8,9},{9,8},{10,11... | collective-permute-start | bytes 897032 | tf_op jit(solution)/shard_map/ppermute | solution.py:533
  127.8 2.4 %shard_map.161 = (f32[3456,128]{1,0:T(8,128)}, f32[3456,128]{1,0:T(8,128)}, f32[512,128]{1,0:T(8,128)}, f32[3,128]{1,0:T(4,128)}, f32[3,128]{1,0:T(4,128)}) custom-call(s32[5]{0:T(128)S(1)} %stack.23.where_ref, bf16[1168,128]{1,0:T(8,128)(2,1)S(1)} %shard_map.159.refs_0_, bf16[1168,128]{1,0:T(8,128)(2,1)S(1)} %collective-permute-done.35.refs_1_, ...), custom_call_target="tpu_custom_call" | custom-call | flops 1000000000 | bytes 1048576 | tf_op jit(solution)/shard_map/pallas_call | solution.py:518
  130.3 1.9 %shard_map.162 = (f32[3456,128]{1,0:T(8,128)}, f32[3456,128]{1,0:T(8,128)}, f32[512,128]{1,0:T(8,128)}) custom-call(s32[5]{0:T(128)S(1)} %stack.23.where_ref, bf16[1168,128]{1,0:T(8,128)(2,1)S(1)} %collective-permute-done.39.refs_0_, ...), custom_call_target="tpu_custom_call", output_to_operand_aliasing={{0}: (5, {}), {1}: (6, {}), {2}: (7, {})} | custom-call | flops 1000000000 | bytes 1048576 | tf_op jit(solution)/shard_map/pallas_call | solution.py:518
  (70 shorter events, 9.1 us)
Async XLA Ops:
  2.4 3.3 %collective-permute-start = (bf16[80,2048]{1,0:T(8,128)(2,1)S(1)}, bf16[80,2048]{1,0:T(8,128)(2,1)S(1)}, u32[]{:S(2)}, u32[]{:S(2)}) collective-permute-start(bf16[80,2048]{1,0:T(8,128)(2,1)S(1)} %get-tuple-element.85), channel_id=1, source_target_pairs={{0,1},{1,0},{2,3},{3,2},{4,5},{5,4},{6,7},{7,6},{8,9},{9,8},{10,11... | collective-permute-start | bytes 983048 | tf_op jit(solution)/shard_map/ppermute | solution.py:533
  5.2 8.0 %collective-permute-start.1 = (s32[27,512]{1,0:T(8,128)S(1)}, s32[27,512]{1,0:T(8,128)S(1)}, u32[]{:S(2)}, u32[]{:S(2)}) collective-permute-start(s32[27,512]{1,0:T(8,128)S(1)} %get-tuple-element.95), channel_id=1, source_target_pairs={{0,1},{1,0},{2,3},{3,2},{4,5},{5,4},{6,7},{7,6},{8,9},{9,8},{10,11... | collective-permute-start | bytes 165896 | tf_op jit(solution)/shard_map/ppermute | solution.py:533
  5.8 10.5 %copy-start.2 = (bf16[27,128,128]{2,1,0:T(8,128)(2,1)S(1)}, bf16[27,128,128]{2,1,0:T(8,128)(2,1)}, u32[]{:S(2)}) copy-start(bf16[27,128,128]{2,1,0:T(8,128)(2,1)} %refs_5_.3) | copy-start | bytes 2654212
  5.8 10.5 %copy-start.4 = (f32[3,128]{1,0:T(4,128)S(1)}, f32[3,128]{1,0:T(4,128)}, u32[]{:S(2)}) copy-start(f32[3,128]{1,0:T(4,128)} %refs_7_.3) | copy-start | bytes 4612
  5.8 10.5 %copy-start.5 = (f32[3,128]{1,0:T(4,128)S(1)}, f32[3,128]{1,0:T(4,128)}, u32[]{:S(2)}) copy-start(f32[3,128]{1,0:T(4,128)} %scale_ref.7) | copy-start | bytes 4612
  8.5 5.4 %collective-permute-start.4 = (f32[8,128]{1,0:T(8,128)S(1)}, f32[8,128]{1,0:T(8,128)S(1)}, u32[]{:S(2)}, u32[]{:S(2)}) collective-permute-start(f32[8,128]{1,0:T(8,128)S(1)} %get-tuple-element.96.refs_0_.refs_16_), channel_id=1, source_target_pairs={{0,6},{1,7},{2,4},{3,5},{4,2},{5,3},{6,0},{7,1},{8,14},{9,15},{10,... | collective-permute-start | bytes 12296 | tf_op jit(solution)/shard_map/ppermute | solution.py:533
  12.9 3.4 %collective-permute-start.3 = (f32[8,128]{1,0:T(8,128)S(1)}, f32[8,128]{1,0:T(8,128)S(1)}, u32[]{:S(2)}, u32[]{:S(2)}) collective-permute-start(f32[8,128]{1,0:T(8,128)S(1)} %get-tuple-element.96.refs_0_.refs_16_), channel_id=1, source_target_pairs={{0,4},{1,5},{2,6},{3,7},{4,0},{5,1},{6,2},{7,3},{8,12},{9,13},{10,... | collective-permute-start | bytes 12296 | tf_op jit(solution)/shard_map/ppermute | solution.py:533
  12.9 3.4 %collective-permute-start.2 = (f32[8,128]{1,0:T(8,128)S(1)}, f32[8,128]{1,0:T(8,128)S(1)}, u32[]{:S(2)}, u32[]{:S(2)}) collective-permute-start(f32[8,128]{1,0:T(8,128)S(1)} %get-tuple-element.96.refs_0_.refs_16_), channel_id=1, source_target_pairs={{0,2},{1,3},{2,0},{3,1},{4,6},{5,7},{6,4},{7,5},{8,10},{9,11},{10,... | collective-permute-start | bytes 12296 | tf_op jit(solution)/shard_map/ppermute | solution.py:533
  16.3 10.0 %copy-start = (bf16[8,512,128]{2,1,0:T(8,128)(2,1)S(1)}, bf16[8,512,128]{2,1,0:T(8,128)(2,1)}, u32[]{:S(2)}) copy-start(bf16[8,512,128]{2,1,0:T(8,128)(2,1)} %grad_ref.1) | copy-start | bytes 3145732
  16.3 13.4 %copy-start.1 = (bf16[27,128,128]{2,1,0:T(8,128)(2,1)S(1)}, bf16[27,128,128]{2,1,0:T(8,128)(2,1)}, u32[]{:S(2)}) copy-start(bf16[27,128,128]{2,1,0:T(8,128)(2,1)} %refs_5_.2) | copy-start | bytes 2654212
  22.7 7.0 %collective-permute-start.7 = (f32[8,128]{1,0:T(8,128)S(1)}, f32[8,128]{1,0:T(8,128)S(1)}, u32[]{:S(2)}, u32[]{:S(2)}) collective-permute-start(f32[8,128]{1,0:T(8,128)S(1)} %get-tuple-element.98.refs_0_.refs_16_.refs_8_), channel_id=1, source_target_pairs={{0,6},{1,7},{2,4},{3,5},{4,2},{5,3},{6,0},{7,1},{8,14},{9,15},{10,... | collective-permute-start | bytes 12296 | tf_op jit(solution)/shard_map/ppermute | solution.py:533
  24.2 5.4 %collective-permute-start.6 = (f32[8,128]{1,0:T(8,128)S(1)}, f32[8,128]{1,0:T(8,128)S(1)}, u32[]{:S(2)}, u32[]{:S(2)}) collective-permute-start(f32[8,128]{1,0:T(8,128)S(1)} %get-tuple-element.98.refs_0_.refs_16_.refs_8_), channel_id=1, source_target_pairs={{0,4},{1,5},{2,6},{3,7},{4,0},{5,1},{6,2},{7,3},{8,12},{9,13},{10,... | collective-permute-start | bytes 12296 | tf_op jit(solution)/shard_map/ppermute | solution.py:533
  24.3 5.4 %collective-permute-start.5 = (f32[8,128]{1,0:T(8,128)S(1)}, f32[8,128]{1,0:T(8,128)S(1)}, u32[]{:S(2)}, u32[]{:S(2)}) collective-permute-start(f32[8,128]{1,0:T(8,128)S(1)} %get-tuple-element.98.refs_0_.refs_16_.refs_8_), channel_id=1, source_target_pairs={{0,2},{1,3},{2,0},{3,1},{4,6},{5,7},{6,4},{7,5},{8,10},{9,11},{10,... | collective-permute-start | bytes 12296 | tf_op jit(solution)/shard_map/ppermute | solution.py:533
  26.9 13.0 %collective-permute-start.8 = (bf16[512,128]{1,0:T(8,128)(2,1)S(1)}, bf16[512,128]{1,0:T(8,128)(2,1)S(1)}, u32[]{:S(2)}, u32[]{:S(2)}) collective-permute-start(bf16[512,128]{1,0:T(8,128)(2,1)S(1)} %get-tuple-element.102), channel_id=1, source_target_pairs={{0,1},{1,0},{2,3},{3,2},{4,5},{5,4},{6,7},{7,6},{8,9},{9,8},{10,11... | collective-permute-start | bytes 393224 | tf_op jit(solution)/shard_map/ppermute | solution.py:533
  36.3 4.3 %collective-permute-start.11 = (f32[8,128]{1,0:T(8,128)S(1)}, f32[8,128]{1,0:T(8,128)S(1)}, u32[]{:S(2)}, u32[]{:S(2)}) collective-permute-start(f32[8,128]{1,0:T(8,128)S(1)} %get-tuple-element.103.refs_0_.refs_8_), channel_id=1, source_target_pairs={{0,6},{1,7},{2,4},{3,5},{4,2},{5,3},{6,0},{7,1},{8,14},{9,15},{10,... | collective-permute-start | bytes 12296 | tf_op jit(solution)/shard_map/ppermute | solution.py:533
  37.5 3.4 %collective-permute-start.10 = (f32[8,128]{1,0:T(8,128)S(1)}, f32[8,128]{1,0:T(8,128)S(1)}, u32[]{:S(2)}, u32[]{:S(2)}) collective-permute-start(f32[8,128]{1,0:T(8,128)S(1)} %get-tuple-element.103.refs_0_.refs_8_), channel_id=1, source_target_pairs={{0,4},{1,5},{2,6},{3,7},{4,0},{5,1},{6,2},{7,3},{8,12},{9,13},{10,... | collective-permute-start | bytes 12296 | tf_op jit(solution)/shard_map/ppermute | solution.py:533
  37.5 3.4 %collective-permute-start.9 = (f32[8,128]{1,0:T(8,128)S(1)}, f32[8,128]{1,0:T(8,128)S(1)}, u32[]{:S(2)}, u32[]{:S(2)}) collective-permute-start(f32[8,128]{1,0:T(8,128)S(1)} %get-tuple-element.103.refs_0_.refs_8_), channel_id=1, source_target_pairs={{0,2},{1,3},{2,0},{3,1},{4,6},{5,7},{6,4},{7,5},{8,10},{9,11},{10,... | collective-permute-start | bytes 12296 | tf_op jit(solution)/shard_map/ppermute | solution.py:533
  42.1 7.9 %collective-permute-start.14 = (f32[8,128]{1,0:T(8,128)S(1)}, f32[8,128]{1,0:T(8,128)S(1)}, u32[]{:S(2)}, u32[]{:S(2)}) collective-permute-start(f32[8,128]{1,0:T(8,128)S(1)} %get-tuple-element.106.refs_12_), channel_id=1, source_target_pairs={{0,6},{1,7},{2,4},{3,5},{4,2},{5,3},{6,0},{7,1},{8,14},{9,15},{10,... | collective-permute-start | bytes 12296 | tf_op jit(solution)/shard_map/ppermute | solution.py:533
  44.3 5.8 %collective-permute-start.13 = (f32[8,128]{1,0:T(8,128)S(1)}, f32[8,128]{1,0:T(8,128)S(1)}, u32[]{:S(2)}, u32[]{:S(2)}) collective-permute-start(f32[8,128]{1,0:T(8,128)S(1)} %get-tuple-element.106.refs_12_), channel_id=1, source_target_pairs={{0,4},{1,5},{2,6},{3,7},{4,0},{5,1},{6,2},{7,3},{8,12},{9,13},{10,... | collective-permute-start | bytes 12296 | tf_op jit(solution)/shard_map/ppermute | solution.py:533
  44.8 5.3 %collective-permute-start.12 = (f32[8,128]{1,0:T(8,128)S(1)}, f32[8,128]{1,0:T(8,128)S(1)}, u32[]{:S(2)}, u32[]{:S(2)}) collective-permute-start(f32[8,128]{1,0:T(8,128)S(1)} %get-tuple-element.106.refs_12_), channel_id=1, source_target_pairs={{0,2},{1,3},{2,0},{3,1},{4,6},{5,7},{6,4},{7,5},{8,10},{9,11},{10,... | collective-permute-start | bytes 12296 | tf_op jit(solution)/shard_map/ppermute | solution.py:533
  45.8 18.5 %collective-permute-start.16 = (bf16[512,128]{1,0:T(8,128)(2,1)S(1)}, bf16[512,128]{1,0:T(8,128)(2,1)S(1)}, u32[]{:S(2)}, u32[]{:S(2)}) collective-permute-start(bf16[512,128]{1,0:T(8,128)(2,1)S(1)} %get-tuple-element.109), channel_id=1, source_target_pairs={{0,1},{1,0},{2,3},{3,2},{4,5},{5,4},{6,7},{7,6},{8,9},{9,8},{10,11... | collective-permute-start | bytes 393224 | tf_op jit(solution)/shard_map/ppermute | solution.py:533
  58.2 6.0 %collective-permute-start.19 = (f32[8,128]{1,0:T(8,128)S(1)}, f32[8,128]{1,0:T(8,128)S(1)}, u32[]{:S(2)}, u32[]{:S(2)}) collective-permute-start(f32[8,128]{1,0:T(8,128)S(1)} %get-tuple-element.112.refs_12_.refs_8_), channel_id=1, source_target_pairs={{0,6},{1,7},{2,4},{3,5},{4,2},{5,3},{6,0},{7,1},{8,14},{9,15},{10,... | collective-permute-start | bytes 12296 | tf_op jit(solution)/shard_map/ppermute | solution.py:533
  59.4 4.8 %collective-permute-start.18 = (f32[8,128]{1,0:T(8,128)S(1)}, f32[8,128]{1,0:T(8,128)S(1)}, u32[]{:S(2)}, u32[]{:S(2)}) collective-permute-start(f32[8,128]{1,0:T(8,128)S(1)} %get-tuple-element.112.refs_12_.refs_8_), channel_id=1, source_target_pairs={{0,4},{1,5},{2,6},{3,7},{4,0},{5,1},{6,2},{7,3},{8,12},{9,13},{10,... | collective-permute-start | bytes 12296 | tf_op jit(solution)/shard_map/ppermute | solution.py:533
  59.5 4.8 %collective-permute-start.17 = (f32[8,128]{1,0:T(8,128)S(1)}, f32[8,128]{1,0:T(8,128)S(1)}, u32[]{:S(2)}, u32[]{:S(2)}) collective-permute-start(f32[8,128]{1,0:T(8,128)S(1)} %get-tuple-element.112.refs_12_.refs_8_), channel_id=1, source_target_pairs={{0,2},{1,3},{2,0},{3,1},{4,6},{5,7},{6,4},{7,5},{8,10},{9,11},{10,... | collective-permute-start | bytes 12296 | tf_op jit(solution)/shard_map/ppermute | solution.py:533
  61.9 12.8 %collective-permute-start.15 = (bf16[1792,128]{1,0:T(8,128)(2,1)S(1)}, bf16[1792,128]{1,0:T(8,128)(2,1)S(1)}, u32[]{:S(2)}, u32[]{:S(2)}) collective-permute-start(bf16[1792,128]{1,0:T(8,128)(2,1)S(1)} %get-tuple-element.108), channel_id=1, source_target_pairs={{0,1},{1,0},{2,3},{3,2},{4,5},{5,4},{6,7},{7,6},{8,9},{9,8},{10,11... | collective-permute-start | bytes 1376264 | tf_op jit(solution)/shard_map/ppermute | solution.py:533
  71.9 4.2 %collective-permute-start.20 = (bf16[1792,128]{1,0:T(8,128)(2,1)S(1)}, bf16[1792,128]{1,0:T(8,128)(2,1)S(1)}, u32[]{:S(2)}, u32[]{:S(2)}) collective-permute-start(bf16[1792,128]{1,0:T(8,128)(2,1)S(1)} %get-tuple-element.114), channel_id=1, source_target_pairs={{0,1},{1,0},{2,3},{3,2},{4,5},{5,4},{6,7},{7,6},{8,9},{9,8},{10,11... | collective-permute-start | bytes 1376264 | tf_op jit(solution)/shard_map/ppermute | solution.py:533
  76.8 15.0 %collective-permute-start.21 = (bf16[896,128]{1,0:T(8,128)(2,1)S(1)}, bf16[896,128]{1,0:T(8,128)(2,1)S(1)}, u32[]{:S(2)}, u32[]{:S(2)}) collective-permute-start(bf16[896,128]{1,0:T(8,128)(2,1)S(1)} %get-tuple-element.116), channel_id=1, source_target_pairs={{0,24},{8,16},{16,8},{24,0},{1,25},{9,17},{17,9},{25,1},{2,26},{10... | collective-permute-start | bytes 688136 | tf_op jit(solution)/shard_map/ppermute | solution.py:533
  79.1 12.8 %collective-permute-start.22 = (bf16[896,128]{1,0:T(8,128)(2,1)S(1)}, bf16[896,128]{1,0:T(8,128)(2,1)S(1)}, u32[]{:S(2)}, u32[]{:S(2)}) collective-permute-start(bf16[896,128]{1,0:T(8,128)(2,1)S(1)} %get-tuple-element.117), channel_id=1, source_target_pairs={{0,16},{8,24},{16,0},{24,8},{1,17},{9,25},{17,1},{25,9},{2,18},{10... | collective-permute-start | bytes 688136 | tf_op jit(solution)/shard_map/ppermute | solution.py:533
  79.3 12.6 %collective-permute-start.23 = (bf16[896,128]{1,0:T(8,128)(2,1)S(1)}, bf16[896,128]{1,0:T(8,128)(2,1)S(1)}, u32[]{:S(2)}, u32[]{:S(2)}) collective-permute-start(bf16[896,128]{1,0:T(8,128)(2,1)S(1)} %get-tuple-element.118), channel_id=1, source_target_pairs={{0,8},{8,0},{16,24},{24,16},{1,9},{9,1},{17,25},{25,17},{2,10},{10... | collective-permute-start | bytes 688136 | tf_op jit(solution)/shard_map/ppermute | solution.py:533
  79.5 4.3 %collective-permute-start.26 = (f32[8,128]{1,0:T(8,128)S(1)}, f32[8,128]{1,0:T(8,128)S(1)}, u32[]{:S(2)}, u32[]{:S(2)}) collective-permute-start(f32[8,128]{1,0:T(8,128)S(1)} %get-tuple-element.121.refs_4_), channel_id=1, source_target_pairs={{0,6},{1,7},{2,4},{3,5},{4,2},{5,3},{6,0},{7,1},{8,14},{9,15},{10,... | collective-permute-start | bytes 12296 | tf_op jit(solution)/shard_map/ppermute | solution.py:533
  80.7 3.7 %collective-permute-start.25 = (f32[8,128]{1,0:T(8,128)S(1)}, f32[8,128]{1,0:T(8,128)S(1)}, u32[]{:S(2)}, u32[]{:S(2)}) collective-permute-start(f32[8,128]{1,0:T(8,128)S(1)} %get-tuple-element.121.refs_4_), channel_id=1, source_target_pairs={{0,4},{1,5},{2,6},{3,7},{4,0},{5,1},{6,2},{7,3},{8,12},{9,13},{10,... | collective-permute-start | bytes 12296 | tf_op jit(solution)/shard_map/ppermute | solution.py:533
  83.8 2.8 %collective-permute-start.24 = (f32[8,128]{1,0:T(8,128)S(1)}, f32[8,128]{1,0:T(8,128)S(1)}, u32[]{:S(2)}, u32[]{:S(2)}) collective-permute-start(f32[8,128]{1,0:T(8,128)S(1)} %get-tuple-element.121.refs_4_), channel_id=1, source_target_pairs={{0,2},{1,3},{2,0},{3,1},{4,6},{5,7},{6,4},{7,5},{8,10},{9,11},{10,... | collective-permute-start | bytes 12296 | tf_op jit(solution)/shard_map/ppermute | solution.py:533
  87.7 4.2 %collective-permute-start.27 = (bf16[256,128]{1,0:T(8,128)(2,1)S(1)}, bf16[256,128]{1,0:T(8,128)(2,1)S(1)}, u32[]{:S(2)}, u32[]{:S(2)}) collective-permute-start(bf16[256,128]{1,0:T(8,128)(2,1)S(1)} %get-tuple-element.123), channel_id=1, source_target_pairs={{0,1},{1,0},{2,3},{3,2},{4,5},{5,4},{6,7},{7,6},{8,9},{9,8},{10,11... | collective-permute-start | bytes 196616 | tf_op jit(solution)/shard_map/ppermute | solution.py:533
  92.5 6.8 %collective-permute-start.28 = (bf16[288,128]{1,0:T(8,128)(2,1)S(1)}, bf16[288,128]{1,0:T(8,128)(2,1)S(1)}, u32[]{:S(2)}, u32[]{:S(2)}) collective-permute-start(bf16[288,128]{1,0:T(8,128)(2,1)S(1)} %get-tuple-element.130), channel_id=1, source_target_pairs={{0,6},{1,7},{2,4},{3,5},{4,2},{5,3},{6,0},{7,1},{8,14},{9,15},{10,... | collective-permute-start | bytes 221192 | tf_op jit(solution)/shard_map/ppermute | solution.py:533
  93.7 8.0 %collective-permute-start.29 = (bf16[288,128]{1,0:T(8,128)(2,1)S(1)}, bf16[288,128]{1,0:T(8,128)(2,1)S(1)}, u32[]{:S(2)}, u32[]{:S(2)}) collective-permute-start(bf16[288,128]{1,0:T(8,128)(2,1)S(1)} %get-tuple-element.131), channel_id=1, source_target_pairs={{0,4},{1,5},{2,6},{3,7},{4,0},{5,1},{6,2},{7,3},{8,12},{9,13},{10,... | collective-permute-start | bytes 221192 | tf_op jit(solution)/shard_map/ppermute | solution.py:533
  93.7 8.0 %collective-permute-start.30 = (bf16[288,128]{1,0:T(8,128)(2,1)S(1)}, bf16[288,128]{1,0:T(8,128)(2,1)S(1)}, u32[]{:S(2)}, u32[]{:S(2)}) collective-permute-start(bf16[288,128]{1,0:T(8,128)(2,1)S(1)} %get-tuple-element.132), channel_id=1, source_target_pairs={{0,2},{1,3},{2,0},{3,1},{4,6},{5,7},{6,4},{7,5},{8,10},{9,11},{10,... | collective-permute-start | bytes 221192 | tf_op jit(solution)/shard_map/ppermute | solution.py:533
  102.3 5.8 %collective-permute-start.33 = (bf16[288,128]{1,0:T(8,128)(2,1)S(1)}, bf16[288,128]{1,0:T(8,128)(2,1)S(1)}, u32[]{:S(2)}, u32[]{:S(2)}) collective-permute-start(bf16[288,128]{1,0:T(8,128)(2,1)S(1)} %shard_map.158.refs_0_), channel_id=1, source_target_pairs={{0,2},{1,3},{2,0},{3,1},{4,6},{5,7},{6,4},{7,5},{8,10},{9,11},{10,... | collective-permute-start | bytes 221192 | tf_op jit(solution)/shard_map/ppermute | solution.py:533
  102.4 5.7 %collective-permute-start.32 = (bf16[288,128]{1,0:T(8,128)(2,1)S(1)}, bf16[288,128]{1,0:T(8,128)(2,1)S(1)}, u32[]{:S(2)}, u32[]{:S(2)}) collective-permute-start(bf16[288,128]{1,0:T(8,128)(2,1)S(1)} %shard_map.158.refs_0_), channel_id=1, source_target_pairs={{0,4},{1,5},{2,6},{3,7},{4,0},{5,1},{6,2},{7,3},{8,12},{9,13},{10,... | collective-permute-start | bytes 221192 | tf_op jit(solution)/shard_map/ppermute | solution.py:533
  103.8 5.7 %collective-permute-start.31 = (bf16[288,128]{1,0:T(8,128)(2,1)S(1)}, bf16[288,128]{1,0:T(8,128)(2,1)S(1)}, u32[]{:S(2)}, u32[]{:S(2)}) collective-permute-start(bf16[288,128]{1,0:T(8,128)(2,1)S(1)} %shard_map.158.refs_0_), channel_id=1, source_target_pairs={{0,6},{1,7},{2,4},{3,5},{4,2},{5,3},{6,0},{7,1},{8,14},{9,15},{10,... | collective-permute-start | bytes 221192 | tf_op jit(solution)/shard_map/ppermute | solution.py:533
  106.0 2.2 %collective-permute-start.34 = (f32[8,128]{1,0:T(8,128)S(1)}, f32[8,128]{1,0:T(8,128)S(1)}, u32[]{:S(2)}, u32[]{:S(2)}) collective-permute-start(f32[8,128]{1,0:T(8,128)S(1)} %get-tuple-element.142.refs_4_), channel_id=1, source_target_pairs={{0,1},{1,0},{2,3},{3,2},{4,5},{5,4},{6,7},{7,6},{8,9},{9,8},{10,11... | collective-permute-start | bytes 12296 | tf_op jit(solution)/shard_map/ppermute | solution.py:533
  110.1 8.7 %collective-permute-start.37 = (bf16[1168,128]{1,0:T(8,128)(2,1)S(1)}, bf16[1168,128]{1,0:T(8,128)(2,1)S(1)}, u32[]{:S(2)}, u32[]{:S(2)}) collective-permute-start(bf16[1168,128]{1,0:T(8,128)(2,1)S(1)} %shard_map.159.refs_0_), channel_id=1, source_target_pairs={{0,8},{8,0},{16,24},{24,16},{1,9},{9,1},{17,25},{25,17},{2,10},{10... | collective-permute-start | bytes 897032 | tf_op jit(solution)/shard_map/ppermute | solution.py:533
  111.4 7.4 %collective-permute-start.36 = (bf16[1168,128]{1,0:T(8,128)(2,1)S(1)}, bf16[1168,128]{1,0:T(8,128)(2,1)S(1)}, u32[]{:S(2)}, u32[]{:S(2)}) collective-permute-start(bf16[1168,128]{1,0:T(8,128)(2,1)S(1)} %shard_map.159.refs_0_), channel_id=1, source_target_pairs={{0,16},{8,24},{16,0},{24,8},{1,17},{9,25},{17,1},{25,9},{2,18},{10... | collective-permute-start | bytes 897032 | tf_op jit(solution)/shard_map/ppermute | solution.py:533
  112.6 11.0 %collective-permute-start.35 = (bf16[1168,128]{1,0:T(8,128)(2,1)S(1)}, bf16[1168,128]{1,0:T(8,128)(2,1)S(1)}, u32[]{:S(2)}, u32[]{:S(2)}) collective-permute-start(bf16[1168,128]{1,0:T(8,128)(2,1)S(1)} %shard_map.159.refs_0_), channel_id=1, source_target_pairs={{0,24},{8,16},{16,8},{24,0},{1,25},{9,17},{17,9},{25,1},{2,26},{10... | collective-permute-start | bytes 897032 | tf_op jit(solution)/shard_map/ppermute | solution.py:533
  112.8 4.5 %collective-permute-start.38 = (bf16[64,2048]{1,0:T(8,128)(2,1)S(1)}, bf16[64,2048]{1,0:T(8,128)(2,1)S(1)}, u32[]{:S(2)}, u32[]{:S(2)}) collective-permute-start(bf16[64,2048]{1,0:T(8,128)(2,1)S(1)} %get-tuple-element.146), channel_id=1, source_target_pairs={{0,1},{1,0},{2,3},{3,2},{4,5},{5,4},{6,7},{7,6},{8,9},{9,8},{10,11... | collective-permute-start | bytes 786440 | tf_op jit(solution)/shard_map/ppermute | solution.py:533
  116.1 14.1 %collective-permute-start.39 = (bf16[1168,128]{1,0:T(8,128)(2,1)S(1)}, bf16[1168,128]{1,0:T(8,128)(2,1)S(1)}, u32[]{:S(2)}, u32[]{:S(2)}) collective-permute-start(bf16[1168,128]{1,0:T(8,128)(2,1)S(1)} %shard_map.159.refs_0_), channel_id=1, source_target_pairs={{0,1},{1,0},{2,3},{3,2},{4,5},{5,4},{6,7},{7,6},{8,9},{9,8},{10,11... | collective-permute-start | bytes 897032 | tf_op jit(solution)/shard_map/ppermute | solution.py:533
  123.6 6.6 %collective-permute-start.40 = (bf16[1168,128]{1,0:T(8,128)(2,1)S(1)}, bf16[1168,128]{1,0:T(8,128)(2,1)S(1)}, u32[]{:S(2)}, u32[]{:S(2)}) collective-permute-start(bf16[1168,128]{1,0:T(8,128)(2,1)S(1)} %collective-permute-done.35.refs_1_), channel_id=1, source_target_pairs={{0,1},{1,0},{2,3},{3,2},{4,5},{5,4},{6,7},{7,6},{8,9},{9,8},{10,11... | collective-permute-start | bytes 897032 | tf_op jit(solution)/shard_map/ppermute | solution.py:533
  127.3 3.0 %collective-permute-start.41 = (bf16[1168,128]{1,0:T(8,128)(2,1)S(1)}, bf16[1168,128]{1,0:T(8,128)(2,1)S(1)}, u32[]{:S(2)}, u32[]{:S(2)}) collective-permute-start(bf16[1168,128]{1,0:T(8,128)(2,1)S(1)} %collective-permute-done.36.refs_2_), channel_id=1, source_target_pairs={{0,1},{1,0},{2,3},{3,2},{4,5},{5,4},{6,7},{7,6},{8,9},{9,8},{10,11... | collective-permute-start | bytes 897032 | tf_op jit(solution)/shard_map/ppermute | solution.py:533
  127.3 3.0 %collective-permute-start.42 = (bf16[1168,128]{1,0:T(8,128)(2,1)S(1)}, bf16[1168,128]{1,0:T(8,128)(2,1)S(1)}, u32[]{:S(2)}, u32[]{:S(2)}) collective-permute-start(bf16[1168,128]{1,0:T(8,128)(2,1)S(1)} %collective-permute-done.37.refs_3_), channel_id=1, source_target_pairs={{0,1},{1,0},{2,3},{3,2},{4,5},{5,4},{6,7},{7,6},{8,9},{9,8},{10,11... | collective-permute-start | bytes 897032 | tf_op jit(solution)/shard_map/ppermute | solution.py:533
  (1 other events, 1.9 us)

commit v4 on v3

--- a/solution.py
+++ b/solution.py
@@ -342,7 +342,7 @@
         next_ref[b] = upstream
         add_sums(sums_ref, col_sum(upstream), col_sum(upstream * low_centred), own_count)
 
-    each_bucket(hidden_ref.shape[0], bucket, with_skip)
+    each_bucket(hidden_ref.shape[0], bucket, True)
     put_halves(where_ref, grad_ref, keep_ref, send_ref)
 
 

time: 133 us -> 132 us (level)
  no operation moved by 1% of the time
where the time goes in v4:
time: 132 us
  starting transfers between devices  58.7 us (44%)
  Pallas kernels  50.4 us (38%)
  waiting for transfers between devices  21.7 us (16%)
    ppermute x43, starting transfers between devices, swapped(): return lax.ppermute(value, axis, [(i, i ^ step) for i in range(count)])  58.7 us
    pallas_call x19, Pallas kernels, run(): pl.pallas_call(kernel, in_specs=[pl.BlockSpec(memory_space=pltpu.SMEM)] +...  50.4 us
    ppermute x43, waiting for transfers between devices, swapped(): return lax.ppermute(value, axis, [(i, i ^ step) for i in range(count)])  21.7 us
  transfers between devices with their start and end apart: 43, of which 14 were waited for; matrix products, arithmetic and copies ran while one was open for 0% of the time, Pallas kernels for 28%

profile of v4, /device:TPU:1, one launch (start us, length us, event | category | flops | bytes accessed | tf_op | source)
XLA Modules:
  0.0 132.0 jit_solution(13260977051820786203)
XLA Ops:
  0.7 1.7 %shard_map.144 = (bf16[80,2048]{1,0:T(8,128)(2,1)S(1)}, bf16[64,2048]{1,0:T(8,128)(2,1)S(1)}, s32[8,512]{1,0:T(8,128)S(1)}, bf16[512,128]{1,0:T(8,128)(2,1)S(1)}) custom-call(s32[5]{0:T(128)S(1)} %stack.23.where_ref, bf16[8,64,2048]{2,1,0:T(8,128)(2,1)} %bitcast.13, s32[8,8,512]{2,1,0:T(8,128)} %down_hbm.1, bf16[512,128]{1,0:T(8,128)(2,1)} %bitcast.17), custom_call_target="tpu_custom_call" | custom-call | bytes 1 | tf_op jit(solution)/shard_map/pallas_call | solution.py:518
  2.6 2.7 %shard_map.145 = (f32[512,128]{1,0:T(8,128)S(1)}, f32[8,128]{1,0:T(8,128)S(1)}, bf16[512,512]{1,0:T(8,128)(2,1)S(1)}, f32[8,2048]{1,0:T(8,128)S(1)}, s32[27,512]{1,0:T(8,128)S(1)}, /*index=5*/s32[27,512]{1,0:T(8,128)S(1)}) custom-call(s32[5]{0:T(128)S(1)} %stack.23.where_ref, bf16[64,2048]{1,0:T(8,128)(2,1)S(1)} %get-tuple-element.87.feats_ref, ...), custom_call_target="tpu_custom_call" | custom-call | flops 2000000000 | bytes 1048576 | tf_op jit(solution)/shard_map/pallas_call | solution.py:518
  5.8 2.7 %shard_map.146 = (f32[2,512,128]{2,1,0:T(8,128)S(1)}, f32[8,128]{1,0:T(8,128)S(1)}, bf16[2,512,512]{2,1,0:T(8,128)(2,1)S(1)}, f32[2,8,2048]{2,1,0:T(8,128)S(1)}, s32[2,8,512]{2,1,0:T(8,128)S(1)}) custom-call(s32[5]{0:T(128)S(1)} %stack.23.where_ref, bf16[80,2048]{1,0:T(8,128)(2,1)S(1)} %collective-permute-done.got_ref, ...), custom_call_target="tpu_custom_call" | custom-call | flops 2000000000 | bytes 1048576 | tf_op jit(solution)/shard_map/pallas_call | solution.py:518
  8.5 4.4 %collective-permute-start.4 = (f32[8,128]{1,0:T(8,128)S(1)}, f32[8,128]{1,0:T(8,128)S(1)}, u32[]{:S(2)}, u32[]{:S(2)}) collective-permute-start(f32[8,128]{1,0:T(8,128)S(1)} %get-tuple-element.96.refs_0_.refs_16_), channel_id=1, source_target_pairs={{0,6},{1,7},{2,4},{3,5},{4,2},{5,3},{6,0},{7,1},{8,14},{9,15},{10,... | collective-permute-start | bytes 12296 | tf_op jit(solution)/shard_map/ppermute | solution.py:533
  13.9 2.4 %collective-permute-done.3.refs_2_.refs_18_ = f32[8,128]{1,0:T(8,128)S(1)} collective-permute-done((f32[8,128]{1,0:T(8,128)S(1)}, f32[8,128]{1,0:T(8,128)S(1)}, u32[]{:S(2)}, u32[]{:S(2)}) %collective-permute-start.3) | collective-permute-done | bytes 4128 | tf_op jit(solution)/shard_map/ppermute | solution.py:533
  16.3 6.4 %shard_map.148 = (bf16[2,512,128]{2,1,0:T(8,128)(2,1)S(1)}, f32[2,512,128]{2,1,0:T(8,128)S(1)}, f32[8,128]{1,0:T(8,128)S(1)}) custom-call(s32[5]{0:T(128)S(1)} %stack.23.where_ref, f32[2,512,128]{2,1,0:T(8,128)S(1)} %get-tuple-element.93.hidden_ref.refs_2_, s32[2,27,512]{2,1,0:T(8,128)S(1)} %shard_map.147.near_ref.refs_4_, ...), custom_call_target="tpu_custom_call" | custom-call | flops 14495514624 | bytes 1048576 | tf_op jit(solution)/shard_map/pallas_call | solution.py:518
  22.7 1.5 %collective-permute-start.7 = (f32[8,128]{1,0:T(8,128)S(1)}, f32[8,128]{1,0:T(8,128)S(1)}, u32[]{:S(2)}, u32[]{:S(2)}) collective-permute-start(f32[8,128]{1,0:T(8,128)S(1)} %get-tuple-element.98.refs_0_.refs_16_.refs_8_), channel_id=1, source_target_pairs={{0,6},{1,7},{2,4},{3,5},{4,2},{5,3},{6,0},{7,1},{8,14},{9,15},{10,... | collective-permute-start | bytes 12296 | tf_op jit(solution)/shard_map/ppermute | solution.py:533
  24.3 2.0 %collective-permute-start.5 = (f32[8,128]{1,0:T(8,128)S(1)}, f32[8,128]{1,0:T(8,128)S(1)}, u32[]{:S(2)}, u32[]{:S(2)}) collective-permute-start(f32[8,128]{1,0:T(8,128)S(1)} %get-tuple-element.98.refs_0_.refs_16_.refs_8_), channel_id=1, source_target_pairs={{0,2},{1,3},{2,0},{3,1},{4,6},{5,7},{6,4},{7,5},{8,10},{9,11},{10,... | collective-permute-start | bytes 12296 | tf_op jit(solution)/shard_map/ppermute | solution.py:533
  26.9 2.8 %collective-permute-start.8 = (bf16[512,128]{1,0:T(8,128)(2,1)S(1)}, bf16[512,128]{1,0:T(8,128)(2,1)S(1)}, u32[]{:S(2)}, u32[]{:S(2)}) collective-permute-start(bf16[512,128]{1,0:T(8,128)(2,1)S(1)} %get-tuple-element.102), channel_id=1, source_target_pairs={{0,1},{1,0},{2,3},{3,2},{4,5},{5,4},{6,7},{7,6},{8,9},{9,8},{10,11... | collective-permute-start | bytes 393224 | tf_op jit(solution)/shard_map/ppermute | solution.py:533
  29.7 6.6 %shard_map.149 = (bf16[2,512,128]{2,1,0:T(8,128)(2,1)S(1)}, bf16[2,512,128]{2,1,0:T(8,128)(2,1)S(1)}, f32[8,128]{1,0:T(8,128)S(1)}) custom-call(s32[5]{0:T(128)S(1)} %stack.23.where_ref, f32[2,512,128]{2,1,0:T(8,128)S(1)} %get-tuple-element.97.hidden_ref.refs_2_.refs_1_, s32[2,27,512]{2,1,0:T(8,128)S(1)} %shard_map.147.near_ref.refs_4_, ...), custom_call_target="tpu_custom_call" | custom-call | flops 14495514624 | bytes 1048576 | tf_op jit(solution)/shard_map/pallas_call | solution.py:518
  36.3 1.2 collective-permute-start.11
  37.5 2.4 %collective-permute-start.9 = (f32[8,128]{1,0:T(8,128)S(1)}, f32[8,128]{1,0:T(8,128)S(1)}, u32[]{:S(2)}, u32[]{:S(2)}) collective-permute-start(f32[8,128]{1,0:T(8,128)S(1)} %get-tuple-element.103.refs_0_.refs_8_), channel_id=1, source_target_pairs={{0,2},{1,3},{2,0},{3,1},{4,6},{5,7},{6,4},{7,5},{8,10},{9,11},{10,... | collective-permute-start | bytes 12296 | tf_op jit(solution)/shard_map/ppermute | solution.py:533
  40.9 1.2 shard_map.151
  42.1 2.1 %collective-permute-start.14 = (f32[8,128]{1,0:T(8,128)S(1)}, f32[8,128]{1,0:T(8,128)S(1)}, u32[]{:S(2)}, u32[]{:S(2)}) collective-permute-start(f32[8,128]{1,0:T(8,128)S(1)} %get-tuple-element.106.refs_12_), channel_id=1, source_target_pairs={{0,6},{1,7},{2,4},{3,5},{4,2},{5,3},{6,0},{7,1},{8,14},{9,15},{10,... | collective-permute-start | bytes 12296 | tf_op jit(solution)/shard_map/ppermute | solution.py:533
  44.8 0.9 collective-permute-start.12
  45.8 4.3 %collective-permute-start.16 = (bf16[512,128]{1,0:T(8,128)(2,1)S(1)}, bf16[512,128]{1,0:T(8,128)(2,1)S(1)}, u32[]{:S(2)}, u32[]{:S(2)}) collective-permute-start(bf16[512,128]{1,0:T(8,128)(2,1)S(1)} %get-tuple-element.109), channel_id=1, source_target_pairs={{0,1},{1,0},{2,3},{3,2},{4,5},{5,4},{6,7},{7,6},{8,9},{9,8},{10,11... | collective-permute-start | bytes 393224 | tf_op jit(solution)/shard_map/ppermute | solution.py:533
  50.1 7.6 %shard_map.152 = (f32[2,512,128]{2,1,0:T(8,128)S(1)}, f32[8,128]{1,0:T(8,128)S(1)}, bf16[1792,128]{1,0:T(8,128)(2,1)S(1)}, bf16[1792,128]{1,0:T(8,128)(2,1)S(1)}) custom-call(s32[5]{0:T(128)S(1)} %stack.23.where_ref, f32[2,512,128]{2,1,0:T(8,128)S(1)} %get-tuple-element.104.refs_0_.refs_20_, bf16[2,512,128]{2,1,0:T(8,128)(2,1)S(1)} %get-tuple-element.99.hidden_ref.refs_1_, ...), custom_call_target="tpu_custom_call" | custom-call | flops 14495514624 | bytes 1048576 | tf_op jit(solution)/shard_map/pallas_call | solution.py:518
  57.7 1.2 collective-permute-start.19
  58.9 2.4 %collective-permute-start.17 = (f32[8,128]{1,0:T(8,128)S(1)}, f32[8,128]{1,0:T(8,128)S(1)}, u32[]{:S(2)}, u32[]{:S(2)}) collective-permute-start(f32[8,128]{1,0:T(8,128)S(1)} %get-tuple-element.112.refs_12_.refs_8_), channel_id=1, source_target_pairs={{0,2},{1,3},{2,0},{3,1},{4,6},{5,7},{6,4},{7,5},{8,10},{9,11},{10,... | collective-permute-start | bytes 12296 | tf_op jit(solution)/shard_map/ppermute | solution.py:533
  61.3 2.4 %collective-permute-start.15 = (bf16[1792,128]{1,0:T(8,128)(2,1)S(1)}, bf16[1792,128]{1,0:T(8,128)(2,1)S(1)}, u32[]{:S(2)}, u32[]{:S(2)}) collective-permute-start(bf16[1792,128]{1,0:T(8,128)(2,1)S(1)} %get-tuple-element.108), channel_id=1, source_target_pairs={{0,1},{1,0},{2,3},{3,2},{4,5},{5,4},{6,7},{7,6},{8,9},{9,8},{10,11... | collective-permute-start | bytes 1376264 | tf_op jit(solution)/shard_map/ppermute | solution.py:533
  63.7 7.8 %shard_map.153 = (f32[2,512,128]{2,1,0:T(8,128)S(1)}, f32[8,128]{1,0:T(8,128)S(1)}, bf16[1792,128]{1,0:T(8,128)(2,1)S(1)}, bf16[1792,128]{1,0:T(8,128)(2,1)S(1)}) custom-call(s32[5]{0:T(128)S(1)} %stack.23.where_ref, f32[2,512,128]{2,1,0:T(8,128)S(1)} %get-tuple-element.111.refs_0_, f32[2,512,128]{2,1,0:T(8,128)S(1)} %get-tuple-element.97.hidden_ref.refs_2_.refs_1_, ...), custom_call_target="tpu_custom_call" | custom-call | flops 14495514624 | bytes 1048576 | tf_op jit(solution)/shard_map/pallas_call | solution.py:518
  71.5 2.7 %collective-permute-start.20 = (bf16[1792,128]{1,0:T(8,128)(2,1)S(1)}, bf16[1792,128]{1,0:T(8,128)(2,1)S(1)}, u32[]{:S(2)}, u32[]{:S(2)}) collective-permute-start(bf16[1792,128]{1,0:T(8,128)(2,1)S(1)} %get-tuple-element.114), channel_id=1, source_target_pairs={{0,1},{1,0},{2,3},{3,2},{4,5},{5,4},{6,7},{7,6},{8,9},{9,8},{10,11... | collective-permute-start | bytes 1376264 | tf_op jit(solution)/shard_map/ppermute | solution.py:533
  74.3 1.4 %collective-permute-done.20.refs_3_ = bf16[1792,128]{1,0:T(8,128)(2,1)S(1)} collective-permute-done((bf16[1792,128]{1,0:T(8,128)(2,1)S(1)}, bf16[1792,128]{1,0:T(8,128)(2,1)S(1)}, u32[]{:S(2)}, u32[]{:S(2)}) %collective-permute-start.20) | collective-permute-done | bytes 458784 | tf_op jit(solution)/shard_map/ppermute | solution.py:533
  76.5 2.2 %collective-permute-start.21 = (bf16[896,128]{1,0:T(8,128)(2,1)S(1)}, bf16[896,128]{1,0:T(8,128)(2,1)S(1)}, u32[]{:S(2)}, u32[]{:S(2)}) collective-permute-start(bf16[896,128]{1,0:T(8,128)(2,1)S(1)} %get-tuple-element.116), channel_id=1, source_target_pairs={{0,24},{8,16},{16,8},{24,0},{1,25},{9,17},{17,9},{25,1},{2,26},{10... | collective-permute-start | bytes 688136 | tf_op jit(solution)/shard_map/ppermute | solution.py:533
  79.2 1.1 collective-permute-start.26
  81.0 2.4 %collective-permute-done.26.refs_7_ = f32[8,128]{1,0:T(8,128)S(1)} collective-permute-done((f32[8,128]{1,0:T(8,128)S(1)}, f32[8,128]{1,0:T(8,128)S(1)}, u32[]{:S(2)}, u32[]{:S(2)}) %collective-permute-start.26) | collective-permute-done | bytes 4128 | tf_op jit(solution)/shard_map/ppermute | solution.py:533
  84.0 2.2 %collective-permute-done.24.refs_5_ = f32[8,128]{1,0:T(8,128)S(1)} collective-permute-done((f32[8,128]{1,0:T(8,128)S(1)}, f32[8,128]{1,0:T(8,128)S(1)}, u32[]{:S(2)}, u32[]{:S(2)}) %collective-permute-start.24) | collective-permute-done | bytes 4128 | tf_op jit(solution)/shard_map/ppermute | solution.py:533
  86.2 1.1 shard_map.155
  87.3 3.3 %collective-permute-start.27 = (bf16[256,128]{1,0:T(8,128)(2,1)S(1)}, bf16[256,128]{1,0:T(8,128)(2,1)S(1)}, u32[]{:S(2)}, u32[]{:S(2)}) collective-permute-start(bf16[256,128]{1,0:T(8,128)(2,1)S(1)} %get-tuple-element.123), channel_id=1, source_target_pairs={{0,1},{1,0},{2,3},{3,2},{4,5},{5,4},{6,7},{7,6},{8,9},{9,8},{10,11... | collective-permute-start | bytes 196616 | tf_op jit(solution)/shard_map/ppermute | solution.py:533
  90.6 0.9 collective-permute-done.27.refs_5_
  92.2 1.2 collective-permute-start.28
  93.4 2.4 %collective-permute-start.30 = (bf16[288,128]{1,0:T(8,128)(2,1)S(1)}, bf16[288,128]{1,0:T(8,128)(2,1)S(1)}, u32[]{:S(2)}, u32[]{:S(2)}) collective-permute-start(bf16[288,128]{1,0:T(8,128)(2,1)S(1)} %get-tuple-element.132), channel_id=1, source_target_pairs={{0,2},{1,3},{2,0},{3,1},{4,6},{5,7},{6,4},{7,5},{8,10},{9,11},{10,... | collective-permute-start | bytes 221192 | tf_op jit(solution)/shard_map/ppermute | solution.py:533
  95.8 3.2 %shard_map.157 = (bf16[64,2048]{1,0:T(8,128)(2,1)S(1)}, bf16[64,2048]{1,0:T(8,128)(2,1)S(1)}) custom-call(s32[5]{0:T(128)S(1)} %stack.23.where_ref, bf16[2,512,128]{2,1,0:T(8,128)(2,1)S(1)} %get-tuple-element.133.rows_ref, f32[2,8,2048]{2,1,0:T(8,128)S(1)} %get-tuple-element.134.which_ref, s32[2,8,512]{2,1,0:T(8,128)S(1)} %get-tuple-element.135.tables_ref, ...), custom_call_target="tpu_custom_call" | custom-call | bytes 1 | tf_op jit(solution)/shard_map/pallas_call | solution.py:518
  99.0 2.4 %collective-permute-done.29.refs_2_ = bf16[288,128]{1,0:T(8,128)(2,1)S(1)} collective-permute-done((bf16[288,128]{1,0:T(8,128)(2,1)S(1)}, bf16[288,128]{1,0:T(8,128)(2,1)S(1)}, u32[]{:S(2)}, u32[]{:S(2)}) %collective-permute-start.29) | collective-permute-done | bytes 73760 | tf_op jit(solution)/shard_map/ppermute | solution.py:533
  102.1 1.4 %collective-permute-start.32 = (bf16[288,128]{1,0:T(8,128)(2,1)S(1)}, bf16[288,128]{1,0:T(8,128)(2,1)S(1)}, u32[]{:S(2)}, u32[]{:S(2)}) collective-permute-start(bf16[288,128]{1,0:T(8,128)(2,1)S(1)} %shard_map.158.refs_0_), channel_id=1, source_target_pairs={{0,4},{1,5},{2,6},{3,7},{4,0},{5,1},{6,2},{7,3},{8,12},{9,13},{10,... | collective-permute-start | bytes 221192 | tf_op jit(solution)/shard_map/ppermute | solution.py:533
  103.5 2.1 %collective-permute-start.31 = (bf16[288,128]{1,0:T(8,128)(2,1)S(1)}, bf16[288,128]{1,0:T(8,128)(2,1)S(1)}, u32[]{:S(2)}, u32[]{:S(2)}) collective-permute-start(bf16[288,128]{1,0:T(8,128)(2,1)S(1)} %shard_map.158.refs_0_), channel_id=1, source_target_pairs={{0,6},{1,7},{2,4},{3,5},{4,2},{5,3},{6,0},{7,1},{8,14},{9,15},{10,... | collective-permute-start | bytes 221192 | tf_op jit(solution)/shard_map/ppermute | solution.py:533
  105.6 1.3 %collective-permute-start.34 = (f32[8,128]{1,0:T(8,128)S(1)}, f32[8,128]{1,0:T(8,128)S(1)}, u32[]{:S(2)}, u32[]{:S(2)}) collective-permute-start(f32[8,128]{1,0:T(8,128)S(1)} %get-tuple-element.142.refs_4_), channel_id=1, source_target_pairs={{0,1},{1,0},{2,3},{3,2},{4,5},{5,4},{6,7},{7,6},{8,9},{9,8},{10,11... | collective-permute-start | bytes 12296 | tf_op jit(solution)/shard_map/ppermute | solution.py:533
  106.9 0.8 collective-permute-done.34.refs_5_
  107.8 1.4 %collective-permute-done.31.refs_1_ = bf16[288,128]{1,0:T(8,128)(2,1)S(1)} collective-permute-done((bf16[288,128]{1,0:T(8,128)(2,1)S(1)}, bf16[288,128]{1,0:T(8,128)(2,1)S(1)}, u32[]{:S(2)}, u32[]{:S(2)}) %collective-permute-start.31) | collective-permute-done | bytes 73760 | tf_op jit(solution)/shard_map/ppermute | solution.py:533
  109.8 1.3 collective-permute-start.37
  111.0 1.2 collective-permute-start.36
  112.5 3.3 %collective-permute-start.38 = (bf16[64,2048]{1,0:T(8,128)(2,1)S(1)}, bf16[64,2048]{1,0:T(8,128)(2,1)S(1)}, u32[]{:S(2)}, u32[]{:S(2)}) collective-permute-start(bf16[64,2048]{1,0:T(8,128)(2,1)S(1)} %get-tuple-element.146), channel_id=1, source_target_pairs={{0,1},{1,0},{2,3},{3,2},{4,5},{5,4},{6,7},{7,6},{8,9},{9,8},{10,11... | collective-permute-start | bytes 786440 | tf_op jit(solution)/shard_map/ppermute | solution.py:533
  115.8 1.2 collective-permute-done.38.other_input
  117.0 1.5 %shard_map.160 = (bf16[2,512,128]{2,1,0:T(8,128)(2,1)}, bf16[2,64,2048]{2,1,0:T(8,128)(2,1)}) custom-call(s32[5]{0:T(128)S(1)} %stack.23.where_ref, bf16[512,128]{1,0:T(8,128)(2,1)S(1)} %get-tuple-element.143.own_features, bf16[512,128]{1,0:T(8,128)(2,1)S(1)} %collective-permute-done.16.other_features, bf16[64,2048]{1,0:T(8,128)(2,1)S(1)} %get-tuple-element.145.own_input, ...), custom_call_target="tpu_custom_call" | custom-call | bytes 1 | tf_op jit(solution)/shard_map/pallas_call | solution.py:518
  118.5 4.8 %collective-permute-done.35.refs_1_ = bf16[1168,128]{1,0:T(8,128)(2,1)S(1)} collective-permute-done((bf16[1168,128]{1,0:T(8,128)(2,1)S(1)}, bf16[1168,128]{1,0:T(8,128)(2,1)S(1)}, u32[]{:S(2)}, u32[]{:S(2)}) %collective-permute-start.35) | collective-permute-done | bytes 299040 | tf_op jit(solution)/shard_map/ppermute | solution.py:533
  123.3 3.7 %collective-permute-start.40 = (bf16[1168,128]{1,0:T(8,128)(2,1)S(1)}, bf16[1168,128]{1,0:T(8,128)(2,1)S(1)}, u32[]{:S(2)}, u32[]{:S(2)}) collective-permute-start(bf16[1168,128]{1,0:T(8,128)(2,1)S(1)} %collective-permute-done.35.refs_1_), channel_id=1, source_target_pairs={{0,1},{1,0},{2,3},{3,2},{4,5},{5,4},{6,7},{7,6},{8,9},{9,8},{10,11... | collective-permute-start | bytes 897032 | tf_op jit(solution)/shard_map/ppermute | solution.py:533
  127.5 2.4 %shard_map.161 = (f32[3456,128]{1,0:T(8,128)}, f32[3456,128]{1,0:T(8,128)}, f32[512,128]{1,0:T(8,128)}, f32[3,128]{1,0:T(4,128)}, f32[3,128]{1,0:T(4,128)}) custom-call(s32[5]{0:T(128)S(1)} %stack.23.where_ref, bf16[1168,128]{1,0:T(8,128)(2,1)S(1)} %shard_map.159.refs_0_, bf16[1168,128]{1,0:T(8,128)(2,1)S(1)} %collective-permute-done.35.refs_1_, ...), custom_call_target="tpu_custom_call" | custom-call | flops 1000000000 | bytes 1048576 | tf_op jit(solution)/shard_map/pallas_call | solution.py:518
  130.0 1.9 %shard_map.162 = (f32[3456,128]{1,0:T(8,128)}, f32[3456,128]{1,0:T(8,128)}, f32[512,128]{1,0:T(8,128)}) custom-call(s32[5]{0:T(128)S(1)} %stack.23.where_ref, bf16[1168,128]{1,0:T(8,128)(2,1)S(1)} %collective-permute-done.39.refs_0_, ...), custom_call_target="tpu_custom_call", output_to_operand_aliasing={{0}: (5, {}), {1}: (6, {}), {2}: (7, {})} | custom-call | flops 1000000000 | bytes 1048576 | tf_op jit(solution)/shard_map/pallas_call | solution.py:518
  (70 shorter events, 9.1 us)
Async XLA Ops:
  2.4 3.3 %collective-permute-start = (bf16[80,2048]{1,0:T(8,128)(2,1)S(1)}, bf16[80,2048]{1,0:T(8,128)(2,1)S(1)}, u32[]{:S(2)}, u32[]{:S(2)}) collective-permute-start(bf16[80,2048]{1,0:T(8,128)(2,1)S(1)} %get-tuple-element.85), channel_id=1, source_target_pairs={{0,1},{1,0},{2,3},{3,2},{4,5},{5,4},{6,7},{7,6},{8,9},{9,8},{10,11... | collective-permute-start | bytes 983048 | tf_op jit(solution)/shard_map/ppermute | solution.py:533
  5.2 8.0 %collective-permute-start.1 = (s32[27,512]{1,0:T(8,128)S(1)}, s32[27,512]{1,0:T(8,128)S(1)}, u32[]{:S(2)}, u32[]{:S(2)}) collective-permute-start(s32[27,512]{1,0:T(8,128)S(1)} %get-tuple-element.95), channel_id=1, source_target_pairs={{0,1},{1,0},{2,3},{3,2},{4,5},{5,4},{6,7},{7,6},{8,9},{9,8},{10,11... | collective-permute-start | bytes 165896 | tf_op jit(solution)/shard_map/ppermute | solution.py:533
  5.8 10.5 %copy-start.2 = (bf16[27,128,128]{2,1,0:T(8,128)(2,1)S(1)}, bf16[27,128,128]{2,1,0:T(8,128)(2,1)}, u32[]{:S(2)}) copy-start(bf16[27,128,128]{2,1,0:T(8,128)(2,1)} %refs_5_.3) | copy-start | bytes 2654212
  5.8 10.5 %copy-start.4 = (f32[3,128]{1,0:T(4,128)S(1)}, f32[3,128]{1,0:T(4,128)}, u32[]{:S(2)}) copy-start(f32[3,128]{1,0:T(4,128)} %refs_7_.3) | copy-start | bytes 4612
  5.8 10.5 %copy-start.5 = (f32[3,128]{1,0:T(4,128)S(1)}, f32[3,128]{1,0:T(4,128)}, u32[]{:S(2)}) copy-start(f32[3,128]{1,0:T(4,128)} %scale_ref.7) | copy-start | bytes 4612
  8.5 5.4 %collective-permute-start.4 = (f32[8,128]{1,0:T(8,128)S(1)}, f32[8,128]{1,0:T(8,128)S(1)}, u32[]{:S(2)}, u32[]{:S(2)}) collective-permute-start(f32[8,128]{1,0:T(8,128)S(1)} %get-tuple-element.96.refs_0_.refs_16_), channel_id=1, source_target_pairs={{0,6},{1,7},{2,4},{3,5},{4,2},{5,3},{6,0},{7,1},{8,14},{9,15},{10,... | collective-permute-start | bytes 12296 | tf_op jit(solution)/shard_map/ppermute | solution.py:533
  12.9 3.4 %collective-permute-start.3 = (f32[8,128]{1,0:T(8,128)S(1)}, f32[8,128]{1,0:T(8,128)S(1)}, u32[]{:S(2)}, u32[]{:S(2)}) collective-permute-start(f32[8,128]{1,0:T(8,128)S(1)} %get-tuple-element.96.refs_0_.refs_16_), channel_id=1, source_target_pairs={{0,4},{1,5},{2,6},{3,7},{4,0},{5,1},{6,2},{7,3},{8,12},{9,13},{10,... | collective-permute-start | bytes 12296 | tf_op jit(solution)/shard_map/ppermute | solution.py:533
  12.9 3.4 %collective-permute-start.2 = (f32[8,128]{1,0:T(8,128)S(1)}, f32[8,128]{1,0:T(8,128)S(1)}, u32[]{:S(2)}, u32[]{:S(2)}) collective-permute-start(f32[8,128]{1,0:T(8,128)S(1)} %get-tuple-element.96.refs_0_.refs_16_), channel_id=1, source_target_pairs={{0,2},{1,3},{2,0},{3,1},{4,6},{5,7},{6,4},{7,5},{8,10},{9,11},{10,... | collective-permute-start | bytes 12296 | tf_op jit(solution)/shard_map/ppermute | solution.py:533
  16.3 10.0 %copy-start = (bf16[8,512,128]{2,1,0:T(8,128)(2,1)S(1)}, bf16[8,512,128]{2,1,0:T(8,128)(2,1)}, u32[]{:S(2)}) copy-start(bf16[8,512,128]{2,1,0:T(8,128)(2,1)} %grad_ref.1) | copy-start | bytes 3145732
  16.3 13.4 %copy-start.1 = (bf16[27,128,128]{2,1,0:T(8,128)(2,1)S(1)}, bf16[27,128,128]{2,1,0:T(8,128)(2,1)}, u32[]{:S(2)}) copy-start(bf16[27,128,128]{2,1,0:T(8,128)(2,1)} %refs_5_.2) | copy-start | bytes 2654212
  22.7 7.0 %collective-permute-start.7 = (f32[8,128]{1,0:T(8,128)S(1)}, f32[8,128]{1,0:T(8,128)S(1)}, u32[]{:S(2)}, u32[]{:S(2)}) collective-permute-start(f32[8,128]{1,0:T(8,128)S(1)} %get-tuple-element.98.refs_0_.refs_16_.refs_8_), channel_id=1, source_target_pairs={{0,6},{1,7},{2,4},{3,5},{4,2},{5,3},{6,0},{7,1},{8,14},{9,15},{10,... | collective-permute-start | bytes 12296 | tf_op jit(solution)/shard_map/ppermute | solution.py:533
  24.2 5.4 %collective-permute-start.6 = (f32[8,128]{1,0:T(8,128)S(1)}, f32[8,128]{1,0:T(8,128)S(1)}, u32[]{:S(2)}, u32[]{:S(2)}) collective-permute-start(f32[8,128]{1,0:T(8,128)S(1)} %get-tuple-element.98.refs_0_.refs_16_.refs_8_), channel_id=1, source_target_pairs={{0,4},{1,5},{2,6},{3,7},{4,0},{5,1},{6,2},{7,3},{8,12},{9,13},{10,... | collective-permute-start | bytes 12296 | tf_op jit(solution)/shard_map/ppermute | solution.py:533
  24.3 5.4 %collective-permute-start.5 = (f32[8,128]{1,0:T(8,128)S(1)}, f32[8,128]{1,0:T(8,128)S(1)}, u32[]{:S(2)}, u32[]{:S(2)}) collective-permute-start(f32[8,128]{1,0:T(8,128)S(1)} %get-tuple-element.98.refs_0_.refs_16_.refs_8_), channel_id=1, source_target_pairs={{0,2},{1,3},{2,0},{3,1},{4,6},{5,7},{6,4},{7,5},{8,10},{9,11},{10,... | collective-permute-start | bytes 12296 | tf_op jit(solution)/shard_map/ppermute | solution.py:533
  26.9 13.0 %collective-permute-start.8 = (bf16[512,128]{1,0:T(8,128)(2,1)S(1)}, bf16[512,128]{1,0:T(8,128)(2,1)S(1)}, u32[]{:S(2)}, u32[]{:S(2)}) collective-permute-start(bf16[512,128]{1,0:T(8,128)(2,1)S(1)} %get-tuple-element.102), channel_id=1, source_target_pairs={{0,1},{1,0},{2,3},{3,2},{4,5},{5,4},{6,7},{7,6},{8,9},{9,8},{10,11... | collective-permute-start | bytes 393224 | tf_op jit(solution)/shard_map/ppermute | solution.py:533
  36.3 4.3 %collective-permute-start.11 = (f32[8,128]{1,0:T(8,128)S(1)}, f32[8,128]{1,0:T(8,128)S(1)}, u32[]{:S(2)}, u32[]{:S(2)}) collective-permute-start(f32[8,128]{1,0:T(8,128)S(1)} %get-tuple-element.103.refs_0_.refs_8_), channel_id=1, source_target_pairs={{0,6},{1,7},{2,4},{3,5},{4,2},{5,3},{6,0},{7,1},{8,14},{9,15},{10,... | collective-permute-start | bytes 12296 | tf_op jit(solution)/shard_map/ppermute | solution.py:533
  37.5 3.4 %collective-permute-start.10 = (f32[8,128]{1,0:T(8,128)S(1)}, f32[8,128]{1,0:T(8,128)S(1)}, u32[]{:S(2)}, u32[]{:S(2)}) collective-permute-start(f32[8,128]{1,0:T(8,128)S(1)} %get-tuple-element.103.refs_0_.refs_8_), channel_id=1, source_target_pairs={{0,4},{1,5},{2,6},{3,7},{4,0},{5,1},{6,2},{7,3},{8,12},{9,13},{10,... | collective-permute-start | bytes 12296 | tf_op jit(solution)/shard_map/ppermute | solution.py:533
  37.5 3.4 %collective-permute-start.9 = (f32[8,128]{1,0:T(8,128)S(1)}, f32[8,128]{1,0:T(8,128)S(1)}, u32[]{:S(2)}, u32[]{:S(2)}) collective-permute-start(f32[8,128]{1,0:T(8,128)S(1)} %get-tuple-element.103.refs_0_.refs_8_), channel_id=1, source_target_pairs={{0,2},{1,3},{2,0},{3,1},{4,6},{5,7},{6,4},{7,5},{8,10},{9,11},{10,... | collective-permute-start | bytes 12296 | tf_op jit(solution)/shard_map/ppermute | solution.py:533
  42.1 7.9 %collective-permute-start.14 = (f32[8,128]{1,0:T(8,128)S(1)}, f32[8,128]{1,0:T(8,128)S(1)}, u32[]{:S(2)}, u32[]{:S(2)}) collective-permute-start(f32[8,128]{1,0:T(8,128)S(1)} %get-tuple-element.106.refs_12_), channel_id=1, source_target_pairs={{0,6},{1,7},{2,4},{3,5},{4,2},{5,3},{6,0},{7,1},{8,14},{9,15},{10,... | collective-permute-start | bytes 12296 | tf_op jit(solution)/shard_map/ppermute | solution.py:533
  44.3 5.8 %collective-permute-start.13 = (f32[8,128]{1,0:T(8,128)S(1)}, f32[8,128]{1,0:T(8,128)S(1)}, u32[]{:S(2)}, u32[]{:S(2)}) collective-permute-start(f32[8,128]{1,0:T(8,128)S(1)} %get-tuple-element.106.refs_12_), channel_id=1, source_target_pairs={{0,4},{1,5},{2,6},{3,7},{4,0},{5,1},{6,2},{7,3},{8,12},{9,13},{10,... | collective-permute-start | bytes 12296 | tf_op jit(solution)/shard_map/ppermute | solution.py:533
  44.8 5.3 %collective-permute-start.12 = (f32[8,128]{1,0:T(8,128)S(1)}, f32[8,128]{1,0:T(8,128)S(1)}, u32[]{:S(2)}, u32[]{:S(2)}) collective-permute-start(f32[8,128]{1,0:T(8,128)S(1)} %get-tuple-element.106.refs_12_), channel_id=1, source_target_pairs={{0,2},{1,3},{2,0},{3,1},{4,6},{5,7},{6,4},{7,5},{8,10},{9,11},{10,... | collective-permute-start | bytes 12296 | tf_op jit(solution)/shard_map/ppermute | solution.py:533
  45.8 17.9 %collective-permute-start.16 = (bf16[512,128]{1,0:T(8,128)(2,1)S(1)}, bf16[512,128]{1,0:T(8,128)(2,1)S(1)}, u32[]{:S(2)}, u32[]{:S(2)}) collective-permute-start(bf16[512,128]{1,0:T(8,128)(2,1)S(1)} %get-tuple-element.109), channel_id=1, source_target_pairs={{0,1},{1,0},{2,3},{3,2},{4,5},{5,4},{6,7},{7,6},{8,9},{9,8},{10,11... | collective-permute-start | bytes 393224 | tf_op jit(solution)/shard_map/ppermute | solution.py:533
  57.7 6.0 %collective-permute-start.19 = (f32[8,128]{1,0:T(8,128)S(1)}, f32[8,128]{1,0:T(8,128)S(1)}, u32[]{:S(2)}, u32[]{:S(2)}) collective-permute-start(f32[8,128]{1,0:T(8,128)S(1)} %get-tuple-element.112.refs_12_.refs_8_), channel_id=1, source_target_pairs={{0,6},{1,7},{2,4},{3,5},{4,2},{5,3},{6,0},{7,1},{8,14},{9,15},{10,... | collective-permute-start | bytes 12296 | tf_op jit(solution)/shard_map/ppermute | solution.py:533
  58.9 4.8 %collective-permute-start.18 = (f32[8,128]{1,0:T(8,128)S(1)}, f32[8,128]{1,0:T(8,128)S(1)}, u32[]{:S(2)}, u32[]{:S(2)}) collective-permute-start(f32[8,128]{1,0:T(8,128)S(1)} %get-tuple-element.112.refs_12_.refs_8_), channel_id=1, source_target_pairs={{0,4},{1,5},{2,6},{3,7},{4,0},{5,1},{6,2},{7,3},{8,12},{9,13},{10,... | collective-permute-start | bytes 12296 | tf_op jit(solution)/shard_map/ppermute | solution.py:533
  58.9 4.8 %collective-permute-start.17 = (f32[8,128]{1,0:T(8,128)S(1)}, f32[8,128]{1,0:T(8,128)S(1)}, u32[]{:S(2)}, u32[]{:S(2)}) collective-permute-start(f32[8,128]{1,0:T(8,128)S(1)} %get-tuple-element.112.refs_12_.refs_8_), channel_id=1, source_target_pairs={{0,2},{1,3},{2,0},{3,1},{4,6},{5,7},{6,4},{7,5},{8,10},{9,11},{10,... | collective-permute-start | bytes 12296 | tf_op jit(solution)/shard_map/ppermute | solution.py:533
  61.3 13.0 %collective-permute-start.15 = (bf16[1792,128]{1,0:T(8,128)(2,1)S(1)}, bf16[1792,128]{1,0:T(8,128)(2,1)S(1)}, u32[]{:S(2)}, u32[]{:S(2)}) collective-permute-start(bf16[1792,128]{1,0:T(8,128)(2,1)S(1)} %get-tuple-element.108), channel_id=1, source_target_pairs={{0,1},{1,0},{2,3},{3,2},{4,5},{5,4},{6,7},{7,6},{8,9},{9,8},{10,11... | collective-permute-start | bytes 1376264 | tf_op jit(solution)/shard_map/ppermute | solution.py:533
  71.5 4.2 %collective-permute-start.20 = (bf16[1792,128]{1,0:T(8,128)(2,1)S(1)}, bf16[1792,128]{1,0:T(8,128)(2,1)S(1)}, u32[]{:S(2)}, u32[]{:S(2)}) collective-permute-start(bf16[1792,128]{1,0:T(8,128)(2,1)S(1)} %get-tuple-element.114), channel_id=1, source_target_pairs={{0,1},{1,0},{2,3},{3,2},{4,5},{5,4},{6,7},{7,6},{8,9},{9,8},{10,11... | collective-permute-start | bytes 1376264 | tf_op jit(solution)/shard_map/ppermute | solution.py:533
  76.5 15.0 %collective-permute-start.21 = (bf16[896,128]{1,0:T(8,128)(2,1)S(1)}, bf16[896,128]{1,0:T(8,128)(2,1)S(1)}, u32[]{:S(2)}, u32[]{:S(2)}) collective-permute-start(bf16[896,128]{1,0:T(8,128)(2,1)S(1)} %get-tuple-element.116), channel_id=1, source_target_pairs={{0,24},{8,16},{16,8},{24,0},{1,25},{9,17},{17,9},{25,1},{2,26},{10... | collective-permute-start | bytes 688136 | tf_op jit(solution)/shard_map/ppermute | solution.py:533
  78.7 12.8 %collective-permute-start.22 = (bf16[896,128]{1,0:T(8,128)(2,1)S(1)}, bf16[896,128]{1,0:T(8,128)(2,1)S(1)}, u32[]{:S(2)}, u32[]{:S(2)}) collective-permute-start(bf16[896,128]{1,0:T(8,128)(2,1)S(1)} %get-tuple-element.117), channel_id=1, source_target_pairs={{0,16},{8,24},{16,0},{24,8},{1,17},{9,25},{17,1},{25,9},{2,18},{10... | collective-permute-start | bytes 688136 | tf_op jit(solution)/shard_map/ppermute | solution.py:533
  78.9 12.6 %collective-permute-start.23 = (bf16[896,128]{1,0:T(8,128)(2,1)S(1)}, bf16[896,128]{1,0:T(8,128)(2,1)S(1)}, u32[]{:S(2)}, u32[]{:S(2)}) collective-permute-start(bf16[896,128]{1,0:T(8,128)(2,1)S(1)} %get-tuple-element.118), channel_id=1, source_target_pairs={{0,8},{8,0},{16,24},{24,16},{1,9},{9,1},{17,25},{25,17},{2,10},{10... | collective-permute-start | bytes 688136 | tf_op jit(solution)/shard_map/ppermute | solution.py:533
  79.2 4.3 %collective-permute-start.26 = (f32[8,128]{1,0:T(8,128)S(1)}, f32[8,128]{1,0:T(8,128)S(1)}, u32[]{:S(2)}, u32[]{:S(2)}) collective-permute-start(f32[8,128]{1,0:T(8,128)S(1)} %get-tuple-element.121.refs_4_), channel_id=1, source_target_pairs={{0,6},{1,7},{2,4},{3,5},{4,2},{5,3},{6,0},{7,1},{8,14},{9,15},{10,... | collective-permute-start | bytes 12296 | tf_op jit(solution)/shard_map/ppermute | solution.py:533
  80.3 3.7 %collective-permute-start.25 = (f32[8,128]{1,0:T(8,128)S(1)}, f32[8,128]{1,0:T(8,128)S(1)}, u32[]{:S(2)}, u32[]{:S(2)}) collective-permute-start(f32[8,128]{1,0:T(8,128)S(1)} %get-tuple-element.121.refs_4_), channel_id=1, source_target_pairs={{0,4},{1,5},{2,6},{3,7},{4,0},{5,1},{6,2},{7,3},{8,12},{9,13},{10,... | collective-permute-start | bytes 12296 | tf_op jit(solution)/shard_map/ppermute | solution.py:533
  83.5 2.8 %collective-permute-start.24 = (f32[8,128]{1,0:T(8,128)S(1)}, f32[8,128]{1,0:T(8,128)S(1)}, u32[]{:S(2)}, u32[]{:S(2)}) collective-permute-start(f32[8,128]{1,0:T(8,128)S(1)} %get-tuple-element.121.refs_4_), channel_id=1, source_target_pairs={{0,2},{1,3},{2,0},{3,1},{4,6},{5,7},{6,4},{7,5},{8,10},{9,11},{10,... | collective-permute-start | bytes 12296 | tf_op jit(solution)/shard_map/ppermute | solution.py:533
  87.3 4.2 %collective-permute-start.27 = (bf16[256,128]{1,0:T(8,128)(2,1)S(1)}, bf16[256,128]{1,0:T(8,128)(2,1)S(1)}, u32[]{:S(2)}, u32[]{:S(2)}) collective-permute-start(bf16[256,128]{1,0:T(8,128)(2,1)S(1)} %get-tuple-element.123), channel_id=1, source_target_pairs={{0,1},{1,0},{2,3},{3,2},{4,5},{5,4},{6,7},{7,6},{8,9},{9,8},{10,11... | collective-permute-start | bytes 196616 | tf_op jit(solution)/shard_map/ppermute | solution.py:533
  92.2 6.8 %collective-permute-start.28 = (bf16[288,128]{1,0:T(8,128)(2,1)S(1)}, bf16[288,128]{1,0:T(8,128)(2,1)S(1)}, u32[]{:S(2)}, u32[]{:S(2)}) collective-permute-start(bf16[288,128]{1,0:T(8,128)(2,1)S(1)} %get-tuple-element.130), channel_id=1, source_target_pairs={{0,6},{1,7},{2,4},{3,5},{4,2},{5,3},{6,0},{7,1},{8,14},{9,15},{10,... | collective-permute-start | bytes 221192 | tf_op jit(solution)/shard_map/ppermute | solution.py:533
  93.4 8.0 %collective-permute-start.29 = (bf16[288,128]{1,0:T(8,128)(2,1)S(1)}, bf16[288,128]{1,0:T(8,128)(2,1)S(1)}, u32[]{:S(2)}, u32[]{:S(2)}) collective-permute-start(bf16[288,128]{1,0:T(8,128)(2,1)S(1)} %get-tuple-element.131), channel_id=1, source_target_pairs={{0,4},{1,5},{2,6},{3,7},{4,0},{5,1},{6,2},{7,3},{8,12},{9,13},{10,... | collective-permute-start | bytes 221192 | tf_op jit(solution)/shard_map/ppermute | solution.py:533
  93.4 8.0 %collective-permute-start.30 = (bf16[288,128]{1,0:T(8,128)(2,1)S(1)}, bf16[288,128]{1,0:T(8,128)(2,1)S(1)}, u32[]{:S(2)}, u32[]{:S(2)}) collective-permute-start(bf16[288,128]{1,0:T(8,128)(2,1)S(1)} %get-tuple-element.132), channel_id=1, source_target_pairs={{0,2},{1,3},{2,0},{3,1},{4,6},{5,7},{6,4},{7,5},{8,10},{9,11},{10,... | collective-permute-start | bytes 221192 | tf_op jit(solution)/shard_map/ppermute | solution.py:533
  102.0 5.8 %collective-permute-start.33 = (bf16[288,128]{1,0:T(8,128)(2,1)S(1)}, bf16[288,128]{1,0:T(8,128)(2,1)S(1)}, u32[]{:S(2)}, u32[]{:S(2)}) collective-permute-start(bf16[288,128]{1,0:T(8,128)(2,1)S(1)} %shard_map.158.refs_0_), channel_id=1, source_target_pairs={{0,2},{1,3},{2,0},{3,1},{4,6},{5,7},{6,4},{7,5},{8,10},{9,11},{10,... | collective-permute-start | bytes 221192 | tf_op jit(solution)/shard_map/ppermute | solution.py:533
  102.1 5.7 %collective-permute-start.32 = (bf16[288,128]{1,0:T(8,128)(2,1)S(1)}, bf16[288,128]{1,0:T(8,128)(2,1)S(1)}, u32[]{:S(2)}, u32[]{:S(2)}) collective-permute-start(bf16[288,128]{1,0:T(8,128)(2,1)S(1)} %shard_map.158.refs_0_), channel_id=1, source_target_pairs={{0,4},{1,5},{2,6},{3,7},{4,0},{5,1},{6,2},{7,3},{8,12},{9,13},{10,... | collective-permute-start | bytes 221192 | tf_op jit(solution)/shard_map/ppermute | solution.py:533
  103.5 5.7 %collective-permute-start.31 = (bf16[288,128]{1,0:T(8,128)(2,1)S(1)}, bf16[288,128]{1,0:T(8,128)(2,1)S(1)}, u32[]{:S(2)}, u32[]{:S(2)}) collective-permute-start(bf16[288,128]{1,0:T(8,128)(2,1)S(1)} %shard_map.158.refs_0_), channel_id=1, source_target_pairs={{0,6},{1,7},{2,4},{3,5},{4,2},{5,3},{6,0},{7,1},{8,14},{9,15},{10,... | collective-permute-start | bytes 221192 | tf_op jit(solution)/shard_map/ppermute | solution.py:533
  105.6 2.2 %collective-permute-start.34 = (f32[8,128]{1,0:T(8,128)S(1)}, f32[8,128]{1,0:T(8,128)S(1)}, u32[]{:S(2)}, u32[]{:S(2)}) collective-permute-start(f32[8,128]{1,0:T(8,128)S(1)} %get-tuple-element.142.refs_4_), channel_id=1, source_target_pairs={{0,1},{1,0},{2,3},{3,2},{4,5},{5,4},{6,7},{7,6},{8,9},{9,8},{10,11... | collective-permute-start | bytes 12296 | tf_op jit(solution)/shard_map/ppermute | solution.py:533
  109.8 8.7 %collective-permute-start.37 = (bf16[1168,128]{1,0:T(8,128)(2,1)S(1)}, bf16[1168,128]{1,0:T(8,128)(2,1)S(1)}, u32[]{:S(2)}, u32[]{:S(2)}) collective-permute-start(bf16[1168,128]{1,0:T(8,128)(2,1)S(1)} %shard_map.159.refs_0_), channel_id=1, source_target_pairs={{0,8},{8,0},{16,24},{24,16},{1,9},{9,1},{17,25},{25,17},{2,10},{10... | collective-permute-start | bytes 897032 | tf_op jit(solution)/shard_map/ppermute | solution.py:533
  111.0 7.4 %collective-permute-start.36 = (bf16[1168,128]{1,0:T(8,128)(2,1)S(1)}, bf16[1168,128]{1,0:T(8,128)(2,1)S(1)}, u32[]{:S(2)}, u32[]{:S(2)}) collective-permute-start(bf16[1168,128]{1,0:T(8,128)(2,1)S(1)} %shard_map.159.refs_0_), channel_id=1, source_target_pairs={{0,16},{8,24},{16,0},{24,8},{1,17},{9,25},{17,1},{25,9},{2,18},{10... | collective-permute-start | bytes 897032 | tf_op jit(solution)/shard_map/ppermute | solution.py:533
  112.3 11.0 %collective-permute-start.35 = (bf16[1168,128]{1,0:T(8,128)(2,1)S(1)}, bf16[1168,128]{1,0:T(8,128)(2,1)S(1)}, u32[]{:S(2)}, u32[]{:S(2)}) collective-permute-start(bf16[1168,128]{1,0:T(8,128)(2,1)S(1)} %shard_map.159.refs_0_), channel_id=1, source_target_pairs={{0,24},{8,16},{16,8},{24,0},{1,25},{9,17},{17,9},{25,1},{2,26},{10... | collective-permute-start | bytes 897032 | tf_op jit(solution)/shard_map/ppermute | solution.py:533
  112.5 4.5 %collective-permute-start.38 = (bf16[64,2048]{1,0:T(8,128)(2,1)S(1)}, bf16[64,2048]{1,0:T(8,128)(2,1)S(1)}, u32[]{:S(2)}, u32[]{:S(2)}) collective-permute-start(bf16[64,2048]{1,0:T(8,128)(2,1)S(1)} %get-tuple-element.146), channel_id=1, source_target_pairs={{0,1},{1,0},{2,3},{3,2},{4,5},{5,4},{6,7},{7,6},{8,9},{9,8},{10,11... | collective-permute-start | bytes 786440 | tf_op jit(solution)/shard_map/ppermute | solution.py:533
  115.8 14.1 %collective-permute-start.39 = (bf16[1168,128]{1,0:T(8,128)(2,1)S(1)}, bf16[1168,128]{1,0:T(8,128)(2,1)S(1)}, u32[]{:S(2)}, u32[]{:S(2)}) collective-permute-start(bf16[1168,128]{1,0:T(8,128)(2,1)S(1)} %shard_map.159.refs_0_), channel_id=1, source_target_pairs={{0,1},{1,0},{2,3},{3,2},{4,5},{5,4},{6,7},{7,6},{8,9},{9,8},{10,11... | collective-permute-start | bytes 897032 | tf_op jit(solution)/shard_map/ppermute | solution.py:533
  123.3 6.6 %collective-permute-start.40 = (bf16[1168,128]{1,0:T(8,128)(2,1)S(1)}, bf16[1168,128]{1,0:T(8,128)(2,1)S(1)}, u32[]{:S(2)}, u32[]{:S(2)}) collective-permute-start(bf16[1168,128]{1,0:T(8,128)(2,1)S(1)} %collective-permute-done.35.refs_1_), channel_id=1, source_target_pairs={{0,1},{1,0},{2,3},{3,2},{4,5},{5,4},{6,7},{7,6},{8,9},{9,8},{10,11... | collective-permute-start | bytes 897032 | tf_op jit(solution)/shard_map/ppermute | solution.py:533
  127.0 3.0 %collective-permute-start.41 = (bf16[1168,128]{1,0:T(8,128)(2,1)S(1)}, bf16[1168,128]{1,0:T(8,128)(2,1)S(1)}, u32[]{:S(2)}, u32[]{:S(2)}) collective-permute-start(bf16[1168,128]{1,0:T(8,128)(2,1)S(1)} %collective-permute-done.36.refs_2_), channel_id=1, source_target_pairs={{0,1},{1,0},{2,3},{3,2},{4,5},{5,4},{6,7},{7,6},{8,9},{9,8},{10,11... | collective-permute-start | bytes 897032 | tf_op jit(solution)/shard_map/ppermute | solution.py:533
  127.0 3.0 %collective-permute-start.42 = (bf16[1168,128]{1,0:T(8,128)(2,1)S(1)}, bf16[1168,128]{1,0:T(8,128)(2,1)S(1)}, u32[]{:S(2)}, u32[]{:S(2)}) collective-permute-start(bf16[1168,128]{1,0:T(8,128)(2,1)S(1)} %collective-permute-done.37.refs_3_), channel_id=1, source_target_pairs={{0,1},{1,0},{2,3},{3,2},{4,5},{5,4},{6,7},{7,6},{8,9},{9,8},{10,11... | collective-permute-start | bytes 897032 | tf_op jit(solution)/shard_map/ppermute | solution.py:533
  (1 other events, 1.9 us)
